TPU v7x, 32 devices: a whole 2x2x4 slice. The times are simulated.
32 devices in a mesh: dp: 4 (over y, x), mp: 8 (over z, core).
Axes of the slice: x: 2, y: 2, z: 4, core: 2. Of those that a mesh axis runs over, the one named last changes fastest.
Arguments:
- tokens: bfloat16 [3072, 16384], P('dp', 'mp'), may hold values from -6 to 6
- cotangent: bfloat16 [3072, 16384], P('dp', 'mp'), may hold values from -6 to 6
- blocks_w: bfloat16 [16, 5, 1024, 1024], P('mp'), may hold values from -0.078125 to 0.078125
- lowrank_u: bfloat16 [16384, 256], P('mp'), may hold values from -0.046875 to 0.046875
- lowrank_v: bfloat16 [256, 16384], P(None, 'mp'), may hold values from -0.375 to 0.375
Outputs:
- grad_tokens: float32 [3072, 16384], P('dp', 'mp')
- grad_blocks: float32 [1024, 16, 5, 1024], P('dp', 'mp')
- grad_u: float32 [16384, 256], P(('mp', 'dp'))
- grad_v: float32 [256, 16384], P(None, ('mp', 'dp'))
All inputs are finite; a program needn't handle non-finite values.
Results may differ from a plain program's by a relative error of at most 0.0029.
Values may be sent and summed in bfloat16 or wider, within the bound.
No kernel may reach another device: no remote copies, remote signals or barrier semaphores. Data moves between devices by JAX's collectives and lax.ppermute only.
A program may use at most 192 MiB of HBM per device.

v0:
```python
import math

import jax
import jax.numpy as jnp
from jax import lax
from jax.sharding import PartitionSpec as P

FACT = 4


def partner(block, axis, apart):
    count = lax.axis_size(axis)
    route = []
    for low in range(count):
        high = low | 1 << apart
        if high != low and high < count:
            route += [(low, high), (high, low)]
    return lax.ppermute(block, axis, route)


def permute_local(values, distance, local_blocks):
    pieces = [values[:, other ^ distance][:, None] for other in range(local_blocks)]
    return jnp.concatenate(pieces, axis=1)


def per_device(tokens, cotangent, blocks_w, lowrank_u, lowrank_v):
    local_blocks = blocks_w.shape[0]
    block_width = blocks_w.shape[2]
    tok_rows = tokens.shape[0]
    dp_count = lax.axis_size("dp")
    grad_scale = 1.0 / math.sqrt(tok_rows * dp_count)
    tok_blocks = tokens.reshape(tok_rows, local_blocks, block_width)
    cot_blocks = cotangent.reshape(tok_rows, local_blocks, block_width)
    low_part = jnp.dot(tokens, lowrank_u, preferred_element_type=jnp.float32)
    back_part = jnp.einsum("td,rd->tr", cotangent, lowrank_v, preferred_element_type=jnp.float32)
    low_sum, back_sum = lax.psum((low_part, back_part), "mp")
    low_in = low_sum.astype(jnp.bfloat16)
    low_back = back_sum.astype(jnp.bfloat16)
    grad_in = jnp.einsum("tr,dr->td", low_back, lowrank_u, preferred_element_type=jnp.float32)
    grad_in = grad_in.reshape(tok_rows, local_blocks, block_width)
    grad_in = grad_in + jnp.einsum(
        "tbo,bio->tbi", cot_blocks, blocks_w[:, 0], preferred_element_type=jnp.float32
    )
    sources = [tok_blocks]
    for factor in range(FACT):
        distance = 1 << factor
        outgoing = jnp.einsum(
            "tbo,bio->tbi", cot_blocks, blocks_w[:, factor + 1], preferred_element_type=jnp.float32
        )
        if distance < local_blocks:
            partner_tokens = permute_local(tok_blocks, distance, local_blocks)
            partner_term = permute_local(outgoing, distance, local_blocks)
        else:
            bit_index = (distance // local_blocks).bit_length() - 1
            partner_tokens = partner(tok_blocks, "mp", bit_index)
            partner_term = partner(outgoing, "mp", bit_index)
        grad_in = grad_in + partner_term
        sources.append(partner_tokens)
    grad_tokens = grad_in.reshape(tok_rows, local_blocks * block_width)
    stacked = jnp.stack(sources, axis=2)
    summed = lax.psum_scatter(
        jnp.einsum("tbsi,tbo->ibso", stacked, cot_blocks, preferred_element_type=jnp.float32),
        "dp",
        scatter_dimension=0,
        tiled=True,
    )
    grad_blocks = summed * grad_scale
    u_term = jnp.einsum("td,tr->dr", tokens, low_back, preferred_element_type=jnp.float32)
    v_term = jnp.einsum("tr,td->rd", low_in, cotangent, preferred_element_type=jnp.float32)
    grad_u, grad_v = (
        lax.psum_scatter(u_term, "dp", scatter_dimension=0, tiled=True),
        lax.psum_scatter(v_term, "dp", scatter_dimension=1, tiled=True),
    )
    return (grad_tokens, grad_blocks, grad_u * grad_scale, grad_v * grad_scale)


def solution(mesh):
    in_specs = (
        P("dp", "mp"),
        P("dp", "mp"),
        P("mp", None, None, None),
        P("mp", None),
        P(None, "mp"),
    )
    out_specs = (
        P("dp", "mp"),
        P("dp", "mp", None, None),
        P(("mp", "dp"), None),
        P(None, ("mp", "dp")),
    )
    return jax.shard_map(
        per_device, mesh=mesh, in_specs=in_specs, out_specs=out_specs, check_vma=False
    )
```

profile of v0, /device:TPU:0, one launch (start us, length us, event | category | flops | bytes accessed | tf_op | source)
XLA Modules:
  0.0 640.2 jit_solution(13280945959710213200)
XLA Ops:
  7.2 3.3 fusion.61
  10.7 1.0 fusion.62
  11.7 61.6 %all-reduce.2 = (bf16[768,256]{1,0:T(8,128)(2,1)S(1)}, bf16[768,256]{1,0:T(8,128)(2,1)S(1)}) all-reduce(f32[768,256]{1,0:T(8,128)S(1)} %fusion.61, f32[768,256]{1,0:T(8,128)S(1)} %fusion.62), channel_id=1, replica_groups=mesh['dp'=4,'mp'=8] {'mp'}, use_global_device_ids=true, to_apply=%region_0.0 | all-reduce | flops 393216 | bytes 2359296 | tf_op jit(solution)/shard_map/psum | solution.py:36
  73.2 4.2 convolution_bitcast_fusion.1
  77.5 4.6 copy.20
  82.2 2.0 collective-permute-start.5
  84.2 4.2 fusion.63
  88.5 6.2 reshape.21
  94.6 3.9 constant_dynamic-update-slice_fusion
  98.8 1.9 fusion.23
  100.7 3.7 bitcast_dynamic-update-slice_fusion.1
  104.4 114.4 %collective-permute-done.4 = bf16[768,2,1024]{0,2,1:T(8,128)(2,1)} collective-permute-done((bf16[768,2,1024]{0,2,1:T(8,128)(2,1)}, bf16[768,2,1024]{0,2,1:T(8,128)(2,1)}, u32[]{:S(2)}, u32[]{:S(2)}) %collective-permute-start.4) | collective-permute-done | bytes 3145760 | tf_op jit(solution)/shard_map/ppermute | solution.py:18
  218.8 3.8 bitcast_dynamic-update-slice_fusion
  222.5 3.9 bitcast_dynamic-update-slice_fusion.2
  226.4 29.1 %convolution_bitcast_fusion = f32[1024,2,5,1024]{3,0,2,1:T(8,128)} fusion(bf16[768,2,5,1024]{0,3,2,1:T(8,128)(2,1)} %bitcast_dynamic-update-slice_fusion.2, bf16[768,2,1024,1]{2,1,0,3:T(2,128)(2,1)S(1)} %bitcast.117), kind=kOutput, calls=%fused_computation | convolution fusion | flops 16106127360 | bytes 60817408 | tf_op jit(solution)/shard_map/tbsi,tbo->ibso/dot_general | solution.py:62
  255.6 9.4 %fusion.30 = f32[768,2,1024]{0,2,1:T(8,128)} fusion(bf16[2,5,1024,1024]{3,2,1,0:T(8,128)(2,1)} %param.7, bf16[96,2,8,1024]{3,2,1,0:T(8,128)(2,1)} %bitcast.110), kind=kOutput, calls=%fused_computation.35 | convolution fusion | flops 3221225472 | bytes 13631488 | tf_op jit(solution)/shard_map/tbo,bio->tbi/dot_general | solution.py:47
  265.0 8.4 %fusion.35 = f32[768,2,1024]{0,2,1:T(8,128)} fusion(bf16[2,5,1024,1024]{3,2,1,0:T(8,128)(2,1)} %param.7, bf16[96,2,8,1024]{3,2,1,0:T(8,128)(2,1)S(1)} %bitcast.112), kind=kOutput, calls=%fused_computation.36 | convolution fusion | flops 3221225472 | bytes 13631488 | tf_op jit(solution)/shard_map/tbo,bio->tbi/dot_general | solution.py:47
  273.3 8.4 %fusion.40 = f32[768,2,1024]{0,2,1:T(8,128)} fusion(bf16[2,5,1024,1024]{3,2,1,0:T(8,128)(2,1)} %param.7, bf16[96,2,8,1024]{3,2,1,0:T(8,128)(2,1)S(1)} %bitcast.113), kind=kOutput, calls=%fused_computation.37 | convolution fusion | flops 3221225472 | bytes 13631488 | tf_op jit(solution)/shard_map/tbo,bio->tbi/dot_general | solution.py:47
  281.7 3.2 collective-permute-start.2
  284.9 3.7 fusion.64
  288.6 5.5 fusion.25
  294.1 3.1 fusion.59
  297.3 1.2 broadcast_multiply_fusion.2
  298.4 1.0 copy.28
  299.4 1.9 broadcast_multiply_fusion.1
  301.3 236.4 %collective-permute-done.1 = f32[768,2,1024]{0,2,1:T(8,128)} collective-permute-done((f32[768,2,1024]{0,2,1:T(8,128)}, f32[768,2,1024]{0,2,1:T(8,128)}, u32[]{:S(2)}, u32[]{:S(2)}) %collective-permute-start.1) | collective-permute-done | bytes 6291488 | tf_op jit(solution)/shard_map/ppermute | solution.py:18
  537.7 18.4 %collective-permute-done.2 = f32[768,2,1024]{0,2,1:T(8,128)} collective-permute-done((f32[768,2,1024]{0,2,1:T(8,128)}, f32[768,2,1024]{0,2,1:T(8,128)}, u32[]{:S(2)}, u32[]{:S(2)}) %collective-permute-start.2) | collective-permute-done | bytes 6291488 | tf_op jit(solution)/shard_map/ppermute | solution.py:18
  556.1 20.1 %fusion.2 = f32[768,2,1024]{0,2,1:T(8,128)} fusion(f32[768,2,1024]{0,2,1:T(8,128)} %collective-permute-done.2, f32[768,2,1024]{0,2,1:T(8,128)} %collective-permute-done.1, f32[768,2,1024]{0,2,1:T(8,128)} %collective-permute-done, f32[768,1,1024]{0,2,1:T(8,128)} %get-tuple-element.11, f32[768,1,1024]{0,2,1:T(8,128)} %get-tuple-element.10, ...), kind=kOutput, calls=%fused_computation.4 | convolution fusion | flops 3230662656 | bytes 45088768 | tf_op jit(solution)/shard_map/tbo,bio->tbi/dot_general | solution.py:41
  576.2 7.0 %copy.26 = f32[768,2048]{1,0:T(8,128)} copy(f32[768,2048]{0,1:T(8,128)} %bitcast.115) | data formatting | bytes 12582912
  583.2 28.8 %reduce-scatter.4.cloned.1.call-done = f32[256,2,5,1024]{3,0,2,1:T(8,128)} async-done(((f32[1024,2,5,1024]{3,0,2,1:T(8,128)}), f32[256,2,5,1024]{3,0,2,1:T(8,128)}) %reduce-scatter.4.cloned.1.call-update) | async-done | bytes 10485776 | tf_op jit(solution)/shard_map/reduce_scatter | solution.py:61
  612.0 5.3 broadcast_multiply_fusion
  617.3 16.4 %copy.27 = f32[256,2,5,1024]{3,1,2,0:T(2,128)} copy(f32[256,2,5,1024]{3,0,2,1:T(8,128)S(1)} %broadcast_multiply_fusion) | data formatting | bytes 20971520
  (26 shorter events, 0.5 us)
Async XLA Ops:
  7.2 3.4 copy-start
  7.2 290.1 %reduce-scatter.6.cloned.1.call-start = ((), (), s32[]{:S(2)}) async-start(), calls=%async_computation.4 | async-start | bytes 2621440 | tf_op jit(solution)/shard_map/reduce_scatter | solution.py:71
  7.2 3.4 copy-start.3
  77.5 222.0 %reduce-scatter.8.cloned.1.call-start = ((), (), s32[]{:S(2)}) async-start(), calls=%async_computation.5 | async-start | bytes 2621440 | tf_op jit(solution)/shard_map/reduce_scatter | solution.py:72
  82.2 18.5 %collective-permute-start.3 = (bf16[768,2,1024]{0,2,1:T(8,128)(2,1)}, bf16[768,2,1024]{0,2,1:T(8,128)(2,1)}, u32[]{:S(2)}, u32[]{:S(2)}) collective-permute-start(bf16[768,2,1024]{0,2,1:T(8,128)(2,1)} %bitcast.105), channel_id=1, source_target_pairs={{0,1},{1,0},{2,3},{3,2},{4,5},{5,4},{6,7},{7,6},{8,9},{9,8},{10,11... | collective-permute-start | bytes 9437192 | tf_op jit(solution)/shard_map/ppermute | solution.py:18
  82.2 136.6 %collective-permute-start.4 = (bf16[768,2,1024]{0,2,1:T(8,128)(2,1)}, bf16[768,2,1024]{0,2,1:T(8,128)(2,1)}, u32[]{:S(2)}, u32[]{:S(2)}) collective-permute-start(bf16[768,2,1024]{0,2,1:T(8,128)(2,1)} %bitcast.106), channel_id=1, source_target_pairs={{0,2},{2,0},{1,3},{3,1},{4,6},{6,4},{5,7},{7,5},{8,10},{10,8},{9,1... | collective-permute-start | bytes 9437192 | tf_op jit(solution)/shard_map/ppermute | solution.py:18
  82.2 140.4 %collective-permute-start.5 = (bf16[768,2,1024]{0,2,1:T(8,128)(2,1)}, bf16[768,2,1024]{0,2,1:T(8,128)(2,1)}, u32[]{:S(2)}, u32[]{:S(2)}) collective-permute-start(bf16[768,2,1024]{0,2,1:T(8,128)(2,1)} %bitcast.107), channel_id=1, source_target_pairs={{0,4},{4,0},{1,5},{5,1},{2,6},{6,2},{3,7},{7,3},{8,12},{12,8},{9,1... | collective-permute-start | bytes 9437192 | tf_op jit(solution)/shard_map/ppermute | solution.py:18
  88.4 523.6 %reduce-scatter.4.cloned.1.call-start = ((), (), s32[]{:S(2)}) async-start(), calls=%async_computation.3 | async-start | bytes 52428800 | tf_op jit(solution)/shard_map/reduce_scatter | solution.py:61
  94.6 3.9 copy-start.1
  222.5 3.9 copy-start.4
  255.6 9.4 %copy-start.2 = (bf16[768,2048]{1,0:T(8,128)(2,1)S(1)}, bf16[768,2048]{1,0:T(8,128)(2,1)}, u32[]{:S(2)}) copy-start(bf16[768,2048]{1,0:T(8,128)(2,1)} %param.6) | copy-start | bytes 9437188
  265.0 36.4 %collective-permute-start = (f32[768,2,1024]{0,2,1:T(8,128)}, f32[768,2,1024]{0,2,1:T(8,128)}, u32[]{:S(2)}, u32[]{:S(2)}) collective-permute-start(f32[768,2,1024]{0,2,1:T(8,128)} %fusion.30), channel_id=1, source_target_pairs={{0,1},{1,0},{2,3},{3,2},{4,5},{5,4},{6,7},{7,6},{8,9},{9,8},{10,11... | collective-permute-start | bytes 18874376 | tf_op jit(solution)/shard_map/ppermute | solution.py:18
  273.3 264.4 %collective-permute-start.1 = (f32[768,2,1024]{0,2,1:T(8,128)}, f32[768,2,1024]{0,2,1:T(8,128)}, u32[]{:S(2)}, u32[]{:S(2)}) collective-permute-start(f32[768,2,1024]{0,2,1:T(8,128)} %fusion.35), channel_id=1, source_target_pairs={{0,2},{2,0},{1,3},{3,1},{4,6},{6,4},{5,7},{7,5},{8,10},{10,8},{9,1... | collective-permute-start | bytes 18874376 | tf_op jit(solution)/shard_map/ppermute | solution.py:18
  281.7 274.4 %collective-permute-start.2 = (f32[768,2,1024]{0,2,1:T(8,128)}, f32[768,2,1024]{0,2,1:T(8,128)}, u32[]{:S(2)}, u32[]{:S(2)}) collective-permute-start(f32[768,2,1024]{0,2,1:T(8,128)} %fusion.40), channel_id=1, source_target_pairs={{0,4},{4,0},{1,5},{5,1},{2,6},{6,2},{3,7},{7,3},{8,12},{12,8},{9,1... | collective-permute-start | bytes 18874376 | tf_op jit(solution)/shard_map/ppermute | solution.py:18
Sparse Core Ops, SparseCore 0:
  77.6 33.9 reduce-scatter.5
  114.8 35.1 reduce-scatter.7
  255.7 356.3 reduce-scatter.3
where the time goes:
time: 641 us; the launch traced here: 640 us
  waiting for transfers between devices  398 us (62%)
  matrix products  97.3 us (15%)
  blocking collectives  61.6 us (10%)
  local copies, waits for them, and re-layouts  53.9 us (8%)
  between operations  13.8 us (2%)
  other arithmetic  10.2 us (2%)
    ppermute x6, waiting for transfers between devices, partner(): return lax.ppermute(block, axis, route)  369 us
    psum x1, blocking collectives, per_device(): low_sum, back_sum = lax.psum((low_part, back_part), 'mp')  61.6 us
    unnamed x17, local copies, waits for them, and re-layouts  40.5 us
    dot_general x4, matrix products, per_device(): jnp.einsum('tbo,bio->tbi', cot_blocks, blocks_w[:, factor + 1], preferred...  31.6 us
    dot_general x1, matrix products, per_device(): jnp.einsum('tbsi,tbo->ibso', stacked, cot_blocks, preferred_element_type=...  29.1 us
    reduce_scatter x1, waiting for transfers between devices, per_device(): lax.psum_scatter(jnp.einsum('tbsi,tbo->ibso', stacked, cot_blocks, prefer...  28.8 us
    dot_general x1, matrix products, per_device(): jnp.einsum('tbo,bio->tbi', cot_blocks, blocks_w[:, 0], preferred_element_...  20.1 us
  transfers between devices with their start and end apart: 9, of which 4 were waited for; matrix products, arithmetic and copies ran while one was open for 20% of the time, Pallas kernels for 0%

commit v1 on v0

v1 whole, which is shorter than its diff:
```python
import math

import jax
import jax.numpy as jnp
from jax import lax
from jax.experimental import pallas as pl
from jax.experimental.pallas import tpu as pltpu
from jax.sharding import PartitionSpec as P

F32 = jnp.float32
BF16 = jnp.bfloat16
ROOM = 56 * 1024 * 1024
QUICK = pl.CostEstimate(flops=0, bytes_accessed=0, transcendentals=0)


def swap(value, axis, apart):
    count = lax.axis_size(axis)
    return lax.ppermute(value, axis, [(i, i ^ apart) for i in range(count)])


def tie(values, *others):
    return lax.optimization_barrier((values, others))[0]


def dot(a, b, dims):
    return lax.dot_general(a, b, (dims, ((), ())), preferred_element_type=F32)


def ordered(mine, theirs, bit, axis):
    return jnp.where(
        bit == 0,
        jnp.concatenate([mine, theirs], axis),
        jnp.concatenate([theirs, mine], axis),
    )


def call(body, **kwargs):
    return pl.pallas_call(
        body,
        compiler_params=pltpu.CompilerParams(vmem_limit_bytes=ROOM),
        cost_estimate=QUICK,
        **kwargs,
    )


def partner_term(cot, weights, slot, first_row, rows):
    blocks, _, width = weights.shape[:3]

    def body(c, w, o):
        o[...] = dot(c[...], w[0, 0], ((1,), (1,))).astype(BF16)

    start = first_row // rows
    return call(
        body,
        grid=(blocks,),
        in_specs=[
            pl.BlockSpec((rows, width), lambda j: (start, j)),
            pl.BlockSpec((1, 1, width, width), lambda j: (j, slot, 0, 0)),
        ],
        out_specs=pl.BlockSpec((rows, width), lambda j: (0, j)),
        out_shape=jax.ShapeDtypeStruct((rows, blocks * width), BF16),
    )(cot, weights)


def own_terms(cot, weights, count):
    blocks, _, width = weights.shape[:3]
    rows = cot.shape[0]
    tile = width // 2
    tiles = width // tile

    def body(c, *refs):
        o = refs[-1]
        for block in range(blocks):

            @pl.when(pl.program_id(0) == block)
            def _():
                value = None
                for s in range(count):
                    other = block ^ ((1 << s) >> 1)
                    more = dot(c[:, other * width : (other + 1) * width], refs[s][0, 0], ((1,), (1,)))
                    value = more if value is None else value + more
                o[...] = value

    def weight(s):
        return pl.BlockSpec(
            (1, 1, tile, width), lambda i, t: (i ^ ((1 << s) >> 1), s, t, 0)
        )

    return call(
        body,
        grid=(blocks, tiles),
        in_specs=[pl.BlockSpec((rows, blocks * width), lambda i, t: (0, 0))]
        + [weight(s) for s in range(count)],
        out_specs=pl.BlockSpec((rows, tile), lambda i, t: (0, i * tiles + t)),
        out_shape=jax.ShapeDtypeStruct((rows, blocks * width), F32),
    )(cot, *[weights] * count)


def turned_pieces(me, tokens, blocks, count):
    rows = tokens.shape[0]
    part = tokens.shape[1] // blocks // count

    def body(me_ref, *refs):
        for x in range(count):
            refs[count + x][...] = refs[x][...].T

    def columns(x):
        return pl.BlockSpec((rows, part), lambda j, me_ref: (0, j * count + (me_ref[0] ^ x)))

    return call(
        body,
        grid_spec=pltpu.PrefetchScalarGridSpec(
            num_scalar_prefetch=1,
            grid=(blocks,),
            in_specs=[columns(x) for x in range(count)],
            out_specs=[pl.BlockSpec((part, rows), lambda j, me_ref: (j, 0)) for _ in range(count)],
        ),
        out_shape=[jax.ShapeDtypeStruct((blocks * part, rows), BF16) for _ in range(count)],
    )(me, *[tokens] * count)


def row_parts(refs, which, first, count):
    found, at = [], 0
    for ref in refs:
        low, high = max(first, at), min(first + count, at + ref.shape[1])
        if low < high:
            found.append(ref[which, low - at : high - at, :])
        at += ref.shape[1]
    return found


def products(sources, cots, blocks):
    total = None
    for x, start, c in cots:
        lhs = []
        for refs, block in sources:
            part = sum(r.shape[1] for r in refs) // blocks
            lhs += row_parts(refs, x, block * part, part)
        lhs = jnp.concatenate(lhs, 0) if len(lhs) > 1 else lhs[0]
        if c.shape[0] != lhs.shape[1]:
            lhs = lhs[:, start : start + c.shape[0]]
        more = dot(lhs, c[...], ((1,), (0,)))
        total = more if total is None else total + more
    return total


def grouped(refs, groups):
    found = []
    for group in groups:
        found.append(refs[: len(group)])
        refs = refs[len(group) :]
    return found, refs


def early_grads(turned, near, cots, local, blocks, scale):
    part = sum(p.shape[1] for p in turned) // blocks
    width = cots[0][2].shape[1] // blocks
    tile = width // 2
    tiles = width // tile
    count = local + len(near)
    groups = [turned] + near
    pieces = [p for group in groups for p in group]

    def body(*refs):
        held, refs = grouped(refs, groups)
        mine = [(x, start, ref) for (x, start, _), ref in zip(cots, refs)]
        o = refs[-1]
        for block in range(blocks):

            @pl.when(pl.program_id(0) == block)
            def _():
                sources = [(held[0], block ^ ((1 << s) >> 1)) for s in range(local)]
                sources += [(refs_, block) for refs_ in held[1:]]
                value = products(sources, mine, blocks) * scale
                for s in range(count):
                    o[s, 0] = value[s * part : (s + 1) * part]

    return call(
        body,
        grid=(blocks, tiles),
        in_specs=[pl.BlockSpec(p.shape, lambda j, t: (0, 0, 0)) for p in pieces]
        + [pl.BlockSpec((c.shape[0], tile), lambda j, t: (0, j * tiles + t)) for _, _, c in cots],
        out_specs=pl.BlockSpec((count, 1, part, tile), lambda j, t: (0, j, 0, t)),
        out_shape=jax.ShapeDtypeStruct((count, blocks, part, width), F32),
    )(*pieces, *[c for _, _, c in cots])


def all_grads(early, far, cots, blocks, scale):
    count, _, part, width = early.shape
    slots = count + len(far)
    tile = width // 4
    tiles = width // tile
    pieces = [p for group in far for p in group]

    def body(e, *refs):
        held, refs = grouped(refs, far)
        o = refs[-1]
        for block in range(blocks):
            columns = refs[block * len(cots) : (block + 1) * len(cots)]
            mine = [(x, start, ref) for (x, start, _), ref in zip(cots, columns)]
            value = products([(group, block) for group in held], mine, blocks) * scale
            for s in range(count):
                o[:, s, block, :] = e[s, block]
            for k in range(len(far)):
                o[:, count + k, block, :] = value[k * part : (k + 1) * part]

    def columns(c, block):
        return pl.BlockSpec((c.shape[0], tile), lambda t: (0, block * tiles + t))

    out = call(
        body,
        grid=(tiles,),
        in_specs=[pl.BlockSpec((count, blocks, part, tile), lambda t: (0, 0, 0, t))]
        + [pl.BlockSpec(p.shape, lambda t: (0, 0, 0)) for p in pieces]
        + [columns(c, block) for block in range(blocks) for _, _, c in cots],
        out_specs=pl.BlockSpec((part, slots, blocks, tile), lambda t: (0, 0, 0, t)),
        out_shape=jax.ShapeDtypeStruct((part, slots, blocks, width), F32),
    )(early, *pieces, *[c for _, _, c in cots] * blocks)
    return jnp.transpose(out, (0, 2, 1, 3))


def halving(terms, orders):
    count = lax.axis_size("dp")
    me = lax.axis_index("dp")
    parts = []
    for term, axis in terms:
        size = term.shape[axis] // count
        parts.append(
            {x: lax.dynamic_slice_in_dim(term, (me ^ x) * size, size, axis) for x in range(count)}
        )
    for bits in zip(*orders):
        away = [sorted(x for x in p if x >> bit & 1) for p, bit in zip(parts, bits)]
        sent = [jnp.stack([p[x] for x in xs]) for p, xs in zip(parts, away)]
        sent = yield sent
        got = [swap(s, "dp", 1 << bit) for s, bit in zip(sent, bits)]
        got = yield got
        for p, xs, bit, g in zip(parts, away, bits, got):
            for at, x in enumerate(xs):
                p[x ^ 1 << bit] = p[x ^ 1 << bit] + g[at]
                del p[x]
    yield [p[0] for p in parts]


def per_device(tokens, cotangent, blocks_w, lowrank_u, lowrank_v):
    lb, slots, bw = blocks_w.shape[:3]
    rows = tokens.shape[0]
    n_dp = lax.axis_size("dp")
    dp_me = lax.axis_index("dp")
    part = bw // n_dp
    grad_scale = 1.0 / math.sqrt(rows * n_dp)
    bits = range(n_dp.bit_length() - 1)

    local = [s for s in range(1, slots) if 1 << (s - 1) < lb]
    remote = {s: (1 << (s - 1)) // lb for s in range(1, slots) if 1 << (s - 1) >= lb}
    near = [s for s in remote if remote[s] == 1]
    far = [s for s in remote if remote[s] > 1]
    mp_bits = lax.axis_size("mp").bit_length() - 1
    mp_me = lax.axis_index("mp")
    core, side = mp_me & 1, mp_me >> 1 & 1
    half = cut = rows // 2

    low = dot(tokens, lowrank_u, ((1,), (0,)))
    back = dot(cotangent, lowrank_v, ((1,), (1,)))
    kept = jnp.where(core == 0, low, back)
    sent = jnp.where(core == 0, back, low)
    got = swap(sent, "mp", 1)

    cot1 = tie(cotangent, kept, sent)
    first = {}
    for s in far[::-1]:
        first[s] = partner_term(cot1, blocks_w, s, 0, cut)
        cot1 = tie(cot1, first[s])
    first_in = {s: swap(first[s], "mp", remote[s]) for s in far}

    kept = kept + tie(got, cot1)
    sent = lax.dynamic_slice_in_dim(kept, (1 - side) * half, half, 0)
    kept = lax.dynamic_slice_in_dim(kept, side * half, half, 0)
    got = swap(sent, "mp", 2)

    tokens1 = tie(tokens, kept, sent)
    me = jnp.reshape(dp_me, (1,)).astype(jnp.int32)
    turned = turned_pieces(me, tokens1, lb, n_dp)
    turned, got, cot1 = tie((turned, got, cot1))
    turned = [turned[0]] + [swap(turned[x], "dp", x) for x in range(1, n_dp)]
    kept = kept + got

    near_out = {s: partner_term(cot1, blocks_w, s, 0, rows) for s in near}
    cot1 = tie(cot1, near_out)
    base = own_terms(cot1, blocks_w, 1 + len(local))
    cot1 = tie(cot1, base)
    second = {s: partner_term(cot1, blocks_w, s, cut, rows - cut) for s in far}

    turned, kept = tie((turned, kept), second)
    got = swap(kept, "mp", 4)
    middle = lb * part // 2
    turned = (
        jnp.stack([t[:middle] for t in turned]),
        jnp.stack([t[middle:] for t in turned]),
    )

    first_in, turned, got, second, cot1 = tie((first_in, turned, got, second, cotangent))
    far_a = {s: swap(turned[0], "mp", remote[s]) for s in far}
    if n_dp == 4:
        c1, c2 = swap(cot1, "dp", 1), swap(cot1, "dp", 2)
    else:
        cots = [(x, 0, swap(cot1, "dp", x) if x else cotangent) for x in range(n_dp)]
    kept = kept + got
    for bit in range(3, mp_bits):
        kept = kept + swap(kept, "mp", 1 << bit)
    kept = kept.astype(BF16)
    got = swap(kept, "mp", 2)

    if n_dp == 4:
        far_a, got, second_half, c1, c2 = tie((far_a, got, turned[1], c1, c2))
    else:
        far_a, got, second_half = tie((far_a, got, turned[1]))
    far_b = {s: swap(second_half, "mp", remote[s]) for s in far}
    if n_dp == 4:
        c3a = swap(c1[:half], "dp", 2)
        c3b = swap(c2[half:], "dp", 1)
        cots = [(0, 0, cotangent), (1, 0, c1), (2, 0, c2), (3, 0, c3a), (3, half, c3b)]
    whole = ordered(kept, got, side, 0)
    other = swap(whole, "mp", 1)
    low_in = jnp.where(core == 0, whole, other)
    low_back = jnp.where(core == 0, other, whole)
    near_tok = []
    for s in near:
        a = swap(tie(turned[0], low_in, low_back), "mp", remote[s])
        near_tok.append((a, swap(tie(turned[1], a), "mp", remote[s])))
    near_out = tie(near_out, near_tok)
    near_in = {s: swap(near_out[s], "mp", remote[s]) for s in near}

    sums = halving(
        [
            (dot(tokens, low_back, ((0,), (0,))), 0),
            (dot(low_in, cotangent, ((0,), (0,))), 1),
        ],
        [list(bits), list(bits)[::-1]],
    )
    out = next(sums)
    full = base + dot(low_back, lowrank_u, ((1,), (1,)))
    for s in near:
        full = full + near_in[s].astype(F32)
    head = full[:cut]
    for s in far:
        head = head + first_in[s].astype(F32)
    full = lax.dynamic_update_slice(full, head, (0, 0))
    early = early_grads(turned, near_tok, cots, 1 + len(local), lb, grad_scale)

    far_b, second, early, out, full = tie((far_b, second, early, out, full))
    second_in = {s: swap(second[s], "mp", remote[s]) for s in far}
    for step in bits:
        out = sums.send(sums.send(out))
    grad_u, grad_v = out[0] * grad_scale, out[1] * grad_scale
    grad_blocks = all_grads(early, [(far_a[s], far_b[s]) for s in far], cots, lb, grad_scale)

    second_in, full = tie((second_in, full), grad_blocks, grad_u, grad_v)
    tail = full[cut:]
    for s in far:
        tail = tail + second_in[s].astype(F32)
    grad_tokens = lax.dynamic_update_slice(full, tail, (cut, 0))
    return (grad_tokens, grad_blocks, grad_u, grad_v)


def solution(mesh):
    in_specs = (
        P("dp", "mp"),
        P("dp", "mp"),
        P("mp", None, None, None),
        P("mp", None),
        P(None, "mp"),
    )
    out_specs = (
        P("dp", "mp"),
        P("dp", "mp", None, None),
        P(("mp", "dp"), None),
        P(None, ("mp", "dp")),
    )
    return jax.shard_map(
        per_device, mesh=mesh, in_specs=in_specs, out_specs=out_specs, check_vma=False
    )
```

time: 641 us -> 358 us (0.56)
  waiting for transfers between devices: 398 us -> 195 us
  matrix products: 97.3 us -> 10.8 us
  Pallas kernels: 0 us -> 75.7 us
  blocking collectives: 61.6 us -> 0 us
  local copies, waits for them, and re-layouts: 53.9 us -> 13.4 us
  starting transfers between devices: 5.37 us -> 30.4 us
  other arithmetic: 10.2 us -> 30.5 us
  between operations: 13.8 us -> 0.91 us
    ppermute x6 -> x27, waiting for transfers between devices: 369 us -> 195 us  [swap(): return lax.ppermute(value, axis, [(i, i ^ apart) for i in range(count)])]
    dot_general x10 -> x5, matrix products: 93.6 us -> 10.8 us  [dot(): return lax.dot_general(a, b, (dims, ((), ())), preferred_element_type=F32)]
    pallas_call x0 -> x9, Pallas kernels: none -> 75.7 us  [the longest x5 26.1 us: partner_term(): call(body, grid=(blocks,), in_specs=[pl.BlockSpec((rows, width), lambda j...]
    psum x1 -> x0, blocking collectives: 61.6 us -> none  [per_device(): low_sum, back_sum = lax.psum((low_part, back_part), 'mp')]
    unnamed x17 -> x39, local copies, waits for them, and re-layouts: 40.5 us -> 7.7 us
    reduce_scatter x3 -> x0, waiting for transfers between devices: 28.8 us -> none  [the longest x1 28.8 us: per_device(): lax.psum_scatter(jnp.einsum('tbsi,tbo->ibso', stacked, cot_blocks, prefer...]
    ppermute x6 -> x27, starting transfers between devices: 5.25 us -> 30.4 us  [swap(): return lax.ppermute(value, axis, [(i, i ^ apart) for i in range(count)])]
    dynamic_update_slice x0 -> x2, other arithmetic: none -> 9.83 us  [the longest x1 5.31 us: per_device(): grad_tokens = lax.dynamic_update_slice(full, tail, (cut, 0))]
  transfers between devices with their start and end apart: 9 -> 27, of which waited for: 4 -> 14; matrix products, arithmetic and copies ran while one was open for 20% -> 10% of each run, Pallas kernels for 0% -> 21%
where the time goes in v1:
time: 358 us; the launch traced here: 357 us
  waiting for transfers between devices  195 us (54%)
  Pallas kernels  75.7 us (21%)
  other arithmetic  30.5 us (9%)
  starting transfers between devices  30.4 us (8%)
  local copies, waits for them, and re-layouts  13.4 us (4%)
  matrix products  10.8 us (3%)
    ppermute x27, waiting for transfers between devices, swap(): return lax.ppermute(value, axis, [(i, i ^ apart) for i in range(count)])  195 us
    ppermute x27, starting transfers between devices, swap(): return lax.ppermute(value, axis, [(i, i ^ apart) for i in range(count)])  30.4 us
    pallas_call x5, Pallas kernels, partner_term(): call(body, grid=(blocks,), in_specs=[pl.BlockSpec((rows, width), lambda j...  26.1 us
    pallas_call x1, Pallas kernels, all_grads(): call(body, grid=(tiles,), in_specs=[pl.BlockSpec((count, blocks, part, ti...  18 us
    pallas_call x1, Pallas kernels, early_grads(): call(body, grid=(blocks, tiles), in_specs=[pl.BlockSpec(p.shape, lambda j...  16.7 us
    pallas_call x1, Pallas kernels, own_terms(): call(body, grid=(blocks, tiles), in_specs=[pl.BlockSpec((rows, blocks * w...  11.4 us
    dot_general x5, matrix products, dot(): return lax.dot_general(a, b, (dims, ((), ())), preferred_element_type=F32)  10.8 us
    add x1, other arithmetic, per_device(): full = full + near_in[s].astype(F32)  8.99 us
  transfers between devices with their start and end apart: 27, of which 14 were waited for; matrix products, arithmetic and copies ran while one was open for 10% of the time, Pallas kernels for 21%

profile of v1, /device:TPU:0, one launch (start us, length us, event | category | flops | bytes accessed | tf_op | source)
XLA Modules:
  0.0 357.0 jit_solution(13805606461172794386)
XLA Ops:
  1.9 3.0 fusion.12
  4.8 3.0 broadcast_select_fusion.2
  8.3 4.8 %shard_map.84 = bf16[384,2048]{1,0:T(8,128)(2,1)} custom-call(bf16[768,2048]{1,0:T(8,128)(2,1)} %refs_9_.1, bf16[2,5,1024,1024]{3,2,1,0:T(8,128)(2,1)} %w.9), custom_call_target="tpu_custom_call" | custom-call | tf_op jit(solution)/shard_map/pallas_call | solution.py:53
  13.1 4.8 %shard_map.85 = bf16[384,2048]{1,0:T(8,128)(2,1)} custom-call(bf16[768,2048]{1,0:T(8,128)(2,1)} %refs_9_.1, bf16[2,5,1024,1024]{3,2,1,0:T(8,128)(2,1)} %w.9), custom_call_target="tpu_custom_call" | custom-call | tf_op jit(solution)/shard_map/pallas_call | solution.py:53
  18.1 2.7 collective-permute-start.3
  20.8 3.5 shard_map.86
  24.2 6.3 %collective-permute-done.3 = f32[384,256]{1,0:T(8,128)S(1)} collective-permute-done((f32[384,256]{1,0:T(8,128)S(1)}, f32[384,256]{1,0:T(8,128)S(1)}, u32[]{:S(2)}, u32[]{:S(2)}) %collective-permute-start.3) | collective-permute-done | bytes 393248 | tf_op jit(solution)/shard_map/ppermute | solution.py:18
  35.8 2.6 collective-permute-start.1
  38.3 6.9 %shard_map.87 = bf16[768,2048]{1,0:T(8,128)(2,1)} custom-call(bf16[768,2048]{1,0:T(8,128)(2,1)} %refs_9_.1, bf16[2,5,1024,1024]{3,2,1,0:T(8,128)(2,1)} %w.9), custom_call_target="tpu_custom_call" | custom-call | tf_op jit(solution)/shard_map/pallas_call | solution.py:53
  45.2 11.4 %shard_map.88 = f32[768,2048]{1,0:T(8,128)} custom-call(bf16[768,2048]{1,0:T(8,128)(2,1)} %refs_9_.1, bf16[2,5,1024,1024]{3,2,1,0:T(8,128)(2,1)} %w.9, bf16[2,5,1024,1024]{3,2,1,0:T(8,128)(2,1)} %w.9), custom_call_target="tpu_custom_call" | custom-call | tf_op jit(solution)/shard_map/pallas_call | solution.py:89
  56.6 4.8 %shard_map.89 = bf16[384,2048]{1,0:T(8,128)(2,1)} custom-call(bf16[768,2048]{1,0:T(8,128)(2,1)} %refs_9_.1, bf16[2,5,1024,1024]{3,2,1,0:T(8,128)(2,1)} %w.9), custom_call_target="tpu_custom_call" | custom-call | tf_op jit(solution)/shard_map/pallas_call | solution.py:53
  61.4 4.8 %shard_map.90 = bf16[384,2048]{1,0:T(8,128)(2,1)} custom-call(bf16[768,2048]{1,0:T(8,128)(2,1)} %refs_9_.1, bf16[2,5,1024,1024]{3,2,1,0:T(8,128)(2,1)} %w.9), custom_call_target="tpu_custom_call" | custom-call | tf_op jit(solution)/shard_map/pallas_call | solution.py:53
  68.1 2.6 collective-permute-start.7
  74.7 28.7 %collective-permute-done = bf16[384,2048]{1,0:T(8,128)(2,1)S(1)} collective-permute-done((bf16[384,2048]{1,0:T(8,128)(2,1)}, bf16[384,2048]{1,0:T(8,128)(2,1)S(1)}, u32[]{:S(2)}, u32[]{:S(2)}) %collective-permute-start) | collective-permute-done | bytes 1572896 | tf_op jit(solution)/shard_map/ppermute | solution.py:18
  103.4 12.0 %collective-permute-done.1 = bf16[384,2048]{1,0:T(8,128)(2,1)S(1)} collective-permute-done((bf16[384,2048]{1,0:T(8,128)(2,1)S(1)}, bf16[384,2048]{1,0:T(8,128)(2,1)S(1)}, u32[]{:S(2)}, u32[]{:S(2)}) %collective-permute-start.1) | collective-permute-done | bytes 1572896 | tf_op jit(solution)/shard_map/ppermute | solution.py:18
  115.4 6.8 %collective-permute-done.7 = f32[384,256]{1,0:T(8,128)S(1)} collective-permute-done((f32[384,256]{1,0:T(8,128)S(1)}, f32[384,256]{1,0:T(8,128)S(1)}, u32[]{:S(2)}, u32[]{:S(2)}) %collective-permute-start.7) | collective-permute-done | bytes 393248 | tf_op jit(solution)/shard_map/ppermute | solution.py:18
  125.2 3.0 collective-permute-start.9
  128.4 68.3 %collective-permute-done.10 = bf16[384,256]{1,0:T(8,128)(2,1)S(1)} collective-permute-done((bf16[384,256]{1,0:T(8,128)(2,1)S(1)}, bf16[384,256]{1,0:T(8,128)(2,1)S(1)}, u32[]{:S(2)}, u32[]{:S(2)}) %collective-permute-start.10) | collective-permute-done | bytes 196640 | tf_op jit(solution)/shard_map/ppermute | solution.py:18
  198.9 3.3 collective-permute-done.16.refs_2_
  203.5 3.6 %collective-permute-done.17.refs_3_ = bf16[4,256,768]{2,1,0:T(8,128)(2,1)} collective-permute-done((bf16[4,256,768]{2,1,0:T(8,128)(2,1)}, bf16[4,256,768]{2,1,0:T(8,128)(2,1)}, u32[]{:S(2)}, u32[]{:S(2)}) %collective-permute-start.17) | collective-permute-done | bytes 1572896 | tf_op jit(solution)/shard_map/ppermute | solution.py:18
  207.6 2.8 collective-permute-start.14
  215.1 2.9 fusion.14
  224.7 23.4 %collective-permute-done.18.refs_7_.refs_12_ = bf16[384,2048]{1,0:T(8,128)(2,1)} collective-permute-done((bf16[384,2048]{1,0:T(8,128)(2,1)S(1)}, bf16[384,2048]{1,0:T(8,128)(2,1)}, u32[]{:S(2)}, u32[]{:S(2)}) %collective-permute-start.18) | collective-permute-done | bytes 1572896 | tf_op jit(solution)/shard_map/ppermute | solution.py:18
  248.1 2.3 collective-permute-done.19.refs_8_.refs_13_
  250.4 16.7 %shard_map.91.e = f32[3,2,256,1024]{3,2,1,0:T(8,128)} custom-call(bf16[4,256,768]{2,1,0:T(8,128)(2,1)} %copy-done.5, bf16[4,256,768]{2,1,0:T(8,128)(2,1)} %pad_maximum_fusion.1.refs_1_, bf16[4,256,768]{2,1,0:T(8,128)(2,1)} %copy-done.11, bf16[4,256,768]{2,1,0:T(8,128)(2,1)} %collective-permute-done.17.refs_3_, bf16[768,2048]{1,0:T(8,128)(2,1)} %refs_9_.1, ...), custom_call_target="tpu_custom_call" | custom-call | tf_op jit(solution)/shard_map/pallas_call | solution.py:178
  267.2 9.0 %convert_add_fusion = f32[768,2048]{1,0:T(8,128)} fusion(bf16[768,2048]{1,0:T(8,128)(2,1)} %collective-permute-done.20, f32[768,2048]{1,0:T(8,128)} %shard_map.88, f32[768,2048]{1,0:T(8,128)S(1)} %fusion.15), kind=kLoop, calls=%fused_computation | loop fusion | flops 4718592 | bytes 22020096 | tf_op jit(solution)/shard_map/add | solution.py:343
  276.2 4.5 %fusion.1 = f32[768,2048]{1,0:T(8,128)} fusion(f32[768,2048]{1,0:T(8,128)} %convert_add_fusion, bf16[384,2048]{1,0:T(8,128)(2,1)S(1)} %copy-done.9, bf16[384,2048]{1,0:T(8,128)(2,1)S(1)} %copy-done.7), kind=kLoop, calls=%fused_computation.3 | loop fusion | flops 3145728 | bytes 9437184 | tf_op jit(solution)/shard_map/dynamic_update_slice | solution.py:347
  284.4 20.0 %collective-permute-done.23 = f32[2,512,256]{1,2,0:T(8,128)S(1)} collective-permute-done((f32[2,512,256]{1,2,0:T(8,128)S(1)}, f32[2,512,256]{1,2,0:T(8,128)S(1)}, u32[]{:S(2)}, u32[]{:S(2)}) %collective-permute-start.23) | collective-permute-done | bytes 1048608 | tf_op jit(solution)/shard_map/ppermute | solution.py:18
  304.5 2.3 fusion.8
  310.2 18.0 %shard_map.92 = f32[256,5,2,1024]{3,2,1,0:T(2,128)} custom-call(f32[3,2,256,1024]{3,2,1,0:T(8,128)} %shard_map.91.e, bf16[4,256,768]{2,1,0:T(8,128)(2,1)} %collective-permute-done.8.refs_0_, bf16[4,256,768]{2,1,0:T(8,128)(2,1)} %collective-permute-done.13.refs_1_, bf16[4,256,768]{2,1,0:T(8,128)(2,1)} %collective-permute-done.9.refs_2_, ...), custom_call_target="tpu_custom_call" | custom-call | tf_op jit(solution)/shard_map/pallas_call | solution.py:210
  334.6 15.0 %collective-permute-done.21 = bf16[384,2048]{1,0:T(8,128)(2,1)} collective-permute-done((bf16[384,2048]{1,0:T(8,128)(2,1)}, bf16[384,2048]{1,0:T(8,128)(2,1)}, u32[]{:S(2)}, u32[]{:S(2)}) %collective-permute-start.21) | collective-permute-done | bytes 1572896 | tf_op jit(solution)/shard_map/ppermute | solution.py:18
  351.7 5.3 %add_dynamic-update-slice_fusion = f32[768,2048]{1,0:T(8,128)} fusion(f32[768,2048]{1,0:T(8,128)} %fusion.1, bf16[384,2048]{1,0:T(8,128)(2,1)} %collective-permute-done.22, bf16[384,2048]{1,0:T(8,128)(2,1)} %collective-permute-done.21), kind=kLoop, calls=%fused_computation.4 | loop fusion | flops 3145728 | bytes 9437184 | tf_op jit(solution)/shard_map/dynamic_update_slice | solution.py:361
  (98 shorter events, 47.1 us)
Async XLA Ops:
  7.8 10.1 %collective-permute-start.2 = (f32[768,256]{1,0:T(8,128)S(1)}, f32[768,256]{1,0:T(8,128)S(1)}, u32[]{:S(2)}, u32[]{:S(2)}) collective-permute-start(f32[768,256]{1,0:T(8,128)S(1)} %get-tuple-element.112), channel_id=1, source_target_pairs={{0,1},{1,0},{2,3},{3,2},{4,5},{5,4},{6,7},{7,6},{8,9},{9,8},{10,11... | collective-permute-start | bytes 2359304 | tf_op jit(solution)/shard_map/ppermute | solution.py:18
  18.1 12.4 %collective-permute-start.3 = (f32[384,256]{1,0:T(8,128)S(1)}, f32[384,256]{1,0:T(8,128)S(1)}, u32[]{:S(2)}, u32[]{:S(2)}) collective-permute-start(f32[384,256]{1,0:T(8,128)S(1)} %get-tuple-element.124), channel_id=1, source_target_pairs={{0,2},{1,3},{2,0},{3,1},{4,6},{5,7},{6,4},{7,5},{8,10},{9,11},{10,... | collective-permute-start | bytes 1179656 | tf_op jit(solution)/shard_map/ppermute | solution.py:18
  20.8 15.0 %copy-start.10 = (bf16[384,2048]{1,0:T(8,128)(2,1)S(1)}, bf16[384,2048]{1,0:T(8,128)(2,1)}, u32[]{:S(2)}) copy-start(bf16[384,2048]{1,0:T(8,128)(2,1)} %shard_map.84) | copy-start | bytes 4718596
  30.5 35.8 %collective-permute-start.4 = (bf16[512,768]{1,0:T(8,128)(2,1)}, bf16[512,768]{1,0:T(8,128)(2,1)}, u32[]{:S(2)}, u32[]{:S(2)}) collective-permute-start(bf16[512,768]{1,0:T(8,128)(2,1)} %get-tuple-element.64), channel_id=1, source_target_pairs={{0,8},{8,0},{16,24},{24,16},{1,9},{9,1},{17,25},{25,17},{2,10},{10... | collective-permute-start | bytes 2359304 | tf_op jit(solution)/shard_map/ppermute | solution.py:18
  32.2 35.9 %collective-permute-start.5 = (bf16[512,768]{1,0:T(8,128)(2,1)}, bf16[512,768]{1,0:T(8,128)(2,1)S(1)}, u32[]{:S(2)}, u32[]{:S(2)}) collective-permute-start(bf16[512,768]{1,0:T(8,128)(2,1)} %get-tuple-element.65), channel_id=1, source_target_pairs={{0,16},{8,24},{16,0},{24,8},{1,17},{9,25},{17,1},{25,9},{2,18},{10... | collective-permute-start | bytes 2359304 | tf_op jit(solution)/shard_map/ppermute | solution.py:18
  33.7 34.4 %collective-permute-start.6 = (bf16[512,768]{1,0:T(8,128)(2,1)}, bf16[512,768]{1,0:T(8,128)(2,1)}, u32[]{:S(2)}, u32[]{:S(2)}) collective-permute-start(bf16[512,768]{1,0:T(8,128)(2,1)} %get-tuple-element.66), channel_id=1, source_target_pairs={{0,24},{8,16},{16,8},{24,0},{1,25},{9,17},{17,9},{25,1},{2,26},{10... | collective-permute-start | bytes 2359304 | tf_op jit(solution)/shard_map/ppermute | solution.py:18
  34.0 69.4 %collective-permute-start = (bf16[384,2048]{1,0:T(8,128)(2,1)}, bf16[384,2048]{1,0:T(8,128)(2,1)S(1)}, u32[]{:S(2)}, u32[]{:S(2)}) collective-permute-start(bf16[384,2048]{1,0:T(8,128)(2,1)} %shard_map.85), channel_id=1, source_target_pairs={{0,2},{1,3},{2,0},{3,1},{4,6},{5,7},{6,4},{7,5},{8,10},{9,11},{10,... | collective-permute-start | bytes 4718600 | tf_op jit(solution)/shard_map/ppermute | solution.py:18
  35.8 79.6 %collective-permute-start.1 = (bf16[384,2048]{1,0:T(8,128)(2,1)S(1)}, bf16[384,2048]{1,0:T(8,128)(2,1)S(1)}, u32[]{:S(2)}, u32[]{:S(2)}) collective-permute-start(bf16[384,2048]{1,0:T(8,128)(2,1)S(1)} %copy-done.10), channel_id=1, source_target_pairs={{0,4},{1,5},{2,6},{3,7},{4,0},{5,1},{6,2},{7,3},{8,12},{9,13},{10,... | collective-permute-start | bytes 4718600 | tf_op jit(solution)/shard_map/ppermute | solution.py:18
  68.1 54.0 %collective-permute-start.7 = (f32[384,256]{1,0:T(8,128)S(1)}, f32[384,256]{1,0:T(8,128)S(1)}, u32[]{:S(2)}, u32[]{:S(2)}) collective-permute-start(f32[384,256]{1,0:T(8,128)S(1)} %add.70), channel_id=1, source_target_pairs={{0,4},{1,5},{2,6},{3,7},{4,0},{5,1},{6,2},{7,3},{8,12},{9,13},{10,... | collective-permute-start | bytes 1179656 | tf_op jit(solution)/shard_map/ppermute | solution.py:18
  74.7 137.1 %copy-start.5 = (bf16[4,256,768]{2,1,0:T(8,128)(2,1)}, bf16[4,256,768]{2,1,0:T(8,128)(2,1)S(1)}, u32[]{:S(2)}) copy-start(bf16[4,256,768]{2,1,0:T(8,128)(2,1)S(1)} %pad_maximum_fusion.refs_0_) | copy-start | bytes 4718596
  103.4 21.7 %copy-start.6 = (bf16[384,2048]{1,0:T(8,128)(2,1)}, bf16[384,2048]{1,0:T(8,128)(2,1)S(1)}, u32[]{:S(2)}) copy-start(bf16[384,2048]{1,0:T(8,128)(2,1)S(1)} %collective-permute-done) | copy-start | bytes 4718596
  122.1 74.6 %collective-permute-start.11 = (bf16[768,2048]{1,0:T(8,128)(2,1)}, bf16[768,2048]{1,0:T(8,128)(2,1)}, u32[]{:S(2)}, u32[]{:S(2)}) collective-permute-start(bf16[768,2048]{1,0:T(8,128)(2,1)} %refs_9_.1), channel_id=1, source_target_pairs={{0,8},{8,0},{16,24},{24,16},{1,9},{9,1},{17,25},{25,17},{2,10},{10... | collective-permute-start | bytes 9437192 | tf_op jit(solution)/shard_map/ppermute | solution.py:18
  123.6 73.1 %collective-permute-start.12 = (bf16[768,2048]{1,0:T(8,128)(2,1)}, bf16[768,2048]{1,0:T(8,128)(2,1)}, u32[]{:S(2)}, u32[]{:S(2)}) collective-permute-start(bf16[768,2048]{1,0:T(8,128)(2,1)} %refs_9_.1), channel_id=1, source_target_pairs={{0,16},{8,24},{16,0},{24,8},{1,17},{9,25},{17,1},{25,9},{2,18},{10... | collective-permute-start | bytes 9437192 | tf_op jit(solution)/shard_map/ppermute | solution.py:18
  125.1 71.5 %collective-permute-start.8 = (bf16[4,256,768]{2,1,0:T(8,128)(2,1)S(1)}, bf16[4,256,768]{2,1,0:T(8,128)(2,1)}, u32[]{:S(2)}, u32[]{:S(2)}) collective-permute-start(bf16[4,256,768]{2,1,0:T(8,128)(2,1)S(1)} %pad_maximum_fusion.refs_0_), channel_id=1, source_target_pairs={{0,2},{1,3},{2,0},{3,1},{4,6},{5,7},{6,4},{7,5},{8,10},{9,11},{10,... | collective-permute-start | bytes 4718600 | tf_op jit(solution)/shard_map/ppermute | solution.py:18
  125.2 71.5 %collective-permute-start.9 = (bf16[4,256,768]{2,1,0:T(8,128)(2,1)S(1)}, bf16[4,256,768]{2,1,0:T(8,128)(2,1)}, u32[]{:S(2)}, u32[]{:S(2)}) collective-permute-start(bf16[4,256,768]{2,1,0:T(8,128)(2,1)S(1)} %pad_maximum_fusion.refs_0_), channel_id=1, source_target_pairs={{0,4},{1,5},{2,6},{3,7},{4,0},{5,1},{6,2},{7,3},{8,12},{9,13},{10,... | collective-permute-start | bytes 4718600 | tf_op jit(solution)/shard_map/ppermute | solution.py:18
  128.2 68.4 %collective-permute-start.10 = (bf16[384,256]{1,0:T(8,128)(2,1)S(1)}, bf16[384,256]{1,0:T(8,128)(2,1)S(1)}, u32[]{:S(2)}, u32[]{:S(2)}) collective-permute-start(bf16[384,256]{1,0:T(8,128)(2,1)S(1)} %add_convert_fusion), channel_id=1, source_target_pairs={{0,2},{1,3},{2,0},{3,1},{4,6},{5,7},{6,4},{7,5},{8,10},{9,11},{10,... | collective-permute-start | bytes 589832 | tf_op jit(solution)/shard_map/ppermute | solution.py:18
  196.9 1.8 collective-permute-start.15
  198.7 3.5 collective-permute-start.16
  203.3 3.8 %collective-permute-start.17 = (bf16[4,256,768]{2,1,0:T(8,128)(2,1)}, bf16[4,256,768]{2,1,0:T(8,128)(2,1)}, u32[]{:S(2)}, u32[]{:S(2)}) collective-permute-start(bf16[4,256,768]{2,1,0:T(8,128)(2,1)} %pad_maximum_fusion.1.refs_1_), channel_id=1, source_target_pairs={{0,1},{1,0},{2,3},{3,2},{4,5},{5,4},{6,7},{7,6},{8,9},{9,8},{10,11... | collective-permute-start | bytes 4718600 | tf_op jit(solution)/shard_map/ppermute | solution.py:18
  207.1 60.1 %collective-permute-start.20 = (bf16[768,2048]{1,0:T(8,128)(2,1)}, bf16[768,2048]{1,0:T(8,128)(2,1)}, u32[]{:S(2)}, u32[]{:S(2)}) collective-permute-start(bf16[768,2048]{1,0:T(8,128)(2,1)} %shard_map.87), channel_id=1, source_target_pairs={{0,1},{1,0},{2,3},{3,2},{4,5},{5,4},{6,7},{7,6},{8,9},{9,8},{10,11... | collective-permute-start | bytes 9437192 | tf_op jit(solution)/shard_map/ppermute | solution.py:18
  207.2 73.5 %collective-permute-start.13 = (bf16[4,256,768]{2,1,0:T(8,128)(2,1)}, bf16[4,256,768]{2,1,0:T(8,128)(2,1)}, u32[]{:S(2)}, u32[]{:S(2)}) collective-permute-start(bf16[4,256,768]{2,1,0:T(8,128)(2,1)} %pad_maximum_fusion.1.refs_1_), channel_id=1, source_target_pairs={{0,2},{1,3},{2,0},{3,1},{4,6},{5,7},{6,4},{7,5},{8,10},{9,11},{10,... | collective-permute-start | bytes 4718600 | tf_op jit(solution)/shard_map/ppermute | solution.py:18
  207.6 73.1 %collective-permute-start.14 = (bf16[4,256,768]{2,1,0:T(8,128)(2,1)}, bf16[4,256,768]{2,1,0:T(8,128)(2,1)}, u32[]{:S(2)}, u32[]{:S(2)}) collective-permute-start(bf16[4,256,768]{2,1,0:T(8,128)(2,1)} %pad_maximum_fusion.1.refs_1_), channel_id=1, source_target_pairs={{0,4},{1,5},{2,6},{3,7},{4,0},{5,1},{6,2},{7,3},{8,12},{9,13},{10,... | collective-permute-start | bytes 4718600 | tf_op jit(solution)/shard_map/ppermute | solution.py:18
  211.9 36.3 %collective-permute-start.18 = (bf16[384,2048]{1,0:T(8,128)(2,1)S(1)}, bf16[384,2048]{1,0:T(8,128)(2,1)}, u32[]{:S(2)}, u32[]{:S(2)}) collective-permute-start(bf16[384,2048]{1,0:T(8,128)(2,1)S(1)} %slice.56), channel_id=1, source_target_pairs={{0,16},{8,24},{16,0},{24,8},{1,17},{9,25},{17,1},{25,9},{2,18},{10... | collective-permute-start | bytes 4718600 | tf_op jit(solution)/shard_map/ppermute | solution.py:18
  214.4 36.0 %collective-permute-start.19 = (bf16[384,2048]{1,0:T(8,128)(2,1)S(1)}, bf16[384,2048]{1,0:T(8,128)(2,1)}, u32[]{:S(2)}, u32[]{:S(2)}) collective-permute-start(bf16[384,2048]{1,0:T(8,128)(2,1)S(1)} %slice.57), channel_id=1, source_target_pairs={{0,8},{8,0},{16,24},{24,16},{1,9},{9,1},{17,25},{25,17},{2,10},{10... | collective-permute-start | bytes 4718600 | tf_op jit(solution)/shard_map/ppermute | solution.py:18
  276.2 32.6 %copy-start.3 = (f32[256,2048]{1,0:T(8,128)S(1)}, f32[256,2048]{1,0:T(8,128)}, u32[]{:S(2)}) copy-start(f32[256,2048]{1,0:T(8,128)} %copy-done.2) | copy-start | bytes 6291460
  280.7 23.7 %collective-permute-start.23 = (f32[2,512,256]{1,2,0:T(8,128)S(1)}, f32[2,512,256]{1,2,0:T(8,128)S(1)}, u32[]{:S(2)}, u32[]{:S(2)}) collective-permute-start(f32[2,512,256]{1,2,0:T(8,128)S(1)} %copy-done.17), channel_id=1, source_target_pairs={{0,8},{8,0},{16,24},{24,16},{1,9},{9,1},{17,25},{25,17},{2,10},{10... | collective-permute-start | bytes 3145736 | tf_op jit(solution)/shard_map/ppermute | solution.py:18
  281.4 26.4 %collective-permute-start.25 = (f32[2,256,512]{2,1,0:T(8,128)S(1)}, f32[2,256,512]{2,1,0:T(8,128)S(1)}, u32[]{:S(2)}, u32[]{:S(2)}) collective-permute-start(f32[2,256,512]{2,1,0:T(8,128)S(1)} %copy-done.16), channel_id=1, source_target_pairs={{0,16},{8,24},{16,0},{24,8},{1,17},{9,25},{17,1},{25,9},{2,18},{10... | collective-permute-start | bytes 3145736 | tf_op jit(solution)/shard_map/ppermute | solution.py:18
  282.3 67.3 %collective-permute-start.21 = (bf16[384,2048]{1,0:T(8,128)(2,1)}, bf16[384,2048]{1,0:T(8,128)(2,1)}, u32[]{:S(2)}, u32[]{:S(2)}) collective-permute-start(bf16[384,2048]{1,0:T(8,128)(2,1)} %shard_map.89), channel_id=1, source_target_pairs={{0,2},{1,3},{2,0},{3,1},{4,6},{5,7},{6,4},{7,5},{8,10},{9,11},{10,... | collective-permute-start | bytes 4718600 | tf_op jit(solution)/shard_map/ppermute | solution.py:18
  282.7 69.0 %collective-permute-start.22 = (bf16[384,2048]{1,0:T(8,128)(2,1)}, bf16[384,2048]{1,0:T(8,128)(2,1)}, u32[]{:S(2)}, u32[]{:S(2)}) collective-permute-start(bf16[384,2048]{1,0:T(8,128)(2,1)} %shard_map.90), channel_id=1, source_target_pairs={{0,4},{1,5},{2,6},{3,7},{4,0},{5,1},{6,2},{7,3},{8,12},{9,13},{10,... | collective-permute-start | bytes 4718600 | tf_op jit(solution)/shard_map/ppermute | solution.py:18
  306.7 21.5 %collective-permute-start.24 = (f32[1,512,256]{1,2,0:T(8,128)}, f32[1,512,256]{1,2,0:T(8,128)}, u32[]{:S(2)}, u32[]{:S(2)}) collective-permute-start(f32[1,512,256]{1,2,0:T(8,128)} %fusion.8), channel_id=1, source_target_pairs={{0,16},{8,24},{16,0},{24,8},{1,17},{9,25},{17,1},{25,9},{2,18},{10... | collective-permute-start | bytes 1572872 | tf_op jit(solution)/shard_map/ppermute | solution.py:18
  309.6 22.8 %collective-permute-start.26 = (f32[1,256,512]{2,1,0:T(8,128)}, f32[1,256,512]{2,1,0:T(8,128)}, u32[]{:S(2)}, u32[]{:S(2)}) collective-permute-start(f32[1,256,512]{2,1,0:T(8,128)} %fusion.3), channel_id=1, source_target_pairs={{0,8},{8,0},{16,24},{24,16},{1,9},{9,1},{17,25},{25,17},{2,10},{10... | collective-permute-start | bytes 1572872 | tf_op jit(solution)/shard_map/ppermute | solution.py:18
  310.2 18.1 %copy-start.15 = (f32[2,512,256]{1,2,0:T(8,128)S(1)}, f32[2,512,256]{1,2,0:T(8,128)}, u32[]{:S(2)}) copy-start(f32[2,512,256]{1,2,0:T(8,128)} %copy-done.14) | copy-start | bytes 3145732
  (14 other events, 64.7 us)

commit v2 on v0

v2 whole, which is shorter than its diff:
```python
import math

import jax
import jax.numpy as jnp
from jax import lax
from jax.experimental import pallas as pl
from jax.experimental.pallas import tpu as pltpu
from jax.sharding import PartitionSpec as P

F32 = jnp.float32
BF16 = jnp.bfloat16
ROOM = 56 * 1024 * 1024
QUICK = pl.CostEstimate(flops=0, bytes_accessed=0, transcendentals=0)
GATHER = (2, 1)
REDUCE = (1, 2)


def swap(value, axis, apart):
    count = lax.axis_size(axis)
    return lax.ppermute(value, axis, [(i, i ^ apart) for i in range(count)])


def tie(values, *others):
    return lax.optimization_barrier((values, others))[0]


def dot(a, b, dims):
    return lax.dot_general(a, b, (dims, ((), ())), preferred_element_type=F32)


def ordered(mine, theirs, bit, axis):
    return jnp.where(
        bit == 0,
        jnp.concatenate([mine, theirs], axis),
        jnp.concatenate([theirs, mine], axis),
    )


def call(body, **kwargs):
    return pl.pallas_call(
        body,
        compiler_params=pltpu.CompilerParams(vmem_limit_bytes=ROOM),
        cost_estimate=QUICK,
        **kwargs,
    )


def prefetched(body, me, grid, in_specs, out_specs, out_shape, operands, **kwargs):
    spec = pltpu.PrefetchScalarGridSpec(
        num_scalar_prefetch=1, grid=grid, in_specs=in_specs, out_specs=out_specs
    )
    return call(body, grid_spec=spec, out_shape=out_shape, **kwargs)(me, *operands)


def partner_term(cot, weights, slot):
    blocks, _, width = weights.shape[:3]
    rows = cot.shape[0]

    def body(c, w, o):
        o[...] = dot(c[...], w[0, 0], ((1,), (1,))).astype(BF16)

    return call(
        body,
        grid=(blocks,),
        in_specs=[
            pl.BlockSpec((rows, width), lambda j: (0, j)),
            pl.BlockSpec((1, 1, width, width), lambda j: (j, slot, 0, 0)),
        ],
        out_specs=pl.BlockSpec((rows, width), lambda j: (0, j)),
        out_shape=jax.ShapeDtypeStruct((rows, blocks * width), BF16),
    )(cot, weights)


def own_terms(cot, weights, count):
    blocks, _, width = weights.shape[:3]
    rows = cot.shape[0]
    tile = width // 2
    tiles = width // tile

    def body(c, *refs):
        o = refs[-1]
        for block in range(blocks):

            @pl.when(pl.program_id(0) == block)
            def _():
                value = None
                for s in range(count):
                    other = block ^ ((1 << s) >> 1)
                    more = dot(c[:, other * width : (other + 1) * width], refs[s][0, 0], ((1,), (1,)))
                    value = more if value is None else value + more
                o[...] = value

    def weight(s):
        return pl.BlockSpec((1, 1, tile, width), lambda i, t: (i ^ ((1 << s) >> 1), s, t, 0))

    return call(
        body,
        grid=(blocks, tiles),
        in_specs=[pl.BlockSpec((rows, blocks * width), lambda i, t: (0, 0))]
        + [weight(s) for s in range(count)],
        out_specs=pl.BlockSpec((rows, tile), lambda i, t: (0, i * tiles + t)),
        out_shape=jax.ShapeDtypeStruct((rows, blocks * width), F32),
    )(cot, *[weights] * count)


def projections(core, tokens, cot, u, v):
    rows, width = tokens.shape
    rank = u.shape[1]
    tile = rows // 2

    def body(core_ref, t, c, u_ref, v_ref, kept, sent):
        low = dot(t[...], u_ref[...], ((1,), (0,)))
        back = dot(c[...], v_ref[...], ((1,), (1,)))
        first = core_ref[0] == 0
        kept[...] = jnp.where(first, low, back)
        sent[...] = jnp.where(first, back, low)

    shape = jax.ShapeDtypeStruct((rows, rank), F32)
    return call(
        body,
        grid=(rows // tile,),
        in_specs=[
            pl.BlockSpec(memory_space=pltpu.SMEM),
            pl.BlockSpec((tile, width), lambda r: (r, 0)),
            pl.BlockSpec((tile, width), lambda r: (r, 0)),
            pl.BlockSpec((width, rank), lambda r: (0, 0)),
            pl.BlockSpec((rank, width), lambda r: (0, 0)),
        ],
        out_specs=[pl.BlockSpec((tile, rank), lambda r: (r, 0))] * 2,
        out_shape=[shape, shape],
    )(core, tokens, cot, u, v)


def pieces(me, tokens, cot, blocks, part):
    rows, width = tokens.shape
    width //= blocks
    tile = rows // 3

    def body(me_ref, t, c, held, *given):
        def shard(block, x):
            start = pl.multiple_of(block * width + (me_ref[0] ^ x) * part, part)
            return t[:, pl.ds(start, part)]

        for j in range(blocks):
            held[:, 2 * j * part : (2 * j + 1) * part] = shard(j, 0)
            held[:, (2 * j + 1) * part : (2 * j + 2) * part] = shard(j, REDUCE[j])
            for at, block in enumerate((j, j ^ 1)):
                start = 2 * at * part
                given[j][:, start : start + part] = shard(block, GATHER[j])
                given[j][:, start + part : start + 2 * part] = shard(block, GATHER[j] ^ REDUCE[j])
            given[j][:, 4 * part :] = c[:, j * width : (j + 1) * width]

    widths = [2 * blocks * part] + [4 * part + width] * blocks
    return prefetched(
        body,
        me,
        (rows // tile,),
        [pl.BlockSpec((tile, blocks * width), lambda r, m: (r, 0))] * 2,
        [pl.BlockSpec((tile, w), lambda r, m: (r, 0)) for w in widths],
        [jax.ShapeDtypeStruct((rows, w), BF16) for w in widths],
        (tokens, cot),
    )


def slot_sums(me, j, tokens, cot, given, local, partners, part):
    rows = tokens.shape[0]
    width = given.shape[1] - 4 * part
    shards = width // part
    slots = 2 * local + len(partners)
    tile = width // 2
    mine = 4 * local

    def body(me_ref, *refs):
        far = refs[mine + 2 * local : -4]
        c0, c1, kept, sent = refs[-4:]
        first = list(refs[:mine]) + list(far[0::2])
        second = list(refs[mine : mine + 2 * local]) + list(far[1::2])
        value = dot(jnp.concatenate([r[...] for r in first], 1), c0[...], ((0,), (0,)))
        value = value + dot(jnp.concatenate([r[...] for r in second], 1), c1[...], ((0,), (0,)))
        for s in range(slots):
            kept[s] = value[2 * s * part : (2 * s + 1) * part]
            sent[s] = value[(2 * s + 1) * part : (2 * s + 2) * part].astype(BF16)

    def shard(block, x):
        return pl.BlockSpec((rows, part), lambda t, m: (0, block * shards + (m[0] ^ x)))

    def pair(at):
        return pl.BlockSpec((rows, 2 * part), lambda t, m: (0, at))

    in_specs, operands = [], []
    if local:
        in_specs += [shard(j, 0), shard(j, REDUCE[j]), shard(j ^ 1, 0), shard(j ^ 1, REDUCE[j])]
        in_specs += [pair(0), pair(1)]
        operands += [tokens] * 4 + [given] * 2
    for one, two in partners:
        in_specs += [pair(one[1]), pair(two[1])]
        operands += [one[0], two[0]]
    in_specs += [
        pl.BlockSpec((rows, tile), lambda t, m: (0, j * (width // tile) + t)),
        pl.BlockSpec((rows, tile), lambda t, m: (0, 4 * part // tile + t)),
    ]
    out = pl.BlockSpec((slots, part, tile), lambda t, m: (0, 0, t))
    shape = (slots, part, width)
    return prefetched(
        body,
        me,
        (width // tile,),
        in_specs,
        [out, out],
        [jax.ShapeDtypeStruct(shape, F32), jax.ShapeDtypeStruct(shape, BF16)],
        (*operands, cot, given),
    )


def all_grads(kept, got, scale):
    blocks = len(kept)
    counts = [k.shape[0] for k in kept[0]]
    _, part, width = kept[0][0].shape
    slots = sum(counts)
    tile = width // 4

    def body(*refs):
        o = refs[-1]
        refs = iter(refs)
        for j in range(blocks):
            at = 0
            for count in counts:
                mine, theirs = next(refs), next(refs)
                for s in range(count):
                    o[:, at + s, j, :] = (mine[s] + theirs[s].astype(F32)) * scale
                at += count

    operands = [
        x for j in range(blocks) for pair in zip(kept[j], got[j]) for x in pair
    ]
    out = call(
        body,
        grid=(width // tile,),
        in_specs=[pl.BlockSpec((x.shape[0], part, tile), lambda t: (0, 0, t)) for x in operands],
        out_specs=pl.BlockSpec((part, slots, blocks, tile), lambda t: (0, 0, 0, t)),
        out_shape=jax.ShapeDtypeStruct((part, slots, blocks, width), F32),
    )(*operands)
    return jnp.transpose(out, (0, 2, 1, 3))


def joined(base, near, low_back, u):
    rows, width = base.shape
    tile = width // 4

    def body(b, n, l, u_ref, o):
        o[...] = b[...] + n[...].astype(F32) + dot(l[...], u_ref[...], ((1,), (1,)))

    block = pl.BlockSpec((rows, tile), lambda t: (0, t))
    return call(
        body,
        grid=(width // tile,),
        in_specs=[
            block,
            block,
            pl.BlockSpec(low_back.shape, lambda t: (0, 0)),
            pl.BlockSpec((tile, u.shape[1]), lambda t: (t, 0)),
        ],
        out_specs=block,
        out_shape=jax.ShapeDtypeStruct(base.shape, F32),
    )(base, near, low_back, u)


def added(base, *terms):
    rows, width = base.shape
    tile = rows // 6

    def body(b, *refs):
        value = b[...]
        for ref in refs[:-1]:
            value = value + ref[...].astype(F32)
        refs[-1][...] = value

    block = pl.BlockSpec((tile, width), lambda r: (r, 0))
    return call(
        body,
        grid=(rows // tile,),
        in_specs=[block] * (1 + len(terms)),
        out_specs=block,
        out_shape=jax.ShapeDtypeStruct(base.shape, F32),
        input_output_aliases={0: 0},
    )(base, *terms)


def summed_rows(term):
    me = lax.axis_index("dp")
    size = term.shape[0] // 4
    parts = [lax.dynamic_slice_in_dim(term, (me ^ x) * size, size, 0) for x in range(4)]
    got = swap(jnp.concatenate([parts[1], parts[3]], 0).astype(BF16), "dp", 1).astype(F32)
    mine, theirs = parts[0] + got[:size], parts[2] + got[size:]
    return mine + swap(theirs.astype(BF16), "dp", 2).astype(F32)


def square(tokens, cotangent, blocks_w, lowrank_u, lowrank_v):
    lb, slots, bw = blocks_w.shape[:3]
    rows = tokens.shape[0]
    n_dp = lax.axis_size("dp")
    part = bw // n_dp
    scale = 1.0 / math.sqrt(rows * n_dp)
    me = jnp.reshape(lax.axis_index("dp"), (1,)).astype(jnp.int32)
    mp_me = lax.axis_index("mp")
    core, side = mp_me & 1, mp_me >> 1 & 1
    half = rows // 2
    near, far = 2, (3, 4)
    apart = {s: (1 << (s - 1)) // lb for s in (near, *far)}

    held, *given = pieces(me, tokens, cotangent, lb, part)
    given = [swap(g, "dp", GATHER[j]) for j, g in enumerate(given)]
    held_in = {s: swap(held, "mp", apart[s]) for s in far}

    tokens1, cot1 = tie((tokens, cotangent), held)
    kept, sent = projections(
        jnp.reshape(core, (1,)).astype(jnp.int32), tokens1, cot1, lowrank_u, lowrank_v
    )
    got = swap(sent, "mp", 1)
    cot1 = tie(cot1, kept)
    out = {near: partner_term(cot1, blocks_w, near)}
    kept = kept + tie(got, out)
    for s in far:
        cot1 = tie(cot1, out)
        out[s] = partner_term(cot1, blocks_w, s)
    base = own_terms(tie(cot1, out), blocks_w, 2)
    kept = tie(kept, base)
    sent = lax.dynamic_slice_in_dim(kept, (1 - side) * half, half, 0)
    kept = lax.dynamic_slice_in_dim(kept, side * half, half, 0)
    got = swap(sent, "mp", 2)

    given, held_in, out, got = tie((given, held_in, out, got), base)
    more = jnp.concatenate([given[j][:, : 2 * part] for j in range(lb)], 1)
    more_in = {s: swap(more, "mp", apart[s]) for s in far}
    near_tok = swap(jnp.concatenate([held, more], 1), "mp", apart[near])
    near_in = swap(out[near], "mp", apart[near])
    kept = kept + got
    got = swap(kept, "mp", 4)

    kept = (kept + got).astype(BF16)
    got = swap(kept, "mp", 2)
    whole = ordered(kept, got, side, 0)
    other = swap(whole, "mp", 1)
    low_in = jnp.where(core == 0, whole, other)
    low_back = jnp.where(core == 0, other, whole)

    out = tie(out, near_tok, near_in)
    far_in = [swap(out[s], "mp", apart[s]) for s in far]

    sums = [
        slot_sums(
            me,
            j,
            tokens,
            cotangent,
            given[j],
            True,
            [((near_tok, j), (near_tok, lb + j))] + [((held_in[s], j), (more_in[s], j)) for s in far],
            part,
        )
        for j in range(lb)
    ]
    sums_in = [swap(sums[j][1], "dp", REDUCE[j]) for j in range(lb)]

    u_term = dot(tokens, low_back, ((0,), (0,)))
    v_term = dot(cotangent, low_in, ((0,), (0,)))
    uv = summed_rows(jnp.concatenate([u_term, v_term], 1)) * scale
    rank = lowrank_u.shape[1]
    grad_u, grad_v = uv[:, :rank], uv[:, rank:].T
    full = joined(base, near_in, low_back, lowrank_u)
    sums_in = tie(sums_in, full)
    grad_blocks = all_grads([[s[0]] for s in sums], [[s] for s in sums_in], scale)
    far_in, full = tie((far_in, full), grad_blocks)
    return (added(full, *far_in), grad_blocks, grad_u, grad_v)


def general(tokens, cotangent, blocks_w, lowrank_u, lowrank_v):
    lb, slots, bw = blocks_w.shape[:3]
    rows = tokens.shape[0]
    n_dp = lax.axis_size("dp")
    part = bw // n_dp
    scale = 1.0 / math.sqrt(rows * n_dp)

    def blocks_of(value):
        return value.reshape(value.shape[0], lb, -1)

    def partner(value, slot):
        distance = (1 << slot) >> 1
        if distance < lb:
            return jnp.stack([value[:, j ^ distance] for j in range(lb)], 1)
        return swap(value, "mp", distance // lb)

    low = dot(tokens, lowrank_u, ((1,), (0,)))
    back = dot(cotangent, lowrank_v, ((1,), (1,)))
    low, back = lax.psum((low, back), "mp")
    low, back = low.astype(BF16), back.astype(BF16)

    turned = tokens.reshape(rows, lb, n_dp, part)
    turned = lax.all_to_all(turned, "dp", 2, 0, tiled=True).reshape(n_dp * rows, lb, part)
    cot_all = blocks_of(lax.all_gather(cotangent, "dp", tiled=True))
    cot = blocks_of(cotangent)
    total = blocks_of(dot(back, lowrank_u, ((1,), (1,))))
    grads = []
    for s in range(slots):
        term = jnp.einsum("tbo,bio->tbi", cot, blocks_w[:, s], preferred_element_type=F32)
        if (1 << s) >> 1 >= lb:
            term = term.astype(BF16)
        total = total + partner(term, s).astype(F32)
        grads.append(
            jnp.einsum("tbi,tbo->ibo", partner(turned, s), cot_all, preferred_element_type=F32)
        )
    grad_blocks = jnp.stack(grads, 2) * scale
    u_term = dot(tokens, back, ((0,), (0,)))
    v_term = dot(low, cotangent, ((0,), (0,)))
    grad_u = lax.psum_scatter(u_term, "dp", scatter_dimension=0, tiled=True)
    grad_v = lax.psum_scatter(v_term, "dp", scatter_dimension=1, tiled=True)
    return (total.reshape(rows, lb * bw), grad_blocks, grad_u * scale, grad_v * scale)


def per_device(tokens, cotangent, blocks_w, lowrank_u, lowrank_v):
    sizes = (blocks_w.shape[0], lax.axis_size("dp"), lax.axis_size("mp"))
    plan = square if sizes == (2, 4, 8) and blocks_w.shape[1] == 5 else general
    return plan(tokens, cotangent, blocks_w, lowrank_u, lowrank_v)


def solution(mesh):
    in_specs = (
        P("dp", "mp"),
        P("dp", "mp"),
        P("mp", None, None, None),
        P("mp", None),
        P(None, "mp"),
    )
    out_specs = (
        P("dp", "mp"),
        P("dp", "mp", None, None),
        P(("mp", "dp"), None),
        P(None, ("mp", "dp")),
    )
    return jax.shard_map(
        per_device, mesh=mesh, in_specs=in_specs, out_specs=out_specs, check_vma=False
    )
```

time: 641 us -> 334 us (0.52)
  waiting for transfers between devices: 398 us -> 186 us
  Pallas kernels: 0 us -> 100 us
  matrix products: 97.3 us -> 2.03 us
  blocking collectives: 61.6 us -> 0 us
  local copies, waits for them, and re-layouts: 53.9 us -> 4.95 us
  starting transfers between devices: 5.37 us -> 24.9 us
  between operations: 13.8 us -> 0.91 us
    ppermute x6 -> x19, waiting for transfers between devices: 369 us -> 186 us  [swap(): return lax.ppermute(value, axis, [(i, i ^ apart) for i in range(count)])]
    pallas_call x0 -> x11, Pallas kernels: none -> 100 us  [the longest x3 35.9 us: prefetched(): call(body, grid_spec=spec, out_shape=out_shape, **kwargs)(me, *operands)]
    dot_general x10 -> x2, matrix products: 93.6 us -> 2.03 us  [dot(): return lax.dot_general(a, b, (dims, ((), ())), preferred_element_type=F32)]
    psum x1 -> x0, blocking collectives: 61.6 us -> none  [per_device(): low_sum, back_sum = lax.psum((low_part, back_part), 'mp')]
    unnamed x17 -> x25, local copies, waits for them, and re-layouts: 40.5 us -> 2.2 us
    reduce_scatter x3 -> x0, waiting for transfers between devices: 28.8 us -> none  [the longest x1 28.8 us: per_device(): lax.psum_scatter(jnp.einsum('tbsi,tbo->ibso', stacked, cot_blocks, prefer...]
    ppermute x6 -> x19, starting transfers between devices: 5.25 us -> 24.9 us  [swap(): return lax.ppermute(value, axis, [(i, i ^ apart) for i in range(count)])]
    mul x3 -> x1, other arithmetic: 8.34 us -> 1.66 us  [square(): uv = summed_rows(jnp.concatenate([u_term, v_term], 1)) * scale]
  transfers between devices with their start and end apart: 9 -> 19, of which waited for: 4 -> 7; matrix products, arithmetic and copies ran while one was open for 20% -> 5% of each run, Pallas kernels for 0% -> 26%
where the time goes in v2:
time: 334 us; the launch traced here: 333 us
  waiting for transfers between devices  186 us (56%)
  Pallas kernels  100 us (30%)
  starting transfers between devices  24.9 us (7%)
  other arithmetic  13 us (4%)
  local copies, waits for them, and re-layouts  4.95 us (1%)
    ppermute x19, waiting for transfers between devices, swap(): return lax.ppermute(value, axis, [(i, i ^ apart) for i in range(count)])  186 us
    pallas_call x3, Pallas kernels, prefetched(): call(body, grid_spec=spec, out_shape=out_shape, **kwargs)(me, *operands)  35.9 us
    ppermute x19, starting transfers between devices, swap(): return lax.ppermute(value, axis, [(i, i ^ apart) for i in range(count)])  24.9 us
    pallas_call x3, Pallas kernels, partner_term(): call(body, grid=(blocks,), in_specs=[pl.BlockSpec((rows, width), lambda j...  20.8 us
    pallas_call x1, Pallas kernels, own_terms(): call(body, grid=(blocks, tiles), in_specs=[pl.BlockSpec((rows, blocks * w...  11.4 us
    pallas_call x1, Pallas kernels, all_grads(): call(body, grid=(width // tile,), in_specs=[pl.BlockSpec((x.shape[0], par...  11 us
    pallas_call x1, Pallas kernels, added(): call(body, grid=(rows // tile,), in_specs=[block] * (1 + len(terms)), out...  8.26 us
    pallas_call x1, Pallas kernels, joined(): call(body, grid=(width // tile,), in_specs=[block, block, pl.BlockSpec(lo...  7.66 us
  transfers between devices with their start and end apart: 19, of which 7 were waited for; matrix products, arithmetic and copies ran while one was open for 5% of the time, Pallas kernels for 26%

profile of v2, /device:TPU:0, one launch (start us, length us, event | category | flops | bytes accessed | tf_op | source)
XLA Modules:
  0.0 332.6 jit_solution(9750628619280492089)
XLA Ops:
  0.6 6.9 %shard_map.84 = (bf16[768,1024]{1,0:T(8,128)(2,1)}, bf16[768,2048]{1,0:T(8,128)(2,1)}, bf16[768,2048]{1,0:T(8,128)(2,1)}) custom-call(s32[1]{0:T(128)} %bitcast.me_ref, bf16[768,2048]{1,0:T(8,128)(2,1)} %refs_3_.3, bf16[768,2048]{1,0:T(8,128)(2,1)} %refs_12_.3), custom_call_target="tpu_custom_call" | custom-call | tf_op jit(solution)/shard_map/pallas_call | solution.py:52
  7.5 3.0 collective-permute-start
  10.5 1.4 collective-permute-start.1
  12.0 1.6 collective-permute-start.2
  13.5 2.6 collective-permute-start.3
  16.1 5.4 %shard_map.85 = (f32[768,256]{1,0:T(8,128)}, f32[768,256]{1,0:T(8,128)}) custom-call(s32[1]{0:T(128)} %bitcast.1.core_ref, bf16[768,2048]{1,0:T(8,128)(2,1)} %refs_3_.3, bf16[768,2048]{1,0:T(8,128)(2,1)} %refs_12_.3, bf16[2048,256]{1,0:T(8,128)(2,1)} %u_ref.3, bf16[256,2048]{1,0:T(8,128)(2,1)} %v_ref.1), custom_call_target="tpu_custom_call" | custom-call | tf_op jit(solution)/shard_map/pallas_call | solution.py:119
  21.5 6.9 %shard_map.86 = bf16[768,2048]{1,0:T(8,128)(2,1)} custom-call(bf16[768,2048]{1,0:T(8,128)(2,1)} %refs_12_.3, bf16[2,5,1024,1024]{3,2,1,0:T(8,128)(2,1)} %refs_1_.3), custom_call_target="tpu_custom_call" | custom-call | tf_op jit(solution)/shard_map/pallas_call | solution.py:62
  28.4 7.0 %shard_map.87 = bf16[768,2048]{1,0:T(8,128)(2,1)} custom-call(bf16[768,2048]{1,0:T(8,128)(2,1)} %refs_12_.3, bf16[2,5,1024,1024]{3,2,1,0:T(8,128)(2,1)} %refs_1_.3), custom_call_target="tpu_custom_call" | custom-call | tf_op jit(solution)/shard_map/pallas_call | solution.py:62
  35.4 7.0 %shard_map.88 = bf16[768,2048]{1,0:T(8,128)(2,1)} custom-call(bf16[768,2048]{1,0:T(8,128)(2,1)} %refs_12_.3, bf16[2,5,1024,1024]{3,2,1,0:T(8,128)(2,1)} %refs_1_.3), custom_call_target="tpu_custom_call" | custom-call | tf_op jit(solution)/shard_map/pallas_call | solution.py:62
  42.3 11.4 %shard_map.89.b = f32[768,2048]{1,0:T(8,128)} custom-call(bf16[768,2048]{1,0:T(8,128)(2,1)} %refs_12_.3, bf16[2,5,1024,1024]{3,2,1,0:T(8,128)(2,1)} %refs_1_.3, bf16[2,5,1024,1024]{3,2,1,0:T(8,128)(2,1)} %refs_1_.3), custom_call_target="tpu_custom_call" | custom-call | tf_op jit(solution)/shard_map/pallas_call | solution.py:96
  53.7 1.6 add.36
  55.9 34.0 %collective-permute-done.5 = f32[384,256]{1,0:T(8,128)S(1)} collective-permute-done((f32[384,256]{1,0:T(8,128)S(1)}, f32[384,256]{1,0:T(8,128)S(1)}, u32[]{:S(2)}, u32[]{:S(2)}) %collective-permute-start.5) | collective-permute-done | bytes 393248 | tf_op jit(solution)/shard_map/ppermute | solution.py:20
  90.0 1.8 slice.18
  91.8 1.9 pad_maximum_fusion
  95.3 2.7 collective-permute-start.10
  98.0 17.8 %collective-permute-done.10 = f32[384,256]{1,0:T(8,128)S(1)} collective-permute-done((f32[384,256]{1,0:T(8,128)S(1)}, f32[384,256]{1,0:T(8,128)S(1)}, u32[]{:S(2)}, u32[]{:S(2)}) %collective-permute-start.10) | collective-permute-done | bytes 393248 | tf_op jit(solution)/shard_map/ppermute | solution.py:20
  116.7 2.7 pad_maximum_fusion.1
  120.7 2.1 collective-permute-start.14
  124.2 1.8 collective-permute-done.12
  127.1 2.1 collective-permute-start.8
  129.2 3.1 collective-permute-start.9
  134.4 58.2 %collective-permute-done.13.refs_9_ = bf16[768,1024]{1,0:T(8,128)(2,1)} collective-permute-done((bf16[768,1024]{1,0:T(8,128)(2,1)}, bf16[768,1024]{1,0:T(8,128)(2,1)}, u32[]{:S(2)}, u32[]{:S(2)}) %collective-permute-start.13) | collective-permute-done | bytes 1572896 | tf_op jit(solution)/shard_map/ppermute | solution.py:20
  192.6 14.6 %shard_map.91 = (f32[5,256,1024]{2,1,0:T(8,128)}, bf16[5,256,1024]{2,1,0:T(8,128)(2,1)}) custom-call(s32[1]{0:T(128)} %bitcast.me_ref, bf16[768,2048]{1,0:T(8,128)(2,1)} %refs_3_.3, bf16[768,2048]{1,0:T(8,128)(2,1)} %refs_3_.3, bf16[768,2048]{1,0:T(8,128)(2,1)} %refs_3_.3, bf16[768,2048]{1,0:T(8,128)(2,1)} %refs_3_.3, ...), custom_call_target="tpu_custom_call" | custom-call | tf_op jit(solution)/shard_map/pallas_call | solution.py:52
  207.8 14.4 %shard_map.92 = (f32[5,256,1024]{2,1,0:T(8,128)}, bf16[5,256,1024]{2,1,0:T(8,128)(2,1)}) custom-call(s32[1]{0:T(128)} %bitcast.me_ref, bf16[768,2048]{1,0:T(8,128)(2,1)} %refs_3_.3, bf16[768,2048]{1,0:T(8,128)(2,1)} %refs_3_.3, bf16[768,2048]{1,0:T(8,128)(2,1)} %refs_3_.3, bf16[768,2048]{1,0:T(8,128)(2,1)} %refs_3_.3, bf16[768,2048]{1,0:T(8,128)(2,1)} %copy-done.4, ...), custom_call_target="tpu_custom_call" | custom-call | tf_op jit(solution)/shard_map/pallas_call | solution.py:52
  224.0 1.5 collective-permute-start.17
  225.5 60.2 %collective-permute-done.17 = bf16[1024,512]{0,1:T(8,128)(2,1)S(1)} collective-permute-done((bf16[1024,512]{0,1:T(8,128)(2,1)}, bf16[1024,512]{0,1:T(8,128)(2,1)S(1)}, u32[]{:S(2)}, u32[]{:S(2)}) %collective-permute-start.17) | collective-permute-done | bytes 1048608 | tf_op jit(solution)/shard_map/ppermute | solution.py:20
  287.8 9.5 %collective-permute-done.18 = bf16[512,512]{0,1:T(8,128)(2,1)S(1)} collective-permute-done((bf16[512,512]{0,1:T(8,128)(2,1)S(1)}, bf16[512,512]{0,1:T(8,128)(2,1)S(1)}, u32[]{:S(2)}, u32[]{:S(2)}) %collective-permute-start.18) | collective-permute-done | bytes 524320 | tf_op jit(solution)/shard_map/ppermute | solution.py:20
  297.3 1.7 fusion.6
  300.9 7.7 %shard_map.90.b = f32[768,2048]{1,0:T(8,128)} custom-call(f32[768,2048]{1,0:T(8,128)} %shard_map.89.b, bf16[768,2048]{1,0:T(8,128)(2,1)} %collective-permute-done.7.n, bf16[768,256]{1,0:T(8,128)(2,1)} %copy-done.8, bf16[2048,256]{1,0:T(8,128)(2,1)} %u_ref.3), custom_call_target="tpu_custom_call" | custom-call | tf_op jit(solution)/shard_map/pallas_call | solution.py:254
  308.5 11.0 %shard_map.93 = f32[256,5,2,1024]{3,2,1,0:T(2,128)} custom-call(f32[5,256,1024]{2,1,0:T(8,128)} %get-tuple-element.59.refs_0_, bf16[5,256,1024]{2,1,0:T(8,128)(2,1)} %collective-permute-done.15.refs_1_, f32[5,256,1024]{2,1,0:T(8,128)} %get-tuple-element.63.refs_2_, bf16[5,256,1024]{2,1,0:T(8,128)(2,1)} %collective-permute-done.16.refs_3_), custom_call_target="tpu_custom_call" | custom-call | tf_op jit(solution)/shard_map/pallas_call | solution.py:236
  319.5 4.8 %collective-permute-done.8.refs_0_ = bf16[768,2048]{1,0:T(8,128)(2,1)} collective-permute-done((bf16[768,2048]{1,0:T(8,128)(2,1)}, bf16[768,2048]{1,0:T(8,128)(2,1)}, u32[]{:S(2)}, u32[]{:S(2)}) %collective-permute-start.8) | collective-permute-done | bytes 3145760 | tf_op jit(solution)/shard_map/ppermute | solution.py:20
  324.3 8.3 %shard_map.94 = f32[768,2048]{1,0:T(8,128)} custom-call(f32[768,2048]{1,0:T(8,128)} %shard_map.90.b, bf16[768,2048]{1,0:T(8,128)(2,1)} %collective-permute-done.8.refs_0_, bf16[768,2048]{1,0:T(8,128)(2,1)} %collective-permute-done.9.refs_1_), custom_call_target="tpu_custom_call", output_to_operand_aliasing={{}: (0, {})} | custom-call | tf_op jit(solution)/shard_map/pallas_call | solution.py:279
  (60 shorter events, 15.3 us)
Async XLA Ops:
  7.5 82.4 %collective-permute-start = (bf16[768,2048]{1,0:T(8,128)(2,1)}, bf16[768,2048]{1,0:T(8,128)(2,1)}, u32[]{:S(2)}, u32[]{:S(2)}) collective-permute-start(bf16[768,2048]{1,0:T(8,128)(2,1)} %get-tuple-element.36), channel_id=1, source_target_pairs={{0,16},{8,24},{16,0},{24,8},{1,17},{9,25},{17,1},{25,9},{2,18},{10... | collective-permute-start | bytes 9437192 | tf_op jit(solution)/shard_map/ppermute | solution.py:20
  10.5 79.4 %collective-permute-start.1 = (bf16[768,2048]{1,0:T(8,128)(2,1)}, bf16[768,2048]{1,0:T(8,128)(2,1)S(1)}, u32[]{:S(2)}, u32[]{:S(2)}) collective-permute-start(bf16[768,2048]{1,0:T(8,128)(2,1)} %get-tuple-element.37), channel_id=1, source_target_pairs={{0,8},{8,0},{16,24},{24,16},{1,9},{9,1},{17,25},{25,17},{2,10},{10... | collective-permute-start | bytes 9437192 | tf_op jit(solution)/shard_map/ppermute | solution.py:20
  12.0 77.9 %collective-permute-start.2 = (bf16[768,1024]{1,0:T(8,128)(2,1)}, bf16[768,1024]{1,0:T(8,128)(2,1)}, u32[]{:S(2)}, u32[]{:S(2)}) collective-permute-start(bf16[768,1024]{1,0:T(8,128)(2,1)} %get-tuple-element.38), channel_id=1, source_target_pairs={{0,2},{1,3},{2,0},{3,1},{4,6},{5,7},{6,4},{7,5},{8,10},{9,11},{10,... | collective-permute-start | bytes 4718600 | tf_op jit(solution)/shard_map/ppermute | solution.py:20
  13.5 76.3 %collective-permute-start.3 = (bf16[768,1024]{1,0:T(8,128)(2,1)}, bf16[768,1024]{1,0:T(8,128)(2,1)}, u32[]{:S(2)}, u32[]{:S(2)}) collective-permute-start(bf16[768,1024]{1,0:T(8,128)(2,1)} %get-tuple-element.38), channel_id=1, source_target_pairs={{0,4},{1,5},{2,6},{3,7},{4,0},{5,1},{6,2},{7,3},{8,12},{9,13},{10,... | collective-permute-start | bytes 4718600 | tf_op jit(solution)/shard_map/ppermute | solution.py:20
  21.5 32.2 %collective-permute-start.4 = (f32[768,256]{1,0:T(8,128)}, f32[768,256]{1,0:T(8,128)}, u32[]{:S(2)}, u32[]{:S(2)}) collective-permute-start(f32[768,256]{1,0:T(8,128)} %get-tuple-element.45), channel_id=1, source_target_pairs={{0,1},{1,0},{2,3},{3,2},{4,5},{5,4},{6,7},{7,6},{8,9},{9,8},{10,11... | collective-permute-start | bytes 2359304 | tf_op jit(solution)/shard_map/ppermute | solution.py:20
  53.7 38.1 %copy-start.10 = (bf16[768,1024]{1,0:T(8,128)(2,1)S(1)}, bf16[768,1024]{1,0:T(8,128)(2,1)}, u32[]{:S(2)}) copy-start(bf16[768,1024]{1,0:T(8,128)(2,1)} %get-tuple-element.38) | copy-start | bytes 4718596
  55.3 34.6 %copy-start.9 = (f32[768,256]{1,0:T(8,128)}, f32[768,256]{1,0:T(8,128)S(1)}, u32[]{:S(2)}) copy-start(f32[768,256]{1,0:T(8,128)S(1)} %add.36) | copy-start | bytes 2359300
  55.4 34.5 %collective-permute-start.5 = (f32[384,256]{1,0:T(8,128)S(1)}, f32[384,256]{1,0:T(8,128)S(1)}, u32[]{:S(2)}, u32[]{:S(2)}) collective-permute-start(f32[384,256]{1,0:T(8,128)S(1)} %constant_dynamic-slice_fusion), channel_id=1, source_target_pairs={{0,2},{1,3},{2,0},{3,1},{4,6},{5,7},{6,4},{7,5},{8,10},{9,11},{10,... | collective-permute-start | bytes 1179656 | tf_op jit(solution)/shard_map/ppermute | solution.py:20
  89.9 3.8 %copy-start.4 = (bf16[768,2048]{1,0:T(8,128)(2,1)}, bf16[768,2048]{1,0:T(8,128)(2,1)S(1)}, u32[]{:S(2)}) copy-start(bf16[768,2048]{1,0:T(8,128)(2,1)S(1)} %collective-permute-done.1.refs_4_.refs_5_.refs_13_) | copy-start | bytes 9437188
  90.0 3.7 %copy-start.6 = (bf16[768,512]{1,0:T(8,128)(2,1)}, bf16[768,512]{1,0:T(8,128)(2,1)S(1)}, u32[]{:S(2)}) copy-start(bf16[768,512]{1,0:T(8,128)(2,1)S(1)} %slice.19) | copy-start | bytes 2359300
  91.8 1.9 copy-start.7
  93.7 33.4 %collective-permute-start.6 = (bf16[768,2048]{1,0:T(8,128)(2,1)}, bf16[768,2048]{1,0:T(8,128)(2,1)}, u32[]{:S(2)}, u32[]{:S(2)}) collective-permute-start(bf16[768,2048]{1,0:T(8,128)(2,1)} %pad_maximum_fusion), channel_id=1, source_target_pairs={{0,1},{1,0},{2,3},{3,2},{4,5},{5,4},{6,7},{7,6},{8,9},{9,8},{10,11... | collective-permute-start | bytes 9437192 | tf_op jit(solution)/shard_map/ppermute | solution.py:20
  93.8 33.3 %collective-permute-start.7 = (bf16[768,2048]{1,0:T(8,128)(2,1)}, bf16[768,2048]{1,0:T(8,128)(2,1)}, u32[]{:S(2)}, u32[]{:S(2)}) collective-permute-start(bf16[768,2048]{1,0:T(8,128)(2,1)} %shard_map.86), channel_id=1, source_target_pairs={{0,1},{1,0},{2,3},{3,2},{4,5},{5,4},{6,7},{7,6},{8,9},{9,8},{10,11... | collective-permute-start | bytes 9437192 | tf_op jit(solution)/shard_map/ppermute | solution.py:20
  95.3 37.0 %copy-start = (bf16[768,2048]{1,0:T(8,128)(2,1)S(1)}, bf16[768,2048]{1,0:T(8,128)(2,1)}, u32[]{:S(2)}) copy-start(bf16[768,2048]{1,0:T(8,128)(2,1)} %refs_3_.3) | copy-start | bytes 9437188
  95.3 20.5 %collective-permute-start.10 = (f32[384,256]{1,0:T(8,128)S(1)}, f32[384,256]{1,0:T(8,128)S(1)}, u32[]{:S(2)}, u32[]{:S(2)}) collective-permute-start(f32[384,256]{1,0:T(8,128)S(1)} %dynamic-slice_add_fusion), channel_id=1, source_target_pairs={{0,4},{1,5},{2,6},{3,7},{4,0},{5,1},{6,2},{7,3},{8,12},{9,13},{10,... | collective-permute-start | bytes 1179656 | tf_op jit(solution)/shard_map/ppermute | solution.py:20
  115.9 6.9 %copy-start.11 = (bf16[384,256]{1,0:T(8,128)(2,1)}, bf16[384,256]{1,0:T(8,128)(2,1)S(1)}, u32[]{:S(2)}) copy-start(bf16[384,256]{1,0:T(8,128)(2,1)S(1)} %add_convert_fusion) | copy-start | bytes 589828
  115.9 6.9 %collective-permute-start.11 = (bf16[384,256]{1,0:T(8,128)(2,1)S(1)}, bf16[384,256]{1,0:T(8,128)(2,1)}, u32[]{:S(2)}, u32[]{:S(2)}) collective-permute-start(bf16[384,256]{1,0:T(8,128)(2,1)S(1)} %add_convert_fusion), channel_id=1, source_target_pairs={{0,2},{1,3},{2,0},{3,1},{4,6},{5,7},{6,4},{7,5},{8,10},{9,11},{10,... | collective-permute-start | bytes 589832 | tf_op jit(solution)/shard_map/ppermute | solution.py:20
  119.4 73.2 %collective-permute-start.13 = (bf16[768,1024]{1,0:T(8,128)(2,1)}, bf16[768,1024]{1,0:T(8,128)(2,1)}, u32[]{:S(2)}, u32[]{:S(2)}) collective-permute-start(bf16[768,1024]{1,0:T(8,128)(2,1)} %pad_maximum_fusion.1), channel_id=1, source_target_pairs={{0,2},{1,3},{2,0},{3,1},{4,6},{5,7},{6,4},{7,5},{8,10},{9,11},{10,... | collective-permute-start | bytes 4718600 | tf_op jit(solution)/shard_map/ppermute | solution.py:20
  120.7 71.9 %collective-permute-start.14 = (bf16[768,1024]{1,0:T(8,128)(2,1)}, bf16[768,1024]{1,0:T(8,128)(2,1)}, u32[]{:S(2)}, u32[]{:S(2)}) collective-permute-start(bf16[768,1024]{1,0:T(8,128)(2,1)} %pad_maximum_fusion.1), channel_id=1, source_target_pairs={{0,4},{1,5},{2,6},{3,7},{4,0},{5,1},{6,2},{7,3},{8,12},{9,13},{10,... | collective-permute-start | bytes 4718600 | tf_op jit(solution)/shard_map/ppermute | solution.py:20
  124.1 1.9 collective-permute-start.12
  124.2 9.1 %copy-start.1 = (bf16[768,2048]{1,0:T(8,128)(2,1)S(1)}, bf16[768,2048]{1,0:T(8,128)(2,1)}, u32[]{:S(2)}) copy-start(bf16[768,2048]{1,0:T(8,128)(2,1)} %refs_12_.3) | copy-start | bytes 9437188
  127.1 7.3 %copy-start.8 = (bf16[768,256]{1,0:T(8,128)(2,1)}, bf16[768,256]{1,0:T(8,128)(2,1)S(1)}, u32[]{:S(2)}) copy-start(bf16[768,256]{1,0:T(8,128)(2,1)S(1)} %broadcast_select_fusion.l) | copy-start | bytes 1179652
  127.1 197.2 %collective-permute-start.8 = (bf16[768,2048]{1,0:T(8,128)(2,1)}, bf16[768,2048]{1,0:T(8,128)(2,1)}, u32[]{:S(2)}, u32[]{:S(2)}) collective-permute-start(bf16[768,2048]{1,0:T(8,128)(2,1)} %shard_map.87), channel_id=1, source_target_pairs={{0,2},{1,3},{2,0},{3,1},{4,6},{5,7},{6,4},{7,5},{8,10},{9,11},{10,... | collective-permute-start | bytes 9437192 | tf_op jit(solution)/shard_map/ppermute | solution.py:20
  129.2 195.2 %collective-permute-start.9 = (bf16[768,2048]{1,0:T(8,128)(2,1)}, bf16[768,2048]{1,0:T(8,128)(2,1)}, u32[]{:S(2)}, u32[]{:S(2)}) collective-permute-start(bf16[768,2048]{1,0:T(8,128)(2,1)} %shard_map.88), channel_id=1, source_target_pairs={{0,4},{1,5},{2,6},{3,7},{4,0},{5,1},{6,2},{7,3},{8,12},{9,13},{10,... | collective-permute-start | bytes 9437192 | tf_op jit(solution)/shard_map/ppermute | solution.py:20
  133.3 89.4 %copy-start.2 = (f32[2048,256]{0,1:T(8,128)}, f32[2048,256]{0,1:T(8,128)S(1)}, u32[]{:S(2)}) copy-start(f32[2048,256]{0,1:T(8,128)S(1)} %convolution_bitcast_fusion.1) | copy-start | bytes 6291460
  207.2 101.3 %collective-permute-start.15 = (bf16[5,256,1024]{2,1,0:T(8,128)(2,1)}, bf16[5,256,1024]{2,1,0:T(8,128)(2,1)}, u32[]{:S(2)}, u32[]{:S(2)}) collective-permute-start(bf16[5,256,1024]{2,1,0:T(8,128)(2,1)} %get-tuple-element.60), channel_id=1, source_target_pairs={{0,8},{8,0},{16,24},{24,16},{1,9},{9,1},{17,25},{25,17},{2,10},{10... | collective-permute-start | bytes 7864328 | tf_op jit(solution)/shard_map/ppermute | solution.py:20
  222.2 86.3 %collective-permute-start.16 = (bf16[5,256,1024]{2,1,0:T(8,128)(2,1)}, bf16[5,256,1024]{2,1,0:T(8,128)(2,1)}, u32[]{:S(2)}, u32[]{:S(2)}) collective-permute-start(bf16[5,256,1024]{2,1,0:T(8,128)(2,1)} %get-tuple-element.61), channel_id=1, source_target_pairs={{0,16},{8,24},{16,0},{24,8},{1,17},{9,25},{17,1},{25,9},{2,18},{10... | collective-permute-start | bytes 7864328 | tf_op jit(solution)/shard_map/ppermute | solution.py:20
  224.0 61.7 %collective-permute-start.17 = (bf16[1024,512]{0,1:T(8,128)(2,1)}, bf16[1024,512]{0,1:T(8,128)(2,1)S(1)}, u32[]{:S(2)}, u32[]{:S(2)}) collective-permute-start(bf16[1024,512]{0,1:T(8,128)(2,1)} %pad_maximum_fusion.2), channel_id=1, source_target_pairs={{0,8},{8,0},{16,24},{24,16},{1,9},{9,1},{17,25},{25,17},{2,10},{10... | collective-permute-start | bytes 3145736 | tf_op jit(solution)/shard_map/ppermute | solution.py:20
  225.5 60.4 %copy-start.3 = (f32[2048,256]{0,1:T(8,128)S(1)}, f32[2048,256]{0,1:T(8,128)}, u32[]{:S(2)}) copy-start(f32[2048,256]{0,1:T(8,128)} %copy-done.2) | copy-start | bytes 6291460
  286.0 1.3 copy-start.5
  287.3 10.0 %collective-permute-start.18 = (bf16[512,512]{0,1:T(8,128)(2,1)S(1)}, bf16[512,512]{0,1:T(8,128)(2,1)S(1)}, u32[]{:S(2)}, u32[]{:S(2)}) collective-permute-start(bf16[512,512]{0,1:T(8,128)(2,1)S(1)} %fusion.2), channel_id=1, source_target_pairs={{0,16},{8,24},{16,0},{24,8},{1,17},{9,25},{17,1},{25,9},{2,18},{10... | collective-permute-start | bytes 1572872 | tf_op jit(solution)/shard_map/ppermute | solution.py:20

commit v3 on v2

--- a/solution.py
+++ b/solution.py
@@ -134,7 +134,7 @@
 def pieces(me, tokens, cot, blocks, part):
     rows, width = tokens.shape
     width //= blocks
-    tile = rows // 3
+    tile = rows // 4
 
     def body(me_ref, t, c, held, *given):
         def shard(block, x):
@@ -243,9 +243,29 @@
     return jnp.transpose(out, (0, 2, 1, 3))
 
 
+def gathered(given, width):
+    rows = given[0].shape[0]
+
+    def body(*refs):
+        for j in range(len(given)):
+
+            @pl.when(pl.program_id(0) == j)
+            def _():
+                refs[-1][...] = refs[j][...]
+
+    return call(
+        body,
+        grid=(len(given),),
+        in_specs=[pl.BlockSpec((rows, width), lambda j: (0, 0)) for _ in given],
+        out_specs=pl.BlockSpec((rows, width), lambda j: (0, j)),
+        out_shape=jax.ShapeDtypeStruct((rows, len(given) * width), BF16),
+    )(*given)
+
+
 def joined(base, near, low_back, u):
     rows, width = base.shape
     tile = width // 4
+    skipped = (near.shape[1] - width) // tile
 
     def body(b, n, l, u_ref, o):
         o[...] = b[...] + n[...].astype(F32) + dot(l[...], u_ref[...], ((1,), (1,)))
@@ -256,34 +276,13 @@
         grid=(width // tile,),
         in_specs=[
             block,
-            block,
+            pl.BlockSpec((rows, tile), lambda t: (0, skipped + t)),
             pl.BlockSpec(low_back.shape, lambda t: (0, 0)),
             pl.BlockSpec((tile, u.shape[1]), lambda t: (t, 0)),
         ],
         out_specs=block,
         out_shape=jax.ShapeDtypeStruct(base.shape, F32),
     )(base, near, low_back, u)
-
-
-def added(base, *terms):
-    rows, width = base.shape
-    tile = rows // 6
-
-    def body(b, *refs):
-        value = b[...]
-        for ref in refs[:-1]:
-            value = value + ref[...].astype(F32)
-        refs[-1][...] = value
-
-    block = pl.BlockSpec((tile, width), lambda r: (r, 0))
-    return call(
-        body,
-        grid=(rows // tile,),
-        in_specs=[block] * (1 + len(terms)),
-        out_specs=block,
-        out_shape=jax.ShapeDtypeStruct(base.shape, F32),
-        input_output_aliases={0: 0},
-    )(base, *terms)
 
 
 def summed_rows(term):
@@ -329,11 +328,12 @@
     kept = lax.dynamic_slice_in_dim(kept, side * half, half, 0)
     got = swap(sent, "mp", 2)
 
-    given, held_in, out, got = tie((given, held_in, out, got), base)
-    more = jnp.concatenate([given[j][:, : 2 * part] for j in range(lb)], 1)
+    near_out = jnp.concatenate([held, out[near]], 1)
+    given, held_in, out, near_out, got = tie((given, held_in, out, near_out, got), base)
+    more = gathered(given, 2 * part)
     more_in = {s: swap(more, "mp", apart[s]) for s in far}
-    near_tok = swap(jnp.concatenate([held, more], 1), "mp", apart[near])
-    near_in = swap(out[near], "mp", apart[near])
+    near_in = swap(near_out, "mp", apart[near])
+    near_more = swap(more, "mp", apart[near])
     kept = kept + got
     got = swap(kept, "mp", 4)
 
@@ -344,22 +344,16 @@
     low_in = jnp.where(core == 0, whole, other)
     low_back = jnp.where(core == 0, other, whole)
 
-    out = tie(out, near_tok, near_in)
-    far_in = [swap(out[s], "mp", apart[s]) for s in far]
-
-    sums = [
-        slot_sums(
-            me,
-            j,
-            tokens,
-            cotangent,
-            given[j],
-            True,
-            [((near_tok, j), (near_tok, lb + j))] + [((held_in[s], j), (more_in[s], j)) for s in far],
-            part,
-        )
-        for j in range(lb)
-    ]
+    out = tie(out, near_more, near_in)
+    more_in[3], last = tie((more_in[3], out[3]))
+    far_in = [swap(last, "mp", apart[3]), swap(out[4], "mp", apart[4])]
+
+    sums, tokens1 = [], tokens
+    for j in range(lb):
+        partners = [(near_in, near_more)] + [(held_in[s], more_in[s]) for s in far]
+        partners = [((one, j), (two, j)) for one, two in partners]
+        sums.append(slot_sums(me, j, tokens1, cotangent, given[j], True, partners, part))
+        tokens1 = tie(tokens1, sums[j])
     sums_in = [swap(sums[j][1], "dp", REDUCE[j]) for j in range(lb)]
 
     u_term = dot(tokens, low_back, ((0,), (0,)))
@@ -371,7 +365,8 @@
     sums_in = tie(sums_in, full)
     grad_blocks = all_grads([[s[0]] for s in sums], [[s] for s in sums_in], scale)
     far_in, full = tie((far_in, full), grad_blocks)
-    return (added(full, *far_in), grad_blocks, grad_u, grad_v)
+    grad_tokens = full + far_in[0].astype(F32) + far_in[1].astype(F32)
+    return (grad_tokens, grad_blocks, grad_u, grad_v)
 
 
 def general(tokens, cotangent, blocks_w, lowrank_u, lowrank_v):

time: 334 us -> 327 us (0.979)
  other arithmetic: 13 us -> 20.2 us
  Pallas kernels: 100 us -> 95.4 us
  starting transfers between devices: 24.9 us -> 21.1 us
    add x0 -> x1, other arithmetic: none -> 7.4 us  [square(): grad_tokens = full + far_in[0].astype(F32) + far_in[1].astype(F32)]
    pallas_call x2, Pallas kernels: 15.9 us -> 10.4 us  [the longest x1 7.7 us: joined(): call(body, grid=(width // tile,), in_specs=[block, pl.BlockSpec((rows, ti...]
    ppermute x19, starting transfers between devices: 24.9 us -> 21.1 us  [swap(): return lax.ppermute(value, axis, [(i, i ^ apart) for i in range(count)])]
  transfers between devices with their start and end apart: 19 -> 19, of which waited for: 7 -> 8; matrix products, arithmetic and copies ran while one was open for 5% -> 5% of each run, Pallas kernels for 26% -> 27%
where the time goes in v3:
time: 327 us
  waiting for transfers between devices  184 us (56%)
  Pallas kernels  95.4 us (29%)
  starting transfers between devices  21.1 us (6%)
  other arithmetic  20.2 us (6%)
  local copies, waits for them, and re-layouts  3.46 us (1%)
    ppermute x19, waiting for transfers between devices, swap(): return lax.ppermute(value, axis, [(i, i ^ apart) for i in range(count)])  184 us
    pallas_call x3, Pallas kernels, prefetched(): call(body, grid_spec=spec, out_shape=out_shape, **kwargs)(me, *operands)  35.5 us
    ppermute x19, starting transfers between devices, swap(): return lax.ppermute(value, axis, [(i, i ^ apart) for i in range(count)])  21.1 us
    pallas_call x3, Pallas kernels, partner_term(): call(body, grid=(blocks,), in_specs=[pl.BlockSpec((rows, width), lambda j...  20.7 us
    pallas_call x1, Pallas kernels, all_grads(): call(body, grid=(width // tile,), in_specs=[pl.BlockSpec((x.shape[0], par...  12 us
    pallas_call x1, Pallas kernels, own_terms(): call(body, grid=(blocks, tiles), in_specs=[pl.BlockSpec((rows, blocks * w...  11.4 us
    pallas_call x1, Pallas kernels, joined(): call(body, grid=(width // tile,), in_specs=[block, pl.BlockSpec((rows, ti...  7.7 us
    add x1, other arithmetic, square(): grad_tokens = full + far_in[0].astype(F32) + far_in[1].astype(F32)  7.4 us
  transfers between devices with their start and end apart: 19, of which 8 were waited for; matrix products, arithmetic and copies ran while one was open for 5% of the time, Pallas kernels for 27%

profile of v3, /device:TPU:0, one launch (start us, length us, event | category | flops | bytes accessed | tf_op | source)
XLA Modules:
  0.0 326.7 jit_solution(1853302138171412332)
XLA Ops:
  0.6 6.5 %shard_map.84 = (bf16[768,1024]{1,0:T(8,128)(2,1)}, bf16[768,2048]{1,0:T(8,128)(2,1)}, bf16[768,2048]{1,0:T(8,128)(2,1)}) custom-call(s32[1]{0:T(128)} %bitcast.me_ref, bf16[768,2048]{1,0:T(8,128)(2,1)} %refs_3_.2, bf16[768,2048]{1,0:T(8,128)(2,1)} %refs_12_.3), custom_call_target="tpu_custom_call" | custom-call | tf_op jit(solution)/shard_map/pallas_call | solution.py:52
  7.1 3.0 collective-permute-start
  10.1 1.5 collective-permute-start.1
  11.6 2.6 collective-permute-start.3
  14.2 1.6 collective-permute-start.2
  15.7 5.4 %shard_map.85 = (f32[768,256]{1,0:T(8,128)}, f32[768,256]{1,0:T(8,128)}) custom-call(s32[1]{0:T(128)} %bitcast.1.core_ref, bf16[768,2048]{1,0:T(8,128)(2,1)} %refs_3_.2, bf16[768,2048]{1,0:T(8,128)(2,1)} %refs_12_.3, bf16[2048,256]{1,0:T(8,128)(2,1)} %u_ref.3, bf16[256,2048]{1,0:T(8,128)(2,1)} %v_ref.1), custom_call_target="tpu_custom_call" | custom-call | tf_op jit(solution)/shard_map/pallas_call | solution.py:119
  21.1 6.9 %shard_map.86 = bf16[768,2048]{1,0:T(8,128)(2,1)} custom-call(bf16[768,2048]{1,0:T(8,128)(2,1)} %refs_12_.3, bf16[2,5,1024,1024]{3,2,1,0:T(8,128)(2,1)} %refs_1_.2), custom_call_target="tpu_custom_call" | custom-call | tf_op jit(solution)/shard_map/pallas_call | solution.py:62
  28.0 6.9 %shard_map.87 = bf16[768,2048]{1,0:T(8,128)(2,1)} custom-call(bf16[768,2048]{1,0:T(8,128)(2,1)} %refs_12_.3, bf16[2,5,1024,1024]{3,2,1,0:T(8,128)(2,1)} %refs_1_.2), custom_call_target="tpu_custom_call" | custom-call | tf_op jit(solution)/shard_map/pallas_call | solution.py:62
  34.9 6.9 %shard_map.88 = bf16[768,2048]{1,0:T(8,128)(2,1)} custom-call(bf16[768,2048]{1,0:T(8,128)(2,1)} %refs_12_.3, bf16[2,5,1024,1024]{3,2,1,0:T(8,128)(2,1)} %refs_1_.2), custom_call_target="tpu_custom_call" | custom-call | tf_op jit(solution)/shard_map/pallas_call | solution.py:62
  41.9 11.4 %shard_map.89.b = f32[768,2048]{1,0:T(8,128)} custom-call(bf16[768,2048]{1,0:T(8,128)(2,1)} %refs_12_.3, bf16[2,5,1024,1024]{3,2,1,0:T(8,128)(2,1)} %refs_1_.2, bf16[2,5,1024,1024]{3,2,1,0:T(8,128)(2,1)} %refs_1_.2), custom_call_target="tpu_custom_call" | custom-call | tf_op jit(solution)/shard_map/pallas_call | solution.py:96
  53.3 1.6 add.42
  55.6 4.0 %pad_maximum_fusion = bf16[768,3072]{1,0:T(8,128)(2,1)} fusion(bf16[768,2048]{1,0:T(8,128)(2,1)S(1)} %copy-done.5, bf16[768,1024]{1,0:T(8,128)(2,1)} %get-tuple-element.41), kind=kLoop, calls=%fused_computation.9 | loop fusion | flops 9437184 | bytes 9437184 | tf_op jit(solution)/shard_map/concatenate | solution.py:331
  59.6 31.0 %collective-permute-done.5 = f32[384,256]{1,0:T(8,128)S(1)} collective-permute-done((f32[384,256]{1,0:T(8,128)S(1)}, f32[384,256]{1,0:T(8,128)S(1)}, u32[]{:S(2)}, u32[]{:S(2)}) %collective-permute-start.5) | collective-permute-done | bytes 393248 | tf_op jit(solution)/shard_map/ppermute | solution.py:20
  90.8 1.3 dynamic-slice_add_fusion
  93.7 2.7 shard_map.90
  96.5 2.4 collective-permute-start.6
  98.9 14.3 %collective-permute-done.11 = f32[384,256]{1,0:T(8,128)S(1)} collective-permute-done((f32[384,256]{1,0:T(8,128)S(1)}, f32[384,256]{1,0:T(8,128)S(1)}, u32[]{:S(2)}, u32[]{:S(2)}) %collective-permute-start.11) | collective-permute-done | bytes 393248 | tf_op jit(solution)/shard_map/ppermute | solution.py:20
  113.3 2.8 collective-permute-start.14
  116.1 56.5 %collective-permute-done.12 = bf16[384,256]{1,0:T(8,128)(2,1)} collective-permute-done((bf16[384,256]{1,0:T(8,128)(2,1)S(1)}, bf16[384,256]{1,0:T(8,128)(2,1)}, u32[]{:S(2)}, u32[]{:S(2)}) %collective-permute-start.12) | collective-permute-done | bytes 196640 | tf_op jit(solution)/shard_map/ppermute | solution.py:20
  174.0 1.8 collective-permute-done.13
  176.9 2.1 collective-permute-start.10
  181.1 4.6 %collective-permute-done.14.refs_11_ = bf16[768,1024]{1,0:T(8,128)(2,1)} collective-permute-done((bf16[768,1024]{1,0:T(8,128)(2,1)}, bf16[768,1024]{1,0:T(8,128)(2,1)}, u32[]{:S(2)}, u32[]{:S(2)}) %collective-permute-start.14) | collective-permute-done | bytes 1572896 | tf_op jit(solution)/shard_map/ppermute | solution.py:20
  185.7 14.5 %shard_map.92 = (f32[5,256,1024]{2,1,0:T(8,128)}, bf16[5,256,1024]{2,1,0:T(8,128)(2,1)}) custom-call(s32[1]{0:T(128)} %bitcast.me_ref, bf16[768,2048]{1,0:T(8,128)(2,1)} %refs_3_.2, bf16[768,2048]{1,0:T(8,128)(2,1)} %refs_3_.2, bf16[768,2048]{1,0:T(8,128)(2,1)} %refs_3_.2, bf16[768,2048]{1,0:T(8,128)(2,1)} %refs_3_.2, ...), custom_call_target="tpu_custom_call" | custom-call | tf_op jit(solution)/shard_map/pallas_call | solution.py:52
  200.8 14.5 %shard_map.93 = (f32[5,256,1024]{2,1,0:T(8,128)}, bf16[5,256,1024]{2,1,0:T(8,128)(2,1)}) custom-call(s32[1]{0:T(128)} %bitcast.me_ref, bf16[768,2048]{1,0:T(8,128)(2,1)} %refs_3_.2, bf16[768,2048]{1,0:T(8,128)(2,1)} %refs_3_.2, bf16[768,2048]{1,0:T(8,128)(2,1)} %refs_3_.2, bf16[768,2048]{1,0:T(8,128)(2,1)} %refs_3_.2, bf16[768,2048]{1,0:T(8,128)(2,1)} %copy-done.2, ...), custom_call_target="tpu_custom_call" | custom-call | tf_op jit(solution)/shard_map/pallas_call | solution.py:52
  217.0 1.5 collective-permute-start.17
  218.5 60.9 %collective-permute-done.17 = bf16[1024,512]{0,1:T(8,128)(2,1)S(1)} collective-permute-done((bf16[1024,512]{0,1:T(8,128)(2,1)}, bf16[1024,512]{0,1:T(8,128)(2,1)S(1)}, u32[]{:S(2)}, u32[]{:S(2)}) %collective-permute-start.17) | collective-permute-done | bytes 1048608 | tf_op jit(solution)/shard_map/ppermute | solution.py:20
  281.5 10.2 %collective-permute-done.18 = bf16[512,512]{0,1:T(8,128)(2,1)S(1)} collective-permute-done((bf16[512,512]{0,1:T(8,128)(2,1)S(1)}, bf16[512,512]{0,1:T(8,128)(2,1)S(1)}, u32[]{:S(2)}, u32[]{:S(2)}) %collective-permute-start.18) | collective-permute-done | bytes 524320 | tf_op jit(solution)/shard_map/ppermute | solution.py:20
  291.7 1.7 fusion.6
  295.3 7.7 %shard_map.91 = f32[768,2048]{1,0:T(8,128)} custom-call(f32[768,2048]{1,0:T(8,128)} %shard_map.89.b, bf16[768,3072]{1,0:T(8,128)(2,1)} %collective-permute-done.8.n.refs_6_, bf16[768,256]{1,0:T(8,128)(2,1)} %copy-done.7, bf16[2048,256]{1,0:T(8,128)(2,1)} %u_ref.3), custom_call_target="tpu_custom_call" | custom-call | tf_op jit(solution)/shard_map/pallas_call | solution.py:274
  303.0 12.0 %shard_map.94 = f32[256,5,2,1024]{3,2,1,0:T(2,128)} custom-call(f32[5,256,1024]{2,1,0:T(8,128)} %get-tuple-element.64.refs_0_, bf16[5,256,1024]{2,1,0:T(8,128)(2,1)} %collective-permute-done.15.refs_1_, f32[5,256,1024]{2,1,0:T(8,128)} %get-tuple-element.69.refs_2_, bf16[5,256,1024]{2,1,0:T(8,128)(2,1)} %collective-permute-done.16.refs_3_), custom_call_target="tpu_custom_call" | custom-call | tf_op jit(solution)/shard_map/pallas_call | solution.py:236
  315.0 4.3 %collective-permute-done.10 = bf16[768,2048]{1,0:T(8,128)(2,1)} collective-permute-done((bf16[768,2048]{1,0:T(8,128)(2,1)}, bf16[768,2048]{1,0:T(8,128)(2,1)}, u32[]{:S(2)}, u32[]{:S(2)}) %collective-permute-start.10) | collective-permute-done | bytes 3145760 | tf_op jit(solution)/shard_map/ppermute | solution.py:20
  319.3 7.4 %convert_add_fusion = f32[768,2048]{1,0:T(8,128)} fusion(bf16[768,2048]{1,0:T(8,128)(2,1)} %collective-permute-done.10, f32[768,2048]{1,0:T(8,128)S(1)} %bitcast.13, bf16[768,2048]{1,0:T(8,128)(2,1)} %collective-permute-done.9), kind=kLoop, calls=%fused_computation.8 | loop fusion | flops 6291456 | bytes 18874368 | tf_op jit(solution)/shard_map/add | solution.py:368
  (59 shorter events, 13.4 us)
Async XLA Ops:
  7.1 83.6 %collective-permute-start = (bf16[768,2048]{1,0:T(8,128)(2,1)}, bf16[768,2048]{1,0:T(8,128)(2,1)}, u32[]{:S(2)}, u32[]{:S(2)}) collective-permute-start(bf16[768,2048]{1,0:T(8,128)(2,1)} %get-tuple-element.39), channel_id=1, source_target_pairs={{0,16},{8,24},{16,0},{24,8},{1,17},{9,25},{17,1},{25,9},{2,18},{10... | collective-permute-start | bytes 9437192 | tf_op jit(solution)/shard_map/ppermute | solution.py:20
  10.1 80.6 %collective-permute-start.1 = (bf16[768,2048]{1,0:T(8,128)(2,1)}, bf16[768,2048]{1,0:T(8,128)(2,1)S(1)}, u32[]{:S(2)}, u32[]{:S(2)}) collective-permute-start(bf16[768,2048]{1,0:T(8,128)(2,1)} %get-tuple-element.40), channel_id=1, source_target_pairs={{0,8},{8,0},{16,24},{24,16},{1,9},{9,1},{17,25},{25,17},{2,10},{10... | collective-permute-start | bytes 9437192 | tf_op jit(solution)/shard_map/ppermute | solution.py:20
  11.6 79.1 %collective-permute-start.3 = (bf16[768,1024]{1,0:T(8,128)(2,1)}, bf16[768,1024]{1,0:T(8,128)(2,1)}, u32[]{:S(2)}, u32[]{:S(2)}) collective-permute-start(bf16[768,1024]{1,0:T(8,128)(2,1)} %get-tuple-element.41), channel_id=1, source_target_pairs={{0,4},{1,5},{2,6},{3,7},{4,0},{5,1},{6,2},{7,3},{8,12},{9,13},{10,... | collective-permute-start | bytes 4718600 | tf_op jit(solution)/shard_map/ppermute | solution.py:20
  14.2 76.5 %collective-permute-start.2 = (bf16[768,1024]{1,0:T(8,128)(2,1)}, bf16[768,1024]{1,0:T(8,128)(2,1)}, u32[]{:S(2)}, u32[]{:S(2)}) collective-permute-start(bf16[768,1024]{1,0:T(8,128)(2,1)} %get-tuple-element.41), channel_id=1, source_target_pairs={{0,2},{1,3},{2,0},{3,1},{4,6},{5,7},{6,4},{7,5},{8,10},{9,11},{10,... | collective-permute-start | bytes 4718600 | tf_op jit(solution)/shard_map/ppermute | solution.py:20
  21.1 32.1 %collective-permute-start.4 = (f32[768,256]{1,0:T(8,128)}, f32[768,256]{1,0:T(8,128)}, u32[]{:S(2)}, u32[]{:S(2)}) collective-permute-start(f32[768,256]{1,0:T(8,128)} %get-tuple-element.48), channel_id=1, source_target_pairs={{0,1},{1,0},{2,3},{3,2},{4,5},{5,4},{6,7},{7,6},{8,9},{9,8},{10,11... | collective-permute-start | bytes 2359304 | tf_op jit(solution)/shard_map/ppermute | solution.py:20
  53.3 2.4 copy-start.5
  54.9 4.7 %copy-start.8 = (f32[768,256]{1,0:T(8,128)}, f32[768,256]{1,0:T(8,128)S(1)}, u32[]{:S(2)}) copy-start(f32[768,256]{1,0:T(8,128)S(1)} %add.42) | copy-start | bytes 2359300
  54.9 35.7 %collective-permute-start.5 = (f32[384,256]{1,0:T(8,128)S(1)}, f32[384,256]{1,0:T(8,128)S(1)}, u32[]{:S(2)}, u32[]{:S(2)}) collective-permute-start(f32[384,256]{1,0:T(8,128)S(1)} %constant_dynamic-slice_fusion), channel_id=1, source_target_pairs={{0,2},{1,3},{2,0},{3,1},{4,6},{5,7},{6,4},{7,5},{8,10},{9,11},{10,... | collective-permute-start | bytes 1179656 | tf_op jit(solution)/shard_map/ppermute | solution.py:20
  90.7 1.6 copy-start.2
  90.7 86.1 %collective-permute-start.8 = (bf16[768,3072]{1,0:T(8,128)(2,1)}, bf16[768,3072]{1,0:T(8,128)(2,1)}, u32[]{:S(2)}, u32[]{:S(2)}) collective-permute-start(bf16[768,3072]{1,0:T(8,128)(2,1)} %pad_maximum_fusion), channel_id=1, source_target_pairs={{0,1},{1,0},{2,3},{3,2},{4,5},{5,4},{6,7},{7,6},{8,9},{9,8},{10,11... | collective-permute-start | bytes 14155784 | tf_op jit(solution)/shard_map/ppermute | solution.py:20
  92.3 20.8 %collective-permute-start.11 = (f32[384,256]{1,0:T(8,128)S(1)}, f32[384,256]{1,0:T(8,128)S(1)}, u32[]{:S(2)}, u32[]{:S(2)}) collective-permute-start(f32[384,256]{1,0:T(8,128)S(1)} %dynamic-slice_add_fusion), channel_id=1, source_target_pairs={{0,4},{1,5},{2,6},{3,7},{4,0},{5,1},{6,2},{7,3},{8,12},{9,13},{10,... | collective-permute-start | bytes 1179656 | tf_op jit(solution)/shard_map/ppermute | solution.py:20
  93.7 85.4 %copy-start = (bf16[768,2048]{1,0:T(8,128)(2,1)S(1)}, bf16[768,2048]{1,0:T(8,128)(2,1)}, u32[]{:S(2)}) copy-start(bf16[768,2048]{1,0:T(8,128)(2,1)} %refs_3_.2) | copy-start | bytes 9437188
  96.4 80.4 %collective-permute-start.7 = (bf16[768,1024]{1,0:T(8,128)(2,1)}, bf16[768,1024]{1,0:T(8,128)(2,1)}, u32[]{:S(2)}, u32[]{:S(2)}) collective-permute-start(bf16[768,1024]{1,0:T(8,128)(2,1)} %shard_map.90), channel_id=1, source_target_pairs={{0,1},{1,0},{2,3},{3,2},{4,5},{5,4},{6,7},{7,6},{8,9},{9,8},{10,11... | collective-permute-start | bytes 4718600 | tf_op jit(solution)/shard_map/ppermute | solution.py:20
  96.5 80.4 %collective-permute-start.6 = (bf16[768,1024]{1,0:T(8,128)(2,1)}, bf16[768,1024]{1,0:T(8,128)(2,1)}, u32[]{:S(2)}, u32[]{:S(2)}) collective-permute-start(bf16[768,1024]{1,0:T(8,128)(2,1)} %shard_map.90), channel_id=1, source_target_pairs={{0,2},{1,3},{2,0},{3,1},{4,6},{5,7},{6,4},{7,5},{8,10},{9,11},{10,... | collective-permute-start | bytes 4718600 | tf_op jit(solution)/shard_map/ppermute | solution.py:20
  113.2 2.9 copy-start.9
  113.2 59.3 %collective-permute-start.12 = (bf16[384,256]{1,0:T(8,128)(2,1)S(1)}, bf16[384,256]{1,0:T(8,128)(2,1)}, u32[]{:S(2)}, u32[]{:S(2)}) collective-permute-start(bf16[384,256]{1,0:T(8,128)(2,1)S(1)} %add_convert_fusion), channel_id=1, source_target_pairs={{0,2},{1,3},{2,0},{3,1},{4,6},{5,7},{6,4},{7,5},{8,10},{9,11},{10,... | collective-permute-start | bytes 589832 | tf_op jit(solution)/shard_map/ppermute | solution.py:20
  113.3 72.4 %collective-permute-start.14 = (bf16[768,1024]{1,0:T(8,128)(2,1)}, bf16[768,1024]{1,0:T(8,128)(2,1)}, u32[]{:S(2)}, u32[]{:S(2)}) collective-permute-start(bf16[768,1024]{1,0:T(8,128)(2,1)} %shard_map.90), channel_id=1, source_target_pairs={{0,4},{1,5},{2,6},{3,7},{4,0},{5,1},{6,2},{7,3},{8,12},{9,13},{10,... | collective-permute-start | bytes 4718600 | tf_op jit(solution)/shard_map/ppermute | solution.py:20
  173.9 1.9 collective-permute-start.13
  174.0 6.1 %copy-start.1 = (bf16[768,2048]{1,0:T(8,128)(2,1)S(1)}, bf16[768,2048]{1,0:T(8,128)(2,1)}, u32[]{:S(2)}) copy-start(bf16[768,2048]{1,0:T(8,128)(2,1)} %refs_12_.3) | copy-start | bytes 9437188
  176.8 4.3 %copy-start.7 = (bf16[768,256]{1,0:T(8,128)(2,1)}, bf16[768,256]{1,0:T(8,128)(2,1)S(1)}, u32[]{:S(2)}) copy-start(bf16[768,256]{1,0:T(8,128)(2,1)S(1)} %broadcast_select_fusion.l) | copy-start | bytes 1179652
  176.9 138.1 %collective-permute-start.9 = (bf16[768,2048]{1,0:T(8,128)(2,1)}, bf16[768,2048]{1,0:T(8,128)(2,1)}, u32[]{:S(2)}, u32[]{:S(2)}) collective-permute-start(bf16[768,2048]{1,0:T(8,128)(2,1)} %shard_map.87), channel_id=1, source_target_pairs={{0,2},{1,3},{2,0},{3,1},{4,6},{5,7},{6,4},{7,5},{8,10},{9,11},{10,... | collective-permute-start | bytes 9437192 | tf_op jit(solution)/shard_map/ppermute | solution.py:20
  176.9 142.3 %collective-permute-start.10 = (bf16[768,2048]{1,0:T(8,128)(2,1)}, bf16[768,2048]{1,0:T(8,128)(2,1)}, u32[]{:S(2)}, u32[]{:S(2)}) collective-permute-start(bf16[768,2048]{1,0:T(8,128)(2,1)} %shard_map.88), channel_id=1, source_target_pairs={{0,4},{1,5},{2,6},{3,7},{4,0},{5,1},{6,2},{7,3},{8,12},{9,13},{10,... | collective-permute-start | bytes 9437192 | tf_op jit(solution)/shard_map/ppermute | solution.py:20
  180.1 35.6 %copy-start.3 = (f32[2048,256]{0,1:T(8,128)}, f32[2048,256]{0,1:T(8,128)S(1)}, u32[]{:S(2)}) copy-start(f32[2048,256]{0,1:T(8,128)S(1)} %convolution_bitcast_fusion.1) | copy-start | bytes 6291460
  200.2 102.8 %collective-permute-start.15 = (bf16[5,256,1024]{2,1,0:T(8,128)(2,1)}, bf16[5,256,1024]{2,1,0:T(8,128)(2,1)}, u32[]{:S(2)}, u32[]{:S(2)}) collective-permute-start(bf16[5,256,1024]{2,1,0:T(8,128)(2,1)} %get-tuple-element.65), channel_id=1, source_target_pairs={{0,8},{8,0},{16,24},{24,16},{1,9},{9,1},{17,25},{25,17},{2,10},{10... | collective-permute-start | bytes 7864328 | tf_op jit(solution)/shard_map/ppermute | solution.py:20
  215.3 87.7 %collective-permute-start.16 = (bf16[5,256,1024]{2,1,0:T(8,128)(2,1)}, bf16[5,256,1024]{2,1,0:T(8,128)(2,1)}, u32[]{:S(2)}, u32[]{:S(2)}) collective-permute-start(bf16[5,256,1024]{2,1,0:T(8,128)(2,1)} %get-tuple-element.67), channel_id=1, source_target_pairs={{0,16},{8,24},{16,0},{24,8},{1,17},{9,25},{17,1},{25,9},{2,18},{10... | collective-permute-start | bytes 7864328 | tf_op jit(solution)/shard_map/ppermute | solution.py:20
  217.0 62.4 %collective-permute-start.17 = (bf16[1024,512]{0,1:T(8,128)(2,1)}, bf16[1024,512]{0,1:T(8,128)(2,1)S(1)}, u32[]{:S(2)}, u32[]{:S(2)}) collective-permute-start(bf16[1024,512]{0,1:T(8,128)(2,1)} %pad_maximum_fusion.1), channel_id=1, source_target_pairs={{0,8},{8,0},{16,24},{24,16},{1,9},{9,1},{17,25},{25,17},{2,10},{10... | collective-permute-start | bytes 3145736 | tf_op jit(solution)/shard_map/ppermute | solution.py:20
  218.5 61.1 %copy-start.4 = (f32[2048,256]{0,1:T(8,128)S(1)}, f32[2048,256]{0,1:T(8,128)}, u32[]{:S(2)}) copy-start(f32[2048,256]{0,1:T(8,128)} %copy-done.3) | copy-start | bytes 6291460
  279.6 1.4 copy-start.6
  281.0 10.7 %collective-permute-start.18 = (bf16[512,512]{0,1:T(8,128)(2,1)S(1)}, bf16[512,512]{0,1:T(8,128)(2,1)S(1)}, u32[]{:S(2)}, u32[]{:S(2)}) collective-permute-start(bf16[512,512]{0,1:T(8,128)(2,1)S(1)} %fusion.2), channel_id=1, source_target_pairs={{0,16},{8,24},{16,0},{24,8},{1,17},{9,25},{17,1},{25,9},{2,18},{10... | collective-permute-start | bytes 1572872 | tf_op jit(solution)/shard_map/ppermute | solution.py:20
  303.0 16.3 %slice-start = ((s8[6291456]{0:T(1024)(128)(4,1)}), s8[4194304]{0:T(1024)(128)(4,1)S(1)}, s32[]{:S(2)}) async-start(s8[6291456]{0:T(1024)(128)(4,1)} %bitcast.12), calls=%async_computation | async-start | bytes 8388608
  303.0 16.3 %slice-start.1 = ((s8[6291456]{0:T(1024)(128)(4,1)}), s8[2097152]{0:T(1024)(128)(4,1)S(1)}, s32[]{:S(2)}) async-start(s8[6291456]{0:T(1024)(128)(4,1)} %bitcast.12), calls=%async_computation.1 | async-start | bytes 4194304

commit v4 on v3

--- a/solution.py
+++ b/solution.py
@@ -52,23 +52,29 @@
     return call(body, grid_spec=spec, out_shape=out_shape, **kwargs)(me, *operands)
 
 
-def partner_term(cot, weights, slot):
+def partner_term(cot, weights, slot, cut=0):
     blocks, _, width = weights.shape[:3]
     rows = cot.shape[0]
-
-    def body(c, w, o):
-        o[...] = dot(c[...], w[0, 0], ((1,), (1,))).astype(BF16)
-
-    return call(
+    heights = (cut, rows - cut) if cut else (rows,)
+
+    def body(c, w, *out):
+        value = dot(c[...], w[0, 0], ((1,), (1,))).astype(BF16)
+        at = 0
+        for o in out:
+            o[...] = value[at : at + o.shape[0]]
+            at += o.shape[0]
+
+    parts = call(
         body,
         grid=(blocks,),
         in_specs=[
             pl.BlockSpec((rows, width), lambda j: (0, j)),
             pl.BlockSpec((1, 1, width, width), lambda j: (j, slot, 0, 0)),
         ],
-        out_specs=pl.BlockSpec((rows, width), lambda j: (0, j)),
-        out_shape=jax.ShapeDtypeStruct((rows, blocks * width), BF16),
+        out_specs=[pl.BlockSpec((h, width), lambda j: (0, j)) for h in heights],
+        out_shape=[jax.ShapeDtypeStruct((h, blocks * width), BF16) for h in heights],
     )(cot, weights)
+    return parts if cut else parts[0]
 
 
 def own_terms(cot, weights, count):
@@ -134,7 +140,7 @@
 def pieces(me, tokens, cot, blocks, part):
     rows, width = tokens.shape
     width //= blocks
-    tile = rows // 4
+    tile = rows // 2
 
     def body(me_ref, t, c, held, *given):
         def shard(block, x):
@@ -285,13 +291,36 @@
     )(base, near, low_back, u)
 
 
-def summed_rows(term):
+def added(base, terms, first):
+    rows, width = terms[0].shape
+    tile = rows // 4 if rows > 256 else rows
+
+    def body(b, *refs):
+        value = b[...]
+        for ref in refs[:-1]:
+            value = value + ref[...].astype(F32)
+        refs[-1][...] = value
+
+    block = pl.BlockSpec((tile, width), lambda r: (r + first // tile, 0))
+    return call(
+        body,
+        grid=(rows // tile,),
+        in_specs=[block] + [pl.BlockSpec((tile, width), lambda r: (r, 0)) for _ in terms],
+        out_specs=block,
+        out_shape=jax.ShapeDtypeStruct(base.shape, F32),
+        input_output_aliases={0: 0},
+    )(base, *terms)
+
+
+def summed_rows(term, before):
     me = lax.axis_index("dp")
     size = term.shape[0] // 4
     parts = [lax.dynamic_slice_in_dim(term, (me ^ x) * size, size, 0) for x in range(4)]
-    got = swap(jnp.concatenate([parts[1], parts[3]], 0).astype(BF16), "dp", 1).astype(F32)
+    got = swap(jnp.concatenate([parts[1], parts[3]], 0).astype(BF16), "dp", 1)
+    got = tie(got, before[0]).astype(F32)
     mine, theirs = parts[0] + got[:size], parts[2] + got[size:]
-    return mine + swap(theirs.astype(BF16), "dp", 2).astype(F32)
+    got = swap(theirs.astype(BF16), "dp", 2)
+    return mine + tie(got, before[1]).astype(F32)
 
 
 def square(tokens, cotangent, blocks_w, lowrank_u, lowrank_v):
@@ -303,7 +332,7 @@
     me = jnp.reshape(lax.axis_index("dp"), (1,)).astype(jnp.int32)
     mp_me = lax.axis_index("mp")
     core, side = mp_me & 1, mp_me >> 1 & 1
-    half = rows // 2
+    half, cut = rows // 2, rows // 12 * 11
     near, far = 2, (3, 4)
     apart = {s: (1 << (s - 1)) // lb for s in (near, *far)}
 
@@ -321,7 +350,7 @@
     kept = kept + tie(got, out)
     for s in far:
         cot1 = tie(cot1, out)
-        out[s] = partner_term(cot1, blocks_w, s)
+        out[s] = partner_term(cot1, blocks_w, s, cut)
     base = own_terms(tie(cot1, out), blocks_w, 2)
     kept = tie(kept, base)
     sent = lax.dynamic_slice_in_dim(kept, (1 - side) * half, half, 0)
@@ -329,43 +358,50 @@
     got = swap(sent, "mp", 2)
 
     near_out = jnp.concatenate([held, out[near]], 1)
-    given, held_in, out, near_out, got = tie((given, held_in, out, near_out, got), base)
+    given = tie(given, base)
     more = gathered(given, 2 * part)
-    more_in = {s: swap(more, "mp", apart[s]) for s in far}
+    given, held_in, out, near_out, got, more = tie((given, held_in, out, near_out, got, more))
+    more_in = {3: swap(more, "mp", apart[3])}
     near_in = swap(near_out, "mp", apart[near])
     near_more = swap(more, "mp", apart[near])
     kept = kept + got
     got = swap(kept, "mp", 4)
+    got, more4 = tie((got, more))
+    more_in[4] = swap(more4, "mp", apart[4])
 
     kept = (kept + got).astype(BF16)
     got = swap(kept, "mp", 2)
+    got, near_in, near_more = tie((got, near_in, near_more))
     whole = ordered(kept, got, side, 0)
     other = swap(whole, "mp", 1)
     low_in = jnp.where(core == 0, whole, other)
     low_back = jnp.where(core == 0, other, whole)
 
     out = tie(out, near_more, near_in)
-    more_in[3], last = tie((more_in[3], out[3]))
-    far_in = [swap(last, "mp", apart[3]), swap(out[4], "mp", apart[4])]
+    more_in[3], first = tie((more_in[3], out[3][0]))
+    far_in = [swap(first, "mp", apart[3]), swap(out[4][0], "mp", apart[4])]
 
     sums, tokens1 = [], tokens
     for j in range(lb):
         partners = [(near_in, near_more)] + [(held_in[s], more_in[s]) for s in far]
         partners = [((one, j), (two, j)) for one, two in partners]
         sums.append(slot_sums(me, j, tokens1, cotangent, given[j], True, partners, part))
-        tokens1 = tie(tokens1, sums[j])
     sums_in = [swap(sums[j][1], "dp", REDUCE[j]) for j in range(lb)]
 
-    u_term = dot(tokens, low_back, ((0,), (0,)))
-    v_term = dot(cotangent, low_in, ((0,), (0,)))
-    uv = summed_rows(jnp.concatenate([u_term, v_term], 1)) * scale
-    rank = lowrank_u.shape[1]
-    grad_u, grad_v = uv[:, :rank], uv[:, rank:].T
     full = joined(base, near_in, low_back, lowrank_u)
     sums_in = tie(sums_in, full)
     grad_blocks = all_grads([[s[0]] for s in sums], [[s] for s in sums_in], scale)
+
+    u_term = dot(tokens, low_back, ((0,), (0,)))
+    v_term = dot(cotangent, low_in, ((0,), (0,)))
+    uv = summed_rows(jnp.concatenate([u_term, v_term], 1), (full, grad_blocks)) * scale
+    rank = lowrank_u.shape[1]
+    grad_u, grad_v = uv[:, :rank], uv[:, rank:].T
+    last_in = [swap(out[s][1], "mp", apart[s]) for s in far]
     far_in, full = tie((far_in, full), grad_blocks)
-    grad_tokens = full + far_in[0].astype(F32) + far_in[1].astype(F32)
+    full = added(full, far_in, 0)
+    last_in = tie(last_in, full)
+    grad_tokens = added(full, last_in, cut)
     return (grad_tokens, grad_blocks, grad_u, grad_v)
 
 

time: 327 us -> 320 us (0.979)
  waiting for transfers between devices: 184 us -> 166 us
  other arithmetic: 20.2 us -> 11.8 us
  starting transfers between devices: 21.1 us -> 29.4 us
  Pallas kernels: 95.4 us -> 103 us
    ppermute x19 -> x21, waiting for transfers between devices: 184 us -> 166 us  [swap(): return lax.ppermute(value, axis, [(i, i ^ apart) for i in range(count)])]
    pallas_call x0 -> x2, Pallas kernels: none -> 9 us  [added(): call(body, grid=(rows // tile,), in_specs=[block] + [pl.BlockSpec((tile,...]
    ppermute x19 -> x21, starting transfers between devices: 21.1 us -> 29.4 us  [swap(): return lax.ppermute(value, axis, [(i, i ^ apart) for i in range(count)])]
    add x1 -> x0, other arithmetic: 7.4 us -> none  [square(): grad_tokens = full + far_in[0].astype(F32) + far_in[1].astype(F32)]
  transfers between devices with their start and end apart: 19 -> 21, of which waited for: 8 -> 11; matrix products, arithmetic and copies ran while one was open for 5% -> 5% of each run, Pallas kernels for 27% -> 30%
where the time goes in v4:
time: 320 us; the launch traced here: 319 us
  waiting for transfers between devices  166 us (52%)
  Pallas kernels  103 us (32%)
  starting transfers between devices  29.4 us (9%)
  other arithmetic  11.8 us (4%)
  local copies, waits for them, and re-layouts  5.72 us (2%)
    ppermute x21, waiting for transfers between devices, swap(): return lax.ppermute(value, axis, [(i, i ^ apart) for i in range(count)])  166 us
    pallas_call x3, Pallas kernels, prefetched(): call(body, grid_spec=spec, out_shape=out_shape, **kwargs)(me, *operands)  34.8 us
    ppermute x21, starting transfers between devices, swap(): return lax.ppermute(value, axis, [(i, i ^ apart) for i in range(count)])  29.4 us
    pallas_call x3, Pallas kernels, partner_term(): call(body, grid=(blocks,), in_specs=[pl.BlockSpec((rows, width), lambda j...  20.7 us
    pallas_call x1, Pallas kernels, own_terms(): call(body, grid=(blocks, tiles), in_specs=[pl.BlockSpec((rows, blocks * w...  11.4 us
    pallas_call x1, Pallas kernels, all_grads(): call(body, grid=(width // tile,), in_specs=[pl.BlockSpec((x.shape[0], par...  11.4 us
    pallas_call x2, Pallas kernels, added(): call(body, grid=(rows // tile,), in_specs=[block] + [pl.BlockSpec((tile,...  9 us
    pallas_call x1, Pallas kernels, joined(): call(body, grid=(width // tile,), in_specs=[block, pl.BlockSpec((rows, ti...  7.72 us
  transfers between devices with their start and end apart: 21, of which 11 were waited for; matrix products, arithmetic and copies ran while one was open for 5% of the time, Pallas kernels for 30%

profile of v4, /device:TPU:0, one launch (start us, length us, event | category | flops | bytes accessed | tf_op | source)
XLA Modules:
  0.0 319.2 jit_solution(14625662695573458583)
XLA Ops:
  0.6 5.5 %shard_map.84 = (bf16[768,1024]{1,0:T(8,128)(2,1)}, bf16[768,2048]{1,0:T(8,128)(2,1)}, bf16[768,2048]{1,0:T(8,128)(2,1)}) custom-call(s32[1]{0:T(128)} %bitcast.me_ref, bf16[768,2048]{1,0:T(8,128)(2,1)} %refs_3_.3, bf16[768,2048]{1,0:T(8,128)(2,1)} %refs_12_.3), custom_call_target="tpu_custom_call" | custom-call | tf_op jit(solution)/shard_map/pallas_call | solution.py:52
  6.1 3.0 collective-permute-start
  12.1 2.6 collective-permute-start.3
  14.7 5.4 %shard_map.85 = (f32[768,256]{1,0:T(8,128)}, f32[768,256]{1,0:T(8,128)}) custom-call(s32[1]{0:T(128)} %bitcast.1.core_ref, bf16[768,2048]{1,0:T(8,128)(2,1)} %refs_3_.3, bf16[768,2048]{1,0:T(8,128)(2,1)} %refs_12_.3, bf16[2048,256]{1,0:T(8,128)(2,1)} %u_ref.3, bf16[256,2048]{1,0:T(8,128)(2,1)} %v_ref.1), custom_call_target="tpu_custom_call" | custom-call | tf_op jit(solution)/shard_map/pallas_call | solution.py:125
  20.1 6.9 %shard_map.86 = bf16[768,2048]{1,0:T(8,128)(2,1)} custom-call(bf16[768,2048]{1,0:T(8,128)(2,1)} %refs_12_.3, bf16[2,5,1024,1024]{3,2,1,0:T(8,128)(2,1)} %refs_1_.3), custom_call_target="tpu_custom_call" | custom-call | tf_op jit(solution)/shard_map/pallas_call | solution.py:67
  27.0 6.9 %shard_map.87 = (bf16[704,2048]{1,0:T(8,128)(2,1)}, bf16[64,2048]{1,0:T(8,128)(2,1)}) custom-call(bf16[768,2048]{1,0:T(8,128)(2,1)} %refs_12_.3, bf16[2,5,1024,1024]{3,2,1,0:T(8,128)(2,1)} %refs_1_.3), custom_call_target="tpu_custom_call" | custom-call | tf_op jit(solution)/shard_map/pallas_call | solution.py:67
  33.9 6.9 %shard_map.88 = (bf16[704,2048]{1,0:T(8,128)(2,1)}, bf16[64,2048]{1,0:T(8,128)(2,1)}) custom-call(bf16[768,2048]{1,0:T(8,128)(2,1)} %refs_12_.3, bf16[2,5,1024,1024]{3,2,1,0:T(8,128)(2,1)} %refs_1_.3), custom_call_target="tpu_custom_call" | custom-call | tf_op jit(solution)/shard_map/pallas_call | solution.py:67
  40.9 11.4 %shard_map.89.b = f32[768,2048]{1,0:T(8,128)} custom-call(bf16[768,2048]{1,0:T(8,128)(2,1)} %refs_12_.3, bf16[2,5,1024,1024]{3,2,1,0:T(8,128)(2,1)} %refs_1_.3, bf16[2,5,1024,1024]{3,2,1,0:T(8,128)(2,1)} %refs_1_.3), custom_call_target="tpu_custom_call" | custom-call | tf_op jit(solution)/shard_map/pallas_call | solution.py:102
  54.7 4.0 %pad_maximum_fusion = bf16[768,3072]{1,0:T(8,128)(2,1)} fusion(bf16[768,2048]{1,0:T(8,128)(2,1)S(1)} %copy-done.6, bf16[768,1024]{1,0:T(8,128)(2,1)} %get-tuple-element.60), kind=kLoop, calls=%fused_computation.8 | loop fusion | flops 9437184 | bytes 9437184 | tf_op jit(solution)/shard_map/concatenate | solution.py:360
  58.7 18.9 %collective-permute-done.refs_0_.refs_4_.refs_5_.refs_13_ = bf16[768,2048]{1,0:T(8,128)(2,1)} collective-permute-done((bf16[768,2048]{1,0:T(8,128)(2,1)}, bf16[768,2048]{1,0:T(8,128)(2,1)}, u32[]{:S(2)}, u32[]{:S(2)}) %collective-permute-start) | collective-permute-done | bytes 3145760 | tf_op jit(solution)/shard_map/ppermute | solution.py:20
  78.9 1.6 copy-done.2
  80.5 2.6 shard_map.90
  83.2 5.3 %collective-permute-done.5 = f32[384,256]{1,0:T(8,128)S(1)} collective-permute-done((f32[384,256]{1,0:T(8,128)S(1)}, f32[384,256]{1,0:T(8,128)S(1)}, u32[]{:S(2)}, u32[]{:S(2)}) %collective-permute-start.5) | collective-permute-done | bytes 393248 | tf_op jit(solution)/shard_map/ppermute | solution.py:20
  90.1 2.7 collective-permute-start.7
  94.3 16.4 %collective-permute-done.7 = f32[384,256]{1,0:T(8,128)S(1)} collective-permute-done((f32[384,256]{1,0:T(8,128)S(1)}, f32[384,256]{1,0:T(8,128)S(1)}, u32[]{:S(2)}, u32[]{:S(2)}) %collective-permute-start.7) | collective-permute-done | bytes 393248 | tf_op jit(solution)/shard_map/ppermute | solution.py:20
  110.7 4.2 %collective-permute-start.8 = (bf16[384,256]{1,0:T(8,128)(2,1)S(1)}, bf16[384,256]{1,0:T(8,128)(2,1)S(1)}, u32[]{:S(2)}, u32[]{:S(2)}) collective-permute-start(bf16[384,256]{1,0:T(8,128)(2,1)S(1)} %add_convert_fusion), channel_id=1, source_target_pairs={{0,2},{1,3},{2,0},{3,1},{4,6},{5,7},{6,4},{7,5},{8,10},{9,11},{10,... | collective-permute-start | bytes 589832 | tf_op jit(solution)/shard_map/ppermute | solution.py:20
  114.9 58.2 %collective-permute-done.8 = bf16[384,256]{1,0:T(8,128)(2,1)S(1)} collective-permute-done((bf16[384,256]{1,0:T(8,128)(2,1)S(1)}, bf16[384,256]{1,0:T(8,128)(2,1)S(1)}, u32[]{:S(2)}, u32[]{:S(2)}) %collective-permute-start.8) | collective-permute-done | bytes 196640 | tf_op jit(solution)/shard_map/ppermute | solution.py:20
  173.8 1.9 maximum_select_fusion
  175.8 2.6 collective-permute-start.11
  178.3 2.8 collective-permute-done.14.refs_11_
  181.2 14.7 %shard_map.92 = (f32[5,256,1024]{2,1,0:T(8,128)}, bf16[5,256,1024]{2,1,0:T(8,128)(2,1)}) custom-call(s32[1]{0:T(128)} %bitcast.me_ref, bf16[768,2048]{1,0:T(8,128)(2,1)} %refs_3_.3, bf16[768,2048]{1,0:T(8,128)(2,1)} %refs_3_.3, bf16[768,2048]{1,0:T(8,128)(2,1)} %refs_3_.3, bf16[768,2048]{1,0:T(8,128)(2,1)} %refs_3_.3, ...), custom_call_target="tpu_custom_call" | custom-call | tf_op jit(solution)/shard_map/pallas_call | solution.py:52
  196.5 14.6 %shard_map.93 = (f32[5,256,1024]{2,1,0:T(8,128)}, bf16[5,256,1024]{2,1,0:T(8,128)(2,1)}) custom-call(s32[1]{0:T(128)} %bitcast.me_ref, bf16[768,2048]{1,0:T(8,128)(2,1)} %refs_3_.3, bf16[768,2048]{1,0:T(8,128)(2,1)} %refs_3_.3, bf16[768,2048]{1,0:T(8,128)(2,1)} %refs_3_.3, bf16[768,2048]{1,0:T(8,128)(2,1)} %refs_3_.3, bf16[768,2048]{1,0:T(8,128)(2,1)} %copy-done.2, ...), custom_call_target="tpu_custom_call" | custom-call | tf_op jit(solution)/shard_map/pallas_call | solution.py:52
  217.7 7.7 %shard_map.91.b = f32[768,2048]{1,0:T(8,128)} custom-call(f32[768,2048]{1,0:T(8,128)} %shard_map.89.b, bf16[768,3072]{1,0:T(8,128)(2,1)} %collective-permute-done.9.n.refs_6_, bf16[768,256]{1,0:T(8,128)(2,1)} %copy-done.11, bf16[2048,256]{1,0:T(8,128)(2,1)} %u_ref.3), custom_call_target="tpu_custom_call" | custom-call | tf_op jit(solution)/shard_map/pallas_call | solution.py:280
  225.4 50.2 %collective-permute-done.19 = bf16[1024,512]{0,1:T(8,128)(2,1)S(1)} collective-permute-done((bf16[1024,512]{0,1:T(8,128)(2,1)}, bf16[1024,512]{0,1:T(8,128)(2,1)S(1)}, u32[]{:S(2)}, u32[]{:S(2)}) %collective-permute-start.19) | collective-permute-done | bytes 1048608 | tf_op jit(solution)/shard_map/ppermute | solution.py:20
  277.7 2.4 collective-permute-start.17
  280.1 3.4 %collective-permute-start.18 = (bf16[64,2048]{1,0:T(8,128)(2,1)}, bf16[64,2048]{1,0:T(8,128)(2,1)}, u32[]{:S(2)}, u32[]{:S(2)}) collective-permute-start(bf16[64,2048]{1,0:T(8,128)(2,1)} %get-tuple-element.107), channel_id=1, source_target_pairs={{0,4},{1,5},{2,6},{3,7},{4,0},{5,1},{6,2},{7,3},{8,12},{9,13},{10,... | collective-permute-start | bytes 786440 | tf_op jit(solution)/shard_map/ppermute | solution.py:20
  283.5 11.4 %shard_map.94 = f32[256,5,2,1024]{3,2,1,0:T(2,128)} custom-call(f32[5,256,1024]{2,1,0:T(8,128)} %get-tuple-element.96.refs_0_, bf16[5,256,1024]{2,1,0:T(8,128)(2,1)} %collective-permute-done.15.refs_1_, f32[5,256,1024]{2,1,0:T(8,128)} %get-tuple-element.101.refs_2_, bf16[5,256,1024]{2,1,0:T(8,128)(2,1)} %collective-permute-done.16.refs_3_), custom_call_target="tpu_custom_call" | custom-call | tf_op jit(solution)/shard_map/pallas_call | solution.py:242
  297.1 6.4 %collective-permute-done.11.refs_0_ = bf16[704,2048]{1,0:T(8,128)(2,1)} collective-permute-done((bf16[704,2048]{1,0:T(8,128)(2,1)}, bf16[704,2048]{1,0:T(8,128)(2,1)}, u32[]{:S(2)}, u32[]{:S(2)}) %collective-permute-start.11) | collective-permute-done | bytes 2883616 | tf_op jit(solution)/shard_map/ppermute | solution.py:20
  303.5 3.4 %collective-permute-done.12.refs_1_ = bf16[704,2048]{1,0:T(8,128)(2,1)} collective-permute-done((bf16[704,2048]{1,0:T(8,128)(2,1)}, bf16[704,2048]{1,0:T(8,128)(2,1)}, u32[]{:S(2)}, u32[]{:S(2)}) %collective-permute-start.12) | collective-permute-done | bytes 2883616 | tf_op jit(solution)/shard_map/ppermute | solution.py:20
  306.8 6.9 %shard_map.95.b = f32[768,2048]{1,0:T(8,128)} custom-call(f32[768,2048]{1,0:T(8,128)} %shard_map.91.b, bf16[704,2048]{1,0:T(8,128)(2,1)} %collective-permute-done.11.refs_0_, bf16[704,2048]{1,0:T(8,128)(2,1)} %collective-permute-done.12.refs_1_), custom_call_target="tpu_custom_call", output_to_operand_aliasing={{}: (0, {})} | custom-call | tf_op jit(solution)/shard_map/pallas_call | solution.py:305
  314.6 2.6 collective-permute-done.18.refs_1_
  317.1 2.1 shard_map.96
  (71 shorter events, 22.8 us)
Async XLA Ops:
  6.1 71.4 %collective-permute-start = (bf16[768,2048]{1,0:T(8,128)(2,1)}, bf16[768,2048]{1,0:T(8,128)(2,1)}, u32[]{:S(2)}, u32[]{:S(2)}) collective-permute-start(bf16[768,2048]{1,0:T(8,128)(2,1)} %get-tuple-element.58), channel_id=1, source_target_pairs={{0,16},{8,24},{16,0},{24,8},{1,17},{9,25},{17,1},{25,9},{2,18},{10... | collective-permute-start | bytes 9437192 | tf_op jit(solution)/shard_map/ppermute | solution.py:20
  9.1 69.8 %collective-permute-start.1 = (bf16[768,2048]{1,0:T(8,128)(2,1)}, bf16[768,2048]{1,0:T(8,128)(2,1)S(1)}, u32[]{:S(2)}, u32[]{:S(2)}) collective-permute-start(bf16[768,2048]{1,0:T(8,128)(2,1)} %get-tuple-element.59), channel_id=1, source_target_pairs={{0,8},{8,0},{16,24},{24,16},{1,9},{9,1},{17,25},{25,17},{2,10},{10... | collective-permute-start | bytes 9437192 | tf_op jit(solution)/shard_map/ppermute | solution.py:20
  10.6 77.9 %collective-permute-start.2 = (bf16[768,1024]{1,0:T(8,128)(2,1)}, bf16[768,1024]{1,0:T(8,128)(2,1)}, u32[]{:S(2)}, u32[]{:S(2)}) collective-permute-start(bf16[768,1024]{1,0:T(8,128)(2,1)} %get-tuple-element.60), channel_id=1, source_target_pairs={{0,2},{1,3},{2,0},{3,1},{4,6},{5,7},{6,4},{7,5},{8,10},{9,11},{10,... | collective-permute-start | bytes 4718600 | tf_op jit(solution)/shard_map/ppermute | solution.py:20
  12.1 76.3 %collective-permute-start.3 = (bf16[768,1024]{1,0:T(8,128)(2,1)}, bf16[768,1024]{1,0:T(8,128)(2,1)}, u32[]{:S(2)}, u32[]{:S(2)}) collective-permute-start(bf16[768,1024]{1,0:T(8,128)(2,1)} %get-tuple-element.60), channel_id=1, source_target_pairs={{0,4},{1,5},{2,6},{3,7},{4,0},{5,1},{6,2},{7,3},{8,12},{9,13},{10,... | collective-permute-start | bytes 4718600 | tf_op jit(solution)/shard_map/ppermute | solution.py:20
  20.1 32.2 %collective-permute-start.4 = (f32[768,256]{1,0:T(8,128)}, f32[768,256]{1,0:T(8,128)}, u32[]{:S(2)}, u32[]{:S(2)}) collective-permute-start(f32[768,256]{1,0:T(8,128)} %get-tuple-element.74), channel_id=1, source_target_pairs={{0,1},{1,0},{2,3},{3,2},{4,5},{5,4},{6,7},{7,6},{8,9},{9,8},{10,11... | collective-permute-start | bytes 2359304 | tf_op jit(solution)/shard_map/ppermute | solution.py:20
  52.3 2.4 copy-start.6
  53.9 4.7 %copy-start.12 = (f32[768,256]{1,0:T(8,128)}, f32[768,256]{1,0:T(8,128)S(1)}, u32[]{:S(2)}) copy-start(f32[768,256]{1,0:T(8,128)S(1)} %add.36) | copy-start | bytes 2359300
  54.0 34.5 %collective-permute-start.5 = (f32[384,256]{1,0:T(8,128)S(1)}, f32[384,256]{1,0:T(8,128)S(1)}, u32[]{:S(2)}, u32[]{:S(2)}) collective-permute-start(f32[384,256]{1,0:T(8,128)S(1)} %constant_dynamic-slice_fusion), channel_id=1, source_target_pairs={{0,2},{1,3},{2,0},{3,1},{4,6},{5,7},{6,4},{7,5},{8,10},{9,11},{10,... | collective-permute-start | bytes 1179656 | tf_op jit(solution)/shard_map/ppermute | solution.py:20
  88.5 85.3 %collective-permute-start.9 = (bf16[768,3072]{1,0:T(8,128)(2,1)}, bf16[768,3072]{1,0:T(8,128)(2,1)}, u32[]{:S(2)}, u32[]{:S(2)}) collective-permute-start(bf16[768,3072]{1,0:T(8,128)(2,1)} %pad_maximum_fusion), channel_id=1, source_target_pairs={{0,1},{1,0},{2,3},{3,2},{4,5},{5,4},{6,7},{7,6},{8,9},{9,8},{10,11... | collective-permute-start | bytes 14155784 | tf_op jit(solution)/shard_map/ppermute | solution.py:20
  88.5 84.6 %collective-permute-start.10 = (bf16[768,1024]{1,0:T(8,128)(2,1)}, bf16[768,1024]{1,0:T(8,128)(2,1)S(1)}, u32[]{:S(2)}, u32[]{:S(2)}) collective-permute-start(bf16[768,1024]{1,0:T(8,128)(2,1)} %shard_map.90), channel_id=1, source_target_pairs={{0,1},{1,0},{2,3},{3,2},{4,5},{5,4},{6,7},{7,6},{8,9},{9,8},{10,11... | collective-permute-start | bytes 4718600 | tf_op jit(solution)/shard_map/ppermute | solution.py:20
  90.1 20.6 %collective-permute-start.7 = (f32[384,256]{1,0:T(8,128)S(1)}, f32[384,256]{1,0:T(8,128)S(1)}, u32[]{:S(2)}, u32[]{:S(2)}) collective-permute-start(f32[384,256]{1,0:T(8,128)S(1)} %dynamic-slice_add_fusion), channel_id=1, source_target_pairs={{0,4},{1,5},{2,6},{3,7},{4,0},{5,1},{6,2},{7,3},{8,12},{9,13},{10,... | collective-permute-start | bytes 1179656 | tf_op jit(solution)/shard_map/ppermute | solution.py:20
  92.8 83.0 %collective-permute-start.6 = (bf16[768,1024]{1,0:T(8,128)(2,1)}, bf16[768,1024]{1,0:T(8,128)(2,1)S(1)}, u32[]{:S(2)}, u32[]{:S(2)}) collective-permute-start(bf16[768,1024]{1,0:T(8,128)(2,1)} %shard_map.90), channel_id=1, source_target_pairs={{0,2},{1,3},{2,0},{3,1},{4,6},{5,7},{6,4},{7,5},{8,10},{9,11},{10,... | collective-permute-start | bytes 4718600 | tf_op jit(solution)/shard_map/ppermute | solution.py:20
  110.6 70.5 %collective-permute-start.14 = (bf16[768,1024]{1,0:T(8,128)(2,1)}, bf16[768,1024]{1,0:T(8,128)(2,1)}, u32[]{:S(2)}, u32[]{:S(2)}) collective-permute-start(bf16[768,1024]{1,0:T(8,128)(2,1)} %shard_map.90), channel_id=1, source_target_pairs={{0,4},{1,5},{2,6},{3,7},{4,0},{5,1},{6,2},{7,3},{8,12},{9,13},{10,... | collective-permute-start | bytes 4718600 | tf_op jit(solution)/shard_map/ppermute | solution.py:20
  110.7 62.4 %copy-start.13 = (bf16[384,256]{1,0:T(8,128)(2,1)}, bf16[384,256]{1,0:T(8,128)(2,1)S(1)}, u32[]{:S(2)}) copy-start(bf16[384,256]{1,0:T(8,128)(2,1)S(1)} %add_convert_fusion) | copy-start | bytes 589828
  110.7 62.4 %collective-permute-start.8 = (bf16[384,256]{1,0:T(8,128)(2,1)S(1)}, bf16[384,256]{1,0:T(8,128)(2,1)S(1)}, u32[]{:S(2)}, u32[]{:S(2)}) collective-permute-start(bf16[384,256]{1,0:T(8,128)(2,1)S(1)} %add_convert_fusion), channel_id=1, source_target_pairs={{0,2},{1,3},{2,0},{3,1},{4,6},{5,7},{6,4},{7,5},{8,10},{9,11},{10,... | collective-permute-start | bytes 589832 | tf_op jit(solution)/shard_map/ppermute | solution.py:20
  173.8 7.4 %copy-start.9 = (bf16[768,1024]{1,0:T(8,128)(2,1)}, bf16[768,1024]{1,0:T(8,128)(2,1)S(1)}, u32[]{:S(2)}) copy-start(bf16[768,1024]{1,0:T(8,128)(2,1)S(1)} %collective-permute-done.10.refs_7_) | copy-start | bytes 4718596
  175.6 36.1 %collective-permute-start.13 = (bf16[768,256]{1,0:T(8,128)(2,1)S(1)}, bf16[768,256]{1,0:T(8,128)(2,1)}, u32[]{:S(2)}, u32[]{:S(2)}) collective-permute-start(bf16[768,256]{1,0:T(8,128)(2,1)S(1)} %maximum_select_fusion), channel_id=1, source_target_pairs={{0,1},{1,0},{2,3},{3,2},{4,5},{5,4},{6,7},{7,6},{8,9},{9,8},{10,11... | collective-permute-start | bytes 1179656 | tf_op jit(solution)/shard_map/ppermute | solution.py:20
  175.8 5.4 %copy-start.10 = (bf16[768,1024]{1,0:T(8,128)(2,1)}, bf16[768,1024]{1,0:T(8,128)(2,1)S(1)}, u32[]{:S(2)}) copy-start(bf16[768,1024]{1,0:T(8,128)(2,1)S(1)} %collective-permute-done.6.refs_9_) | copy-start | bytes 4718596
  175.8 127.7 %collective-permute-start.11 = (bf16[704,2048]{1,0:T(8,128)(2,1)}, bf16[704,2048]{1,0:T(8,128)(2,1)}, u32[]{:S(2)}, u32[]{:S(2)}) collective-permute-start(bf16[704,2048]{1,0:T(8,128)(2,1)} %get-tuple-element.88), channel_id=1, source_target_pairs={{0,2},{1,3},{2,0},{3,1},{4,6},{5,7},{6,4},{7,5},{8,10},{9,11},{10,... | collective-permute-start | bytes 8650760 | tf_op jit(solution)/shard_map/ppermute | solution.py:20
  178.3 128.5 %collective-permute-start.12 = (bf16[704,2048]{1,0:T(8,128)(2,1)}, bf16[704,2048]{1,0:T(8,128)(2,1)}, u32[]{:S(2)}, u32[]{:S(2)}) collective-permute-start(bf16[704,2048]{1,0:T(8,128)(2,1)} %get-tuple-element.89), channel_id=1, source_target_pairs={{0,4},{1,5},{2,6},{3,7},{4,0},{5,1},{6,2},{7,3},{8,12},{9,13},{10,... | collective-permute-start | bytes 8650760 | tf_op jit(solution)/shard_map/ppermute | solution.py:20
  195.9 15.9 %copy-start.1 = (bf16[768,2048]{1,0:T(8,128)(2,1)S(1)}, bf16[768,2048]{1,0:T(8,128)(2,1)}, u32[]{:S(2)}) copy-start(bf16[768,2048]{1,0:T(8,128)(2,1)} %refs_12_.3) | copy-start | bytes 9437188
  195.9 81.8 %collective-permute-start.15 = (bf16[5,256,1024]{2,1,0:T(8,128)(2,1)}, bf16[5,256,1024]{2,1,0:T(8,128)(2,1)}, u32[]{:S(2)}, u32[]{:S(2)}) collective-permute-start(bf16[5,256,1024]{2,1,0:T(8,128)(2,1)} %get-tuple-element.97), channel_id=1, source_target_pairs={{0,8},{8,0},{16,24},{24,16},{1,9},{9,1},{17,25},{25,17},{2,10},{10... | collective-permute-start | bytes 7864328 | tf_op jit(solution)/shard_map/ppermute | solution.py:20
  211.1 2.7 copy-start
  211.2 69.0 %collective-permute-start.16 = (bf16[5,256,1024]{2,1,0:T(8,128)(2,1)}, bf16[5,256,1024]{2,1,0:T(8,128)(2,1)}, u32[]{:S(2)}, u32[]{:S(2)}) collective-permute-start(bf16[5,256,1024]{2,1,0:T(8,128)(2,1)} %get-tuple-element.99), channel_id=1, source_target_pairs={{0,16},{8,24},{16,0},{24,8},{1,17},{9,25},{17,1},{25,9},{2,18},{10... | collective-permute-start | bytes 7864328 | tf_op jit(solution)/shard_map/ppermute | solution.py:20
  216.5 59.1 %collective-permute-start.19 = (bf16[1024,512]{0,1:T(8,128)(2,1)}, bf16[1024,512]{0,1:T(8,128)(2,1)S(1)}, u32[]{:S(2)}, u32[]{:S(2)}) collective-permute-start(bf16[1024,512]{0,1:T(8,128)(2,1)} %pad_maximum_fusion.1), channel_id=1, source_target_pairs={{0,8},{8,0},{16,24},{24,16},{1,9},{9,1},{17,25},{25,17},{2,10},{10... | collective-permute-start | bytes 3145736 | tf_op jit(solution)/shard_map/ppermute | solution.py:20
  225.4 50.5 %copy-start.4 = (f32[2048,256]{0,1:T(8,128)S(1)}, f32[2048,256]{0,1:T(8,128)}, u32[]{:S(2)}) copy-start(f32[2048,256]{0,1:T(8,128)} %copy-done.3) | copy-start | bytes 6291460
  277.3 17.7 %collective-permute-start.20 = (bf16[512,512]{0,1:T(8,128)(2,1)S(1)}, bf16[512,512]{0,1:T(8,128)(2,1)S(1)}, u32[]{:S(2)}, u32[]{:S(2)}) collective-permute-start(bf16[512,512]{0,1:T(8,128)(2,1)S(1)} %fusion.2), channel_id=1, source_target_pairs={{0,16},{8,24},{16,0},{24,8},{1,17},{9,25},{17,1},{25,9},{2,18},{10... | collective-permute-start | bytes 1572872 | tf_op jit(solution)/shard_map/ppermute | solution.py:20
  277.7 36.8 %collective-permute-start.17 = (bf16[64,2048]{1,0:T(8,128)(2,1)}, bf16[64,2048]{1,0:T(8,128)(2,1)S(1)}, u32[]{:S(2)}, u32[]{:S(2)}) collective-permute-start(bf16[64,2048]{1,0:T(8,128)(2,1)} %get-tuple-element.106), channel_id=1, source_target_pairs={{0,2},{1,3},{2,0},{3,1},{4,6},{5,7},{6,4},{7,5},{8,10},{9,11},{10,... | collective-permute-start | bytes 786440 | tf_op jit(solution)/shard_map/ppermute | solution.py:20
  280.1 37.0 %collective-permute-start.18 = (bf16[64,2048]{1,0:T(8,128)(2,1)}, bf16[64,2048]{1,0:T(8,128)(2,1)}, u32[]{:S(2)}, u32[]{:S(2)}) collective-permute-start(bf16[64,2048]{1,0:T(8,128)(2,1)} %get-tuple-element.107), channel_id=1, source_target_pairs={{0,4},{1,5},{2,6},{3,7},{4,0},{5,1},{6,2},{7,3},{8,12},{9,13},{10,... | collective-permute-start | bytes 786440 | tf_op jit(solution)/shard_map/ppermute | solution.py:20
  283.5 11.4 %copy-start.5 = (f32[2048,256]{0,1:T(8,128)S(1)}, f32[2048,256]{0,1:T(8,128)}, u32[]{:S(2)}) copy-start(f32[2048,256]{0,1:T(8,128)} %copy-done.3) | copy-start | bytes 6291460
  283.5 11.4 %copy-start.8 = (f32[1024,512]{0,1:T(8,128)S(1)}, f32[1024,512]{0,1:T(8,128)}, u32[]{:S(2)}) copy-start(f32[1024,512]{0,1:T(8,128)} %copy-done.7) | copy-start | bytes 6291460
  314.6 2.6 copy-start.14
  (5 other events, 6.5 us)

commit v5 on v4

--- a/solution.py
+++ b/solution.py
@@ -312,15 +312,21 @@
     )(base, *terms)
 
 
-def summed_rows(term, before):
+def summed_rows(terms, before):
     me = lax.axis_index("dp")
-    size = term.shape[0] // 4
-    parts = [lax.dynamic_slice_in_dim(term, (me ^ x) * size, size, 0) for x in range(4)]
-    got = swap(jnp.concatenate([parts[1], parts[3]], 0).astype(BF16), "dp", 1)
-    got = tie(got, before[0]).astype(F32)
-    mine, theirs = parts[0] + got[:size], parts[2] + got[size:]
-    got = swap(theirs.astype(BF16), "dp", 2)
-    return mine + tie(got, before[1]).astype(F32)
+    size = terms[0].shape[0] // 4
+    parts = [
+        [lax.dynamic_slice_in_dim(t, (me ^ x) * size, size, 0) for x in range(4)] for t in terms
+    ]
+    got = [
+        swap(jnp.concatenate([p[1 + k], p[3]], 0).astype(BF16), "dp", 1 + k)
+        for k, p in enumerate(parts)
+    ]
+    got = [g.astype(F32) for g in tie(got, before[0])]
+    mine = [p[0] + g[:size] for p, g in zip(parts, got)]
+    theirs = [p[2 - k] + g[size:] for k, (p, g) in enumerate(zip(parts, got))]
+    got = [swap(t.astype(BF16), "dp", 2 - k) for k, t in enumerate(theirs)]
+    return [m + g.astype(F32) for m, g in zip(mine, tie(got, before[1]))]
 
 
 def square(tokens, cotangent, blocks_w, lowrank_u, lowrank_v):
@@ -362,10 +368,11 @@
     more = gathered(given, 2 * part)
     given, held_in, out, near_out, got, more = tie((given, held_in, out, near_out, got, more))
     more_in = {3: swap(more, "mp", apart[3])}
-    near_in = swap(near_out, "mp", apart[near])
-    near_more = swap(more, "mp", apart[near])
     kept = kept + got
     got = swap(kept, "mp", 4)
+    near_out, near_more = tie((near_out, more), kept)
+    near_in = swap(near_out, "mp", apart[near])
+    near_more = swap(near_more, "mp", apart[near])
     got, more4 = tie((got, more))
     more_in[4] = swap(more4, "mp", apart[4])
 
@@ -394,9 +401,8 @@
 
     u_term = dot(tokens, low_back, ((0,), (0,)))
     v_term = dot(cotangent, low_in, ((0,), (0,)))
-    uv = summed_rows(jnp.concatenate([u_term, v_term], 1), (full, grad_blocks)) * scale
-    rank = lowrank_u.shape[1]
-    grad_u, grad_v = uv[:, :rank], uv[:, rank:].T
+    grad_u, grad_v = summed_rows([u_term, v_term], (full, grad_blocks))
+    grad_u, grad_v = grad_u * scale, grad_v.T * scale
     last_in = [swap(out[s][1], "mp", apart[s]) for s in far]
     far_in, full = tie((far_in, full), grad_blocks)
     full = added(full, far_in, 0)

time: 320 us -> 319 us (level)
  waiting for transfers between devices: 166 us -> 161 us
    ppermute x21 -> x23, waiting for transfers between devices: 166 us -> 161 us  [swap(): return lax.ppermute(value, axis, [(i, i ^ apart) for i in range(count)])]
    mul x1 -> x2, other arithmetic: 0.28 us -> 4.07 us  [square(): grad_u, grad_v = (grad_u * scale, grad_v.T * scale)]
    ppermute x21 -> x23, starting transfers between devices: 29.4 us -> 31.3 us  [swap(): return lax.ppermute(value, axis, [(i, i ^ apart) for i in range(count)])]
  transfers between devices with their start and end apart: 21 -> 23, of which waited for: 11 -> 10; matrix products, arithmetic and copies ran while one was open for 5% -> 6% of each run, Pallas kernels for 30% -> 30%
where the time goes in v5:
time: 319 us; the launch traced here: 318 us
  waiting for transfers between devices  161 us (50%)
  Pallas kernels  103 us (32%)
  starting transfers between devices  31.3 us (10%)
  other arithmetic  14.6 us (5%)
  local copies, waits for them, and re-layouts  5.71 us (2%)
    ppermute x23, waiting for transfers between devices, swap(): return lax.ppermute(value, axis, [(i, i ^ apart) for i in range(count)])  161 us
    pallas_call x3, Pallas kernels, prefetched(): call(body, grid_spec=spec, out_shape=out_shape, **kwargs)(me, *operands)  34.9 us
    ppermute x23, starting transfers between devices, swap(): return lax.ppermute(value, axis, [(i, i ^ apart) for i in range(count)])  31.3 us
    pallas_call x3, Pallas kernels, partner_term(): call(body, grid=(blocks,), in_specs=[pl.BlockSpec((rows, width), lambda j...  20.8 us
    pallas_call x1, Pallas kernels, own_terms(): call(body, grid=(blocks, tiles), in_specs=[pl.BlockSpec((rows, blocks * w...  11.4 us
    pallas_call x1, Pallas kernels, all_grads(): call(body, grid=(width // tile,), in_specs=[pl.BlockSpec((x.shape[0], par...  11 us
    pallas_call x2, Pallas kernels, added(): call(body, grid=(rows // tile,), in_specs=[block] + [pl.BlockSpec((tile,...  9.01 us
    pallas_call x1, Pallas kernels, joined(): call(body, grid=(width // tile,), in_specs=[block, pl.BlockSpec((rows, ti...  7.71 us
  transfers between devices with their start and end apart: 23, of which 10 were waited for; matrix products, arithmetic and copies ran while one was open for 6% of the time, Pallas kernels for 30%

profile of v5, /device:TPU:0, one launch (start us, length us, event | category | flops | bytes accessed | tf_op | source)
XLA Modules:
  0.0 318.2 jit_solution(12559163732572246967)
XLA Ops:
  0.6 5.5 %shard_map.84 = (bf16[768,1024]{1,0:T(8,128)(2,1)}, bf16[768,2048]{1,0:T(8,128)(2,1)}, bf16[768,2048]{1,0:T(8,128)(2,1)}) custom-call(s32[1]{0:T(128)} %bitcast.me_ref, bf16[768,2048]{1,0:T(8,128)(2,1)} %refs_3_.3, bf16[768,2048]{1,0:T(8,128)(2,1)} %refs_12_.3), custom_call_target="tpu_custom_call" | custom-call | tf_op jit(solution)/shard_map/pallas_call | solution.py:52
  6.1 3.0 collective-permute-start
  12.1 2.6 collective-permute-start.3
  14.7 5.4 %shard_map.85 = (f32[768,256]{1,0:T(8,128)}, f32[768,256]{1,0:T(8,128)}) custom-call(s32[1]{0:T(128)} %bitcast.1.core_ref, bf16[768,2048]{1,0:T(8,128)(2,1)} %refs_3_.3, bf16[768,2048]{1,0:T(8,128)(2,1)} %refs_12_.3, bf16[2048,256]{1,0:T(8,128)(2,1)} %u_ref.3, bf16[256,2048]{1,0:T(8,128)(2,1)} %v_ref.1), custom_call_target="tpu_custom_call" | custom-call | tf_op jit(solution)/shard_map/pallas_call | solution.py:125
  20.1 6.9 %shard_map.86 = bf16[768,2048]{1,0:T(8,128)(2,1)} custom-call(bf16[768,2048]{1,0:T(8,128)(2,1)} %refs_12_.3, bf16[2,5,1024,1024]{3,2,1,0:T(8,128)(2,1)} %refs_1_.3), custom_call_target="tpu_custom_call" | custom-call | tf_op jit(solution)/shard_map/pallas_call | solution.py:67
  27.0 6.9 %shard_map.87 = (bf16[704,2048]{1,0:T(8,128)(2,1)}, bf16[64,2048]{1,0:T(8,128)(2,1)}) custom-call(bf16[768,2048]{1,0:T(8,128)(2,1)} %refs_12_.3, bf16[2,5,1024,1024]{3,2,1,0:T(8,128)(2,1)} %refs_1_.3), custom_call_target="tpu_custom_call" | custom-call | tf_op jit(solution)/shard_map/pallas_call | solution.py:67
  33.9 7.0 %shard_map.88 = (bf16[704,2048]{1,0:T(8,128)(2,1)}, bf16[64,2048]{1,0:T(8,128)(2,1)}) custom-call(bf16[768,2048]{1,0:T(8,128)(2,1)} %refs_12_.3, bf16[2,5,1024,1024]{3,2,1,0:T(8,128)(2,1)} %refs_1_.3), custom_call_target="tpu_custom_call" | custom-call | tf_op jit(solution)/shard_map/pallas_call | solution.py:67
  40.9 11.4 %shard_map.89.b = f32[768,2048]{1,0:T(8,128)} custom-call(bf16[768,2048]{1,0:T(8,128)(2,1)} %refs_12_.3, bf16[2,5,1024,1024]{3,2,1,0:T(8,128)(2,1)} %refs_1_.3, bf16[2,5,1024,1024]{3,2,1,0:T(8,128)(2,1)} %refs_1_.3), custom_call_target="tpu_custom_call" | custom-call | tf_op jit(solution)/shard_map/pallas_call | solution.py:102
  54.7 4.0 %pad_maximum_fusion = bf16[768,3072]{1,0:T(8,128)(2,1)} fusion(bf16[768,2048]{1,0:T(8,128)(2,1)S(1)} %copy-done.3, bf16[768,1024]{1,0:T(8,128)(2,1)} %get-tuple-element.64), kind=kLoop, calls=%fused_computation | loop fusion | flops 9437184 | bytes 9437184 | tf_op jit(solution)/shard_map/concatenate | solution.py:366
  58.7 18.8 %collective-permute-done.refs_0_.refs_4_.refs_5_.refs_13_ = bf16[768,2048]{1,0:T(8,128)(2,1)} collective-permute-done((bf16[768,2048]{1,0:T(8,128)(2,1)}, bf16[768,2048]{1,0:T(8,128)(2,1)}, u32[]{:S(2)}, u32[]{:S(2)}) %collective-permute-start) | collective-permute-done | bytes 3145760 | tf_op jit(solution)/shard_map/ppermute | solution.py:20
  80.5 2.6 shard_map.90
  83.2 5.3 %collective-permute-done.5 = f32[384,256]{1,0:T(8,128)S(1)} collective-permute-done((f32[384,256]{1,0:T(8,128)S(1)}, f32[384,256]{1,0:T(8,128)S(1)}, u32[]{:S(2)}, u32[]{:S(2)}) %collective-permute-start.5) | collective-permute-done | bytes 393248 | tf_op jit(solution)/shard_map/ppermute | solution.py:20
  89.1 2.6 collective-permute-start.7
  93.3 16.4 %collective-permute-done.7 = f32[384,256]{1,0:T(8,128)S(1)} collective-permute-done((f32[384,256]{1,0:T(8,128)S(1)}, f32[384,256]{1,0:T(8,128)S(1)}, u32[]{:S(2)}, u32[]{:S(2)}) %collective-permute-start.7) | collective-permute-done | bytes 393248 | tf_op jit(solution)/shard_map/ppermute | solution.py:20
  109.7 4.2 %collective-permute-start.8 = (bf16[384,256]{1,0:T(8,128)(2,1)S(1)}, bf16[384,256]{1,0:T(8,128)(2,1)S(1)}, u32[]{:S(2)}, u32[]{:S(2)}) collective-permute-start(bf16[384,256]{1,0:T(8,128)(2,1)S(1)} %add_convert_fusion), channel_id=1, source_target_pairs={{0,2},{1,3},{2,0},{3,1},{4,6},{5,7},{6,4},{7,5},{8,10},{9,11},{10,... | collective-permute-start | bytes 589832 | tf_op jit(solution)/shard_map/ppermute | solution.py:20
  113.9 58.2 %collective-permute-done.8 = bf16[384,256]{1,0:T(8,128)(2,1)S(1)} collective-permute-done((bf16[384,256]{1,0:T(8,128)(2,1)S(1)}, bf16[384,256]{1,0:T(8,128)(2,1)S(1)}, u32[]{:S(2)}, u32[]{:S(2)}) %collective-permute-start.8) | collective-permute-done | bytes 196640 | tf_op jit(solution)/shard_map/ppermute | solution.py:20
  174.8 2.6 collective-permute-start.11
  177.4 2.8 collective-permute-done.14.refs_11_
  180.2 14.7 %shard_map.92 = (f32[5,256,1024]{2,1,0:T(8,128)}, bf16[5,256,1024]{2,1,0:T(8,128)(2,1)}) custom-call(s32[1]{0:T(128)} %bitcast.me_ref, bf16[768,2048]{1,0:T(8,128)(2,1)} %refs_3_.3, bf16[768,2048]{1,0:T(8,128)(2,1)} %refs_3_.3, bf16[768,2048]{1,0:T(8,128)(2,1)} %refs_3_.3, bf16[768,2048]{1,0:T(8,128)(2,1)} %refs_3_.3, ...), custom_call_target="tpu_custom_call" | custom-call | tf_op jit(solution)/shard_map/pallas_call | solution.py:52
  195.6 14.7 %shard_map.93 = (f32[5,256,1024]{2,1,0:T(8,128)}, bf16[5,256,1024]{2,1,0:T(8,128)(2,1)}) custom-call(s32[1]{0:T(128)} %bitcast.me_ref, bf16[768,2048]{1,0:T(8,128)(2,1)} %refs_3_.3, bf16[768,2048]{1,0:T(8,128)(2,1)} %refs_3_.3, bf16[768,2048]{1,0:T(8,128)(2,1)} %refs_3_.3, bf16[768,2048]{1,0:T(8,128)(2,1)} %refs_3_.3, bf16[768,2048]{1,0:T(8,128)(2,1)} %copy-done.2, ...), custom_call_target="tpu_custom_call" | custom-call | tf_op jit(solution)/shard_map/pallas_call | solution.py:52
  215.6 47.8 %collective-permute-done.19 = bf16[1024,256]{0,1:T(8,128)(2,1)S(1)} collective-permute-done((bf16[1024,256]{0,1:T(8,128)(2,1)S(1)}, bf16[1024,256]{0,1:T(8,128)(2,1)S(1)}, u32[]{:S(2)}, u32[]{:S(2)}) %collective-permute-start.19) | collective-permute-done | bytes 524320 | tf_op jit(solution)/shard_map/ppermute | solution.py:20
  263.9 7.7 %shard_map.91.b = f32[768,2048]{1,0:T(8,128)} custom-call(f32[768,2048]{1,0:T(8,128)} %shard_map.89.b, bf16[768,3072]{1,0:T(8,128)(2,1)} %collective-permute-done.9.n.refs_6_, bf16[768,256]{1,0:T(8,128)(2,1)} %copy-done.8, bf16[2048,256]{1,0:T(8,128)(2,1)} %u_ref.3), custom_call_target="tpu_custom_call" | custom-call | tf_op jit(solution)/shard_map/pallas_call | solution.py:280
  271.6 6.8 %collective-permute-done.20 = bf16[1024,256]{0,1:T(8,128)(2,1)S(1)} collective-permute-done((bf16[1024,256]{0,1:T(8,128)(2,1)S(1)}, bf16[1024,256]{0,1:T(8,128)(2,1)S(1)}, u32[]{:S(2)}, u32[]{:S(2)}) %collective-permute-start.20) | collective-permute-done | bytes 524320 | tf_op jit(solution)/shard_map/ppermute | solution.py:20
  283.0 2.4 collective-permute-start.17
  285.4 11.0 %shard_map.94 = f32[256,5,2,1024]{3,2,1,0:T(2,128)} custom-call(f32[5,256,1024]{2,1,0:T(8,128)} %get-tuple-element.102.refs_0_, bf16[5,256,1024]{2,1,0:T(8,128)(2,1)} %collective-permute-done.15.refs_1_, f32[5,256,1024]{2,1,0:T(8,128)} %get-tuple-element.107.refs_2_, bf16[5,256,1024]{2,1,0:T(8,128)(2,1)} %collective-permute-done.16.refs_3_), custom_call_target="tpu_custom_call" | custom-call | tf_op jit(solution)/shard_map/pallas_call | solution.py:242
  296.4 3.4 %collective-permute-start.18 = (bf16[64,2048]{1,0:T(8,128)(2,1)}, bf16[64,2048]{1,0:T(8,128)(2,1)}, u32[]{:S(2)}, u32[]{:S(2)}) collective-permute-start(bf16[64,2048]{1,0:T(8,128)(2,1)} %get-tuple-element.113), channel_id=1, source_target_pairs={{0,4},{1,5},{2,6},{3,7},{4,0},{5,1},{6,2},{7,3},{8,12},{9,13},{10,... | collective-permute-start | bytes 786440 | tf_op jit(solution)/shard_map/ppermute | solution.py:20
  299.8 2.0 fusion.6
  301.8 2.0 copy.11
  303.9 2.0 fusion.2
  305.9 7.0 %shard_map.95.b = f32[768,2048]{1,0:T(8,128)} custom-call(f32[768,2048]{1,0:T(8,128)} %shard_map.91.b, bf16[704,2048]{1,0:T(8,128)(2,1)} %collective-permute-done.11.refs_0_, bf16[704,2048]{1,0:T(8,128)(2,1)} %collective-permute-done.12.refs_1_), custom_call_target="tpu_custom_call", output_to_operand_aliasing={{}: (0, {})} | custom-call | tf_op jit(solution)/shard_map/pallas_call | solution.py:305
  313.6 2.6 collective-permute-done.18.refs_1_
  316.2 2.1 shard_map.96
  (70 shorter events, 24.9 us)
Async XLA Ops:
  6.1 71.4 %collective-permute-start = (bf16[768,2048]{1,0:T(8,128)(2,1)}, bf16[768,2048]{1,0:T(8,128)(2,1)}, u32[]{:S(2)}, u32[]{:S(2)}) collective-permute-start(bf16[768,2048]{1,0:T(8,128)(2,1)} %get-tuple-element.62), channel_id=1, source_target_pairs={{0,16},{8,24},{16,0},{24,8},{1,17},{9,25},{17,1},{25,9},{2,18},{10... | collective-permute-start | bytes 9437192 | tf_op jit(solution)/shard_map/ppermute | solution.py:20
  9.1 69.8 %collective-permute-start.1 = (bf16[768,2048]{1,0:T(8,128)(2,1)}, bf16[768,2048]{1,0:T(8,128)(2,1)S(1)}, u32[]{:S(2)}, u32[]{:S(2)}) collective-permute-start(bf16[768,2048]{1,0:T(8,128)(2,1)} %get-tuple-element.63), channel_id=1, source_target_pairs={{0,8},{8,0},{16,24},{24,16},{1,9},{9,1},{17,25},{25,17},{2,10},{10... | collective-permute-start | bytes 9437192 | tf_op jit(solution)/shard_map/ppermute | solution.py:20
  10.6 77.9 %collective-permute-start.2 = (bf16[768,1024]{1,0:T(8,128)(2,1)}, bf16[768,1024]{1,0:T(8,128)(2,1)}, u32[]{:S(2)}, u32[]{:S(2)}) collective-permute-start(bf16[768,1024]{1,0:T(8,128)(2,1)} %get-tuple-element.64), channel_id=1, source_target_pairs={{0,2},{1,3},{2,0},{3,1},{4,6},{5,7},{6,4},{7,5},{8,10},{9,11},{10,... | collective-permute-start | bytes 4718600 | tf_op jit(solution)/shard_map/ppermute | solution.py:20
  12.1 76.3 %collective-permute-start.3 = (bf16[768,1024]{1,0:T(8,128)(2,1)}, bf16[768,1024]{1,0:T(8,128)(2,1)}, u32[]{:S(2)}, u32[]{:S(2)}) collective-permute-start(bf16[768,1024]{1,0:T(8,128)(2,1)} %get-tuple-element.64), channel_id=1, source_target_pairs={{0,4},{1,5},{2,6},{3,7},{4,0},{5,1},{6,2},{7,3},{8,12},{9,13},{10,... | collective-permute-start | bytes 4718600 | tf_op jit(solution)/shard_map/ppermute | solution.py:20
  20.1 32.2 %collective-permute-start.4 = (f32[768,256]{1,0:T(8,128)}, f32[768,256]{1,0:T(8,128)}, u32[]{:S(2)}, u32[]{:S(2)}) collective-permute-start(f32[768,256]{1,0:T(8,128)} %get-tuple-element.78), channel_id=1, source_target_pairs={{0,1},{1,0},{2,3},{3,2},{4,5},{5,4},{6,7},{7,6},{8,9},{9,8},{10,11... | collective-permute-start | bytes 2359304 | tf_op jit(solution)/shard_map/ppermute | solution.py:20
  52.3 2.4 copy-start.3
  54.0 34.5 %collective-permute-start.5 = (f32[384,256]{1,0:T(8,128)S(1)}, f32[384,256]{1,0:T(8,128)S(1)}, u32[]{:S(2)}, u32[]{:S(2)}) collective-permute-start(f32[384,256]{1,0:T(8,128)S(1)} %constant_dynamic-slice_fusion), channel_id=1, source_target_pairs={{0,2},{1,3},{2,0},{3,1},{4,6},{5,7},{6,4},{7,5},{8,10},{9,11},{10,... | collective-permute-start | bytes 1179656 | tf_op jit(solution)/shard_map/ppermute | solution.py:20
  78.9 1.7 copy-start.2
  88.5 84.2 %collective-permute-start.9 = (bf16[768,3072]{1,0:T(8,128)(2,1)}, bf16[768,3072]{1,0:T(8,128)(2,1)}, u32[]{:S(2)}, u32[]{:S(2)}) collective-permute-start(bf16[768,3072]{1,0:T(8,128)(2,1)} %pad_maximum_fusion), channel_id=1, source_target_pairs={{0,1},{1,0},{2,3},{3,2},{4,5},{5,4},{6,7},{7,6},{8,9},{9,8},{10,11... | collective-permute-start | bytes 14155784 | tf_op jit(solution)/shard_map/ppermute | solution.py:20
  88.6 83.5 %collective-permute-start.10 = (bf16[768,1024]{1,0:T(8,128)(2,1)}, bf16[768,1024]{1,0:T(8,128)(2,1)S(1)}, u32[]{:S(2)}, u32[]{:S(2)}) collective-permute-start(bf16[768,1024]{1,0:T(8,128)(2,1)} %shard_map.90), channel_id=1, source_target_pairs={{0,1},{1,0},{2,3},{3,2},{4,5},{5,4},{6,7},{7,6},{8,9},{9,8},{10,11... | collective-permute-start | bytes 4718600 | tf_op jit(solution)/shard_map/ppermute | solution.py:20
  89.1 20.5 %collective-permute-start.7 = (f32[384,256]{1,0:T(8,128)S(1)}, f32[384,256]{1,0:T(8,128)S(1)}, u32[]{:S(2)}, u32[]{:S(2)}) collective-permute-start(f32[384,256]{1,0:T(8,128)S(1)} %dynamic-slice_add_fusion), channel_id=1, source_target_pairs={{0,4},{1,5},{2,6},{3,7},{4,0},{5,1},{6,2},{7,3},{8,12},{9,13},{10,... | collective-permute-start | bytes 1179656 | tf_op jit(solution)/shard_map/ppermute | solution.py:20
  91.8 83.0 %collective-permute-start.6 = (bf16[768,1024]{1,0:T(8,128)(2,1)}, bf16[768,1024]{1,0:T(8,128)(2,1)S(1)}, u32[]{:S(2)}, u32[]{:S(2)}) collective-permute-start(bf16[768,1024]{1,0:T(8,128)(2,1)} %shard_map.90), channel_id=1, source_target_pairs={{0,2},{1,3},{2,0},{3,1},{4,6},{5,7},{6,4},{7,5},{8,10},{9,11},{10,... | collective-permute-start | bytes 4718600 | tf_op jit(solution)/shard_map/ppermute | solution.py:20
  109.7 70.5 %collective-permute-start.14 = (bf16[768,1024]{1,0:T(8,128)(2,1)}, bf16[768,1024]{1,0:T(8,128)(2,1)}, u32[]{:S(2)}, u32[]{:S(2)}) collective-permute-start(bf16[768,1024]{1,0:T(8,128)(2,1)} %shard_map.90), channel_id=1, source_target_pairs={{0,4},{1,5},{2,6},{3,7},{4,0},{5,1},{6,2},{7,3},{8,12},{9,13},{10,... | collective-permute-start | bytes 4718600 | tf_op jit(solution)/shard_map/ppermute | solution.py:20
  109.7 62.4 %copy-start.9 = (bf16[384,256]{1,0:T(8,128)(2,1)}, bf16[384,256]{1,0:T(8,128)(2,1)S(1)}, u32[]{:S(2)}) copy-start(bf16[384,256]{1,0:T(8,128)(2,1)S(1)} %add_convert_fusion) | copy-start | bytes 589828
  109.7 62.4 %collective-permute-start.8 = (bf16[384,256]{1,0:T(8,128)(2,1)S(1)}, bf16[384,256]{1,0:T(8,128)(2,1)S(1)}, u32[]{:S(2)}, u32[]{:S(2)}) collective-permute-start(bf16[384,256]{1,0:T(8,128)(2,1)S(1)} %add_convert_fusion), channel_id=1, source_target_pairs={{0,2},{1,3},{2,0},{3,1},{4,6},{5,7},{6,4},{7,5},{8,10},{9,11},{10,... | collective-permute-start | bytes 589832 | tf_op jit(solution)/shard_map/ppermute | solution.py:20
  172.8 7.4 %copy-start.5 = (bf16[768,1024]{1,0:T(8,128)(2,1)}, bf16[768,1024]{1,0:T(8,128)(2,1)S(1)}, u32[]{:S(2)}) copy-start(bf16[768,1024]{1,0:T(8,128)(2,1)S(1)} %collective-permute-done.10.refs_7_) | copy-start | bytes 4718596
  174.6 36.3 %collective-permute-start.13 = (bf16[768,256]{1,0:T(8,128)(2,1)S(1)}, bf16[768,256]{1,0:T(8,128)(2,1)}, u32[]{:S(2)}, u32[]{:S(2)}) collective-permute-start(bf16[768,256]{1,0:T(8,128)(2,1)S(1)} %maximum_select_fusion), channel_id=1, source_target_pairs={{0,1},{1,0},{2,3},{3,2},{4,5},{5,4},{6,7},{7,6},{8,9},{9,8},{10,11... | collective-permute-start | bytes 1179656 | tf_op jit(solution)/shard_map/ppermute | solution.py:20
  174.8 5.4 %copy-start.6 = (bf16[768,1024]{1,0:T(8,128)(2,1)}, bf16[768,1024]{1,0:T(8,128)(2,1)S(1)}, u32[]{:S(2)}) copy-start(bf16[768,1024]{1,0:T(8,128)(2,1)S(1)} %collective-permute-done.6.refs_9_) | copy-start | bytes 4718596
  174.8 131.1 %collective-permute-start.11 = (bf16[704,2048]{1,0:T(8,128)(2,1)}, bf16[704,2048]{1,0:T(8,128)(2,1)}, u32[]{:S(2)}, u32[]{:S(2)}) collective-permute-start(bf16[704,2048]{1,0:T(8,128)(2,1)} %get-tuple-element.94), channel_id=1, source_target_pairs={{0,2},{1,3},{2,0},{3,1},{4,6},{5,7},{6,4},{7,5},{8,10},{9,11},{10,... | collective-permute-start | bytes 8650760 | tf_op jit(solution)/shard_map/ppermute | solution.py:20
  177.3 128.5 %collective-permute-start.12 = (bf16[704,2048]{1,0:T(8,128)(2,1)}, bf16[704,2048]{1,0:T(8,128)(2,1)}, u32[]{:S(2)}, u32[]{:S(2)}) collective-permute-start(bf16[704,2048]{1,0:T(8,128)(2,1)} %get-tuple-element.95), channel_id=1, source_target_pairs={{0,4},{1,5},{2,6},{3,7},{4,0},{5,1},{6,2},{7,3},{8,12},{9,13},{10,... | collective-permute-start | bytes 8650760 | tf_op jit(solution)/shard_map/ppermute | solution.py:20
  194.9 16.0 %copy-start.1 = (bf16[768,2048]{1,0:T(8,128)(2,1)S(1)}, bf16[768,2048]{1,0:T(8,128)(2,1)}, u32[]{:S(2)}) copy-start(bf16[768,2048]{1,0:T(8,128)(2,1)} %refs_12_.3) | copy-start | bytes 9437188
  194.9 87.1 %collective-permute-start.15 = (bf16[5,256,1024]{2,1,0:T(8,128)(2,1)}, bf16[5,256,1024]{2,1,0:T(8,128)(2,1)}, u32[]{:S(2)}, u32[]{:S(2)}) collective-permute-start(bf16[5,256,1024]{2,1,0:T(8,128)(2,1)} %get-tuple-element.103), channel_id=1, source_target_pairs={{0,8},{8,0},{16,24},{24,16},{1,9},{9,1},{17,25},{25,17},{2,10},{10... | collective-permute-start | bytes 7864328 | tf_op jit(solution)/shard_map/ppermute | solution.py:20
  210.3 2.7 copy-start
  210.3 72.7 %collective-permute-start.16 = (bf16[5,256,1024]{2,1,0:T(8,128)(2,1)}, bf16[5,256,1024]{2,1,0:T(8,128)(2,1)}, u32[]{:S(2)}, u32[]{:S(2)}) collective-permute-start(bf16[5,256,1024]{2,1,0:T(8,128)(2,1)} %get-tuple-element.105), channel_id=1, source_target_pairs={{0,16},{8,24},{16,0},{24,8},{1,17},{9,25},{17,1},{25,9},{2,18},{10... | collective-permute-start | bytes 7864328 | tf_op jit(solution)/shard_map/ppermute | solution.py:20
  214.0 64.5 %copy-start.4 = (f32[256,2048]{1,0:T(8,128)}, f32[256,2048]{1,0:T(8,128)S(1)}, u32[]{:S(2)}) copy-start(f32[256,2048]{1,0:T(8,128)S(1)} %fusion.14) | copy-start | bytes 6291460
  214.3 49.2 %collective-permute-start.19 = (bf16[1024,256]{0,1:T(8,128)(2,1)S(1)}, bf16[1024,256]{0,1:T(8,128)(2,1)S(1)}, u32[]{:S(2)}, u32[]{:S(2)}) collective-permute-start(bf16[1024,256]{0,1:T(8,128)(2,1)S(1)} %pad_maximum_fusion.1), channel_id=1, source_target_pairs={{0,8},{8,0},{16,24},{24,16},{1,9},{9,1},{17,25},{25,17},{2,10},{10... | collective-permute-start | bytes 1572872 | tf_op jit(solution)/shard_map/ppermute | solution.py:20
  263.4 15.0 %collective-permute-start.20 = (bf16[1024,256]{0,1:T(8,128)(2,1)S(1)}, bf16[1024,256]{0,1:T(8,128)(2,1)S(1)}, u32[]{:S(2)}, u32[]{:S(2)}) collective-permute-start(bf16[1024,256]{0,1:T(8,128)(2,1)S(1)} %pad_maximum_fusion.2), channel_id=1, source_target_pairs={{0,16},{8,24},{16,0},{24,8},{1,17},{9,25},{17,1},{25,9},{2,18},{10... | collective-permute-start | bytes 1572872 | tf_op jit(solution)/shard_map/ppermute | solution.py:20
  279.4 17.0 %collective-permute-start.21 = (bf16[512,256]{0,1:T(8,128)(2,1)}, bf16[512,256]{0,1:T(8,128)(2,1)}, u32[]{:S(2)}, u32[]{:S(2)}) collective-permute-start(bf16[512,256]{0,1:T(8,128)(2,1)} %fusion.4), channel_id=1, source_target_pairs={{0,16},{8,24},{16,0},{24,8},{1,17},{9,25},{17,1},{25,9},{2,18},{10... | collective-permute-start | bytes 786440 | tf_op jit(solution)/shard_map/ppermute | solution.py:20
  282.0 17.7 %collective-permute-start.22 = (bf16[512,256]{0,1:T(8,128)(2,1)}, bf16[512,256]{0,1:T(8,128)(2,1)}, u32[]{:S(2)}, u32[]{:S(2)}) collective-permute-start(bf16[512,256]{0,1:T(8,128)(2,1)} %fusion.3), channel_id=1, source_target_pairs={{0,8},{8,0},{16,24},{24,16},{1,9},{9,1},{17,25},{25,17},{2,10},{10... | collective-permute-start | bytes 786440 | tf_op jit(solution)/shard_map/ppermute | solution.py:20
  283.0 30.5 %collective-permute-start.17 = (bf16[64,2048]{1,0:T(8,128)(2,1)}, bf16[64,2048]{1,0:T(8,128)(2,1)S(1)}, u32[]{:S(2)}, u32[]{:S(2)}) collective-permute-start(bf16[64,2048]{1,0:T(8,128)(2,1)} %get-tuple-element.112), channel_id=1, source_target_pairs={{0,2},{1,3},{2,0},{3,1},{4,6},{5,7},{6,4},{7,5},{8,10},{9,11},{10,... | collective-permute-start | bytes 786440 | tf_op jit(solution)/shard_map/ppermute | solution.py:20
  296.4 19.8 %collective-permute-start.18 = (bf16[64,2048]{1,0:T(8,128)(2,1)}, bf16[64,2048]{1,0:T(8,128)(2,1)}, u32[]{:S(2)}, u32[]{:S(2)}) collective-permute-start(bf16[64,2048]{1,0:T(8,128)(2,1)} %get-tuple-element.113), channel_id=1, source_target_pairs={{0,4},{1,5},{2,6},{3,7},{4,0},{5,1},{6,2},{7,3},{8,12},{9,13},{10,... | collective-permute-start | bytes 786440 | tf_op jit(solution)/shard_map/ppermute | solution.py:20
  313.6 2.6 copy-start.10
  (3 other events, 2.8 us)
